TPU v7x, 256 devices: a whole 4x4x8 slice. The times are simulated.
256 devices in a mesh: dp: 4 (over x_hi, core), section: 8 (over x_lo, y), tensor: 8 (over z).
Axes of the slice: x: 4 (x_hi: 2, x_lo: 2; x = x_hi * 2 + x_lo), y: 4, z: 8, core: 2. Of those that a mesh axis runs over, the one named last changes fastest.
Arguments:
- text: bfloat16 [8, 64, 8192], P('dp', None, 'tensor'), may hold values from -6 to 6
- order: int32 [4, 2], P('dp'), may hold values from 0 to 1, each once within a row
- lengths: int32 [4, 2], P('dp'), may hold values from 16 to 64
- image: bfloat16 [8, 32, 8192], P('dp', 'section', 'tensor'), may hold values from -6 to 6
- in_gain: float32 [8, 8192], P('section'), may hold values from 0.25 to 1.75
- wq: bfloat16 [8, 8192, 4096], P('section', 'dp', 'tensor'), may hold values from -0.0625 to 0.0625
- wk: bfloat16 [8, 8192, 1024], P('section', 'dp', 'tensor'), may hold values from -0.0625 to 0.0625
- wv: bfloat16 [8, 8192, 1024], P('section', 'dp', 'tensor'), may hold values from -0.0625 to 0.0625
- wo: bfloat16 [8, 4096, 8192], P('section', 'tensor', 'dp'), may hold values from -0.09375 to 0.09375
- query_norm_gain: float32 [8, 128], P('section'), may hold values from 0.5 to 2
- k_gain: float32 [8, 128], P('section'), may hold values from 0.5 to 2
- gate: float32 [8], P('section'), may hold values from -1.5 to 1.5
- cot: bfloat16 [8, 8, 64, 8192], P('section', 'dp'), may hold values from -6 to 6
Outputs:
- states: bfloat16 [8, 8, 64, 8192], P('section', 'dp', None, 'tensor')
- image_grad: float32 [8, 32, 8192], P('dp', 'section', 'tensor')
Inputs may be any that keep to these rules, and one draw needn't show every extreme that they name: `order`: each row lists the 2 micro-batches of one data-parallel group, each once.
All inputs are finite; a program needn't handle non-finite values.
Results may differ from a plain program's by a relative error of at most 0.035.
Values may be sent and summed in bfloat16 or wider, within the bound.
No kernel may reach another device: no remote copies, remote signals or barrier semaphores. Data moves between devices by JAX's collectives and lax.ppermute only.
A program may use at most 128 MiB of HBM per device.

v0:
```python
import functools
import math

import jax
import jax.numpy as jnp
from jax import lax
from jax.experimental import pallas as pl
from jax.experimental.pallas import tpu as pltpu
from jax.sharding import PartitionSpec as P

EPS = 1e-05
HIGH = lax.Precision.HIGHEST
LANES = 128
EXTRA = 16
VMEM_BYTES = 14 * 2**20
ROWS_ROWS = (((1,), (1,)), ((), ()))
COLS_COLS = (((0,), (0,)), ((), ()))


def dot32(a, b, dims=(((1,), (0,)), ((), ()))):
    return lax.dot_general(a, b, dims, precision=HIGH, preferred_element_type=jnp.float32)


def dot16(a, b, dims=(((1,), (0,)), ((), ()))):
    return lax.dot_general(a, b, dims, preferred_element_type=jnp.float32)


def slot_of(step, ints, slots):
    return jnp.clip(step - ints[0], 0, slots - 1)


def query_kernel(step, ints, text_ref, gain_ref, *refs):
    h_ref = refs[0] if len(refs) == 7 else None
    w_refs, q_ref, hq_ref = refs[-6:-2], refs[-2], refs[-1]
    h = text_ref[slot_of(step, ints, text_ref.shape[0])]
    if h_ref is not None:
        h = jnp.where(ints[0] == 0, h, h_ref[...])
    hq_ref[...] = h
    hf = h.astype(jnp.float32)
    x = (hf * gain_ref[...]).astype(jnp.bfloat16)
    ss = jnp.sum(hf * hf, axis=1, keepdims=True)
    hi = ss.astype(jnp.bfloat16).astype(jnp.float32)
    rows = h.shape[0]
    own, lane = own_lanes(rows)
    pair = jnp.where(own, jnp.where(lane < rows, hi, ss - hi), 0.0)
    pair = jnp.broadcast_to(jnp.sum(pair, axis=0, keepdims=True), (EXTRA, LANES))
    pair = pair.astype(jnp.bfloat16)
    n, chunk, cols = w_refs[0].shape
    for k in range(n):
        acc = dot16(x[:, :chunk], w_refs[0][k])
        for j in range(1, 4):
            acc += dot16(x[:, j * chunk : (j + 1) * chunk], w_refs[j][k])
        acc = acc.astype(jnp.bfloat16)
        for i in range(cols // LANES):
            q_ref[k, i * rows : (i + 1) * rows, :] = acc[:, i * LANES : (i + 1) * LANES]
        q_ref[k, cols // LANES * rows :, :] = pair


def query(step, ints, text, gain, h, w):
    rows, feats = text.shape[1:]
    n, _, cols = w[0].shape
    args = [text, gain] + ([] if h is None else [h]) + list(w)
    return pl.pallas_call(
        functools.partial(query_kernel, step),
        in_specs=[pl.BlockSpec(memory_space=pltpu.SMEM)]
        + [pl.BlockSpec(memory_space=pltpu.VMEM)] * len(args),
        out_specs=[pl.BlockSpec(memory_space=pltpu.VMEM)] * 2,
        out_shape=[
            jax.ShapeDtypeStruct((n, cols // LANES * rows + EXTRA, LANES), jnp.bfloat16),
            jax.ShapeDtypeStruct((rows, feats), jnp.bfloat16),
        ],
        compiler_params=pltpu.CompilerParams(vmem_limit_bytes=VMEM_BYTES),
    )(ints, *args)


def output_kernel(step, ints, p_ref, vo_ref, h_ref, o_ref):
    probs = jnp.concatenate([p_ref[i] for i in range(p_ref.shape[0])], axis=1)
    new = h_ref[...].astype(jnp.float32) + dot16(probs, vo_ref[slot_of(step, ints, vo_ref.shape[0])])
    o_ref[...] = new.astype(jnp.bfloat16)


def output(step, ints, probs, vo, h):
    return pl.pallas_call(
        functools.partial(output_kernel, step),
        in_specs=[pl.BlockSpec(memory_space=pltpu.SMEM)]
        + [pl.BlockSpec(memory_space=pltpu.VMEM)] * 3,
        out_specs=pl.BlockSpec(memory_space=pltpu.VMEM),
        out_shape=jax.ShapeDtypeStruct(h.shape, jnp.bfloat16),
        compiler_params=pltpu.CompilerParams(vmem_limit_bytes=VMEM_BYTES),
    )(ints, probs, vo, h)


def own_lanes(rows):
    row = lax.broadcasted_iota(jnp.int32, (rows, LANES), 0)
    lane = lax.broadcasted_iota(jnp.int32, (rows, LANES), 1)
    return (lane == row) | (lane == row + rows), lane


def whole(shape):
    return pl.BlockSpec(shape, lambda *_: (0,) * len(shape))


def attend_kernel(step, width, ints, alpha_ref, gain_ref, k_ref, q_ref, p_ref, qn_ref):
    slot = slot_of(step, ints, k_ref.shape[0])
    total = q_ref[0].astype(jnp.float32)
    for i in range(1, q_ref.shape[0]):
        total += q_ref[i].astype(jnp.float32)
    hd = gain_ref.shape[1]
    rows, cols = qn_ref.shape
    own, _ = own_lanes(rows)
    sums = jnp.broadcast_to(total[cols // hd * rows : cols // hd * rows + 1], (rows, LANES))
    ss = jnp.sum(jnp.where(own, sums, 0.0), axis=1, keepdims=True)
    rs = lax.rsqrt(ss / width + EPS)
    keys = k_ref[slot]
    row = lax.broadcasted_iota(jnp.int32, (rows, keys.shape[0]), 0)
    scale = jnp.where(row < ints[1 + slot], alpha_ref[0], 0.0)
    parts = []
    for h in range(cols // hd):
        q = total[h * rows : (h + 1) * rows] * rs
        r = lax.rsqrt(jnp.mean(q * q, axis=1, keepdims=True) + EPS)
        qn = q * r * gain_ref[...] * (1.0 / math.sqrt(hd))
        qn_ref[:, h * hd : (h + 1) * hd] = qn
        sc = dot32(qn, keys, ROWS_ROWS)
        e = jnp.exp(sc - jnp.max(sc, axis=1, keepdims=True))
        parts.append(scale * e / jnp.sum(e, axis=1, keepdims=True))
    p = jnp.concatenate(parts, axis=1).astype(jnp.bfloat16)
    for i in range(p_ref.shape[0]):
        p_ref[i] = p


def attend(step, ints, alpha, width, gain, keys, parts):
    hd = gain.shape[1]
    toks = keys.shape[1]
    heads = 4
    n = parts.shape[0]
    rows = (parts.shape[1] - EXTRA) // heads
    return pl.pallas_call(
        functools.partial(attend_kernel, step, width),
        in_specs=[pl.BlockSpec(memory_space=pltpu.SMEM)] * 2
        + [pl.BlockSpec(memory_space=pltpu.VMEM)] * 3,
        out_specs=[pl.BlockSpec(memory_space=pltpu.VMEM)] * 2,
        out_shape=[
            jax.ShapeDtypeStruct((n, rows, heads * toks), jnp.bfloat16),
            jax.ShapeDtypeStruct((rows, heads * hd), jnp.float32),
        ],
        compiler_params=pltpu.CompilerParams(vmem_limit_bytes=VMEM_BYTES),
    )(ints, alpha, gain, keys, parts)


def value_out_kernel(slots, v_ref, *refs):
    w_refs, o_ref = refs[:4], refs[4]
    n, vrows, hd = v_ref.shape
    toks = vrows // slots
    heads, chunk = w_refs[0].shape[1] // hd, w_refs[0].shape[2]

    def block(k, carry):
        v = v_ref[k]
        for h in range(heads):
            at = pl.multiple_of((k * heads + h) * toks, toks)
            for j in range(4):
                r = dot16(v, w_refs[j][k, h * hd : (h + 1) * hd, :]).astype(jnp.bfloat16)
                for o in range(slots):
                    o_ref[o, pl.ds(at, toks), j * chunk : (j + 1) * chunk] = r[
                        o * toks : (o + 1) * toks
                    ]
        return carry

    lax.fori_loop(0, n, block, 0)


def value_out(v, w, slots):
    n, vrows, hd = v.shape
    heads = w[0].shape[1] // hd
    chunk = w[0].shape[2]
    toks = vrows // slots
    return pl.pallas_call(
        functools.partial(value_out_kernel, slots),
        in_specs=[pl.BlockSpec(memory_space=pltpu.VMEM)] * 5,
        out_specs=pl.BlockSpec(memory_space=pltpu.VMEM),
        out_shape=jax.ShapeDtypeStruct((slots, n * heads * toks, 4 * chunk), jnp.bfloat16),
        compiler_params=pltpu.CompilerParams(vmem_limit_bytes=VMEM_BYTES),
    )(v, *w)


def back_kernel(qn_ref, k_ref, v_ref, raw_ref, da_ref, gain_ref, o_ref):
    keys, vals, raw, gain = k_ref[0], v_ref[0], raw_ref[0], gain_ref[...]
    hd = keys.shape[1]
    d_kn = jnp.zeros(keys.shape, jnp.float32)
    d_v = jnp.zeros(keys.shape, jnp.float32)
    for h in range(qn_ref.shape[2] // hd):
        qn = qn_ref[0, :, h * hd : (h + 1) * hd]
        da = da_ref[0, :, h * hd : (h + 1) * hd]
        sc = dot32(qn, keys, ROWS_ROWS)
        e = jnp.exp(sc - jnp.max(sc, axis=1, keepdims=True))
        p = e / jnp.sum(e, axis=1, keepdims=True)
        dp = dot32(da, vals, ROWS_ROWS)
        ds = p * (dp - jnp.sum(p * dp, axis=1, keepdims=True))
        d_kn += dot32(ds, qn, COLS_COLS)
        d_v += dot32(p, da, COLS_COLS)
    r = lax.rsqrt(jnp.mean(raw * raw, axis=1, keepdims=True) + EPS)
    u = d_kn * gain
    d_k = r * u - raw * (r * r * r * jnp.mean(raw * u, axis=1, keepdims=True))
    o_ref[0, :, :hd] = d_k.astype(jnp.bfloat16)
    o_ref[0, :, hd:] = d_v.astype(jnp.bfloat16)


def back(qn, keys, vals, raw, da, gain):
    slots, toks, hd = keys.shape
    one = lambda a: pl.BlockSpec((1,) + a.shape[1:], lambda o: (o, 0, 0))
    return pl.pallas_call(
        back_kernel,
        grid=(slots,),
        in_specs=[one(qn), one(keys), one(vals), one(raw), one(da), pl.BlockSpec(gain.shape, lambda o: (0, 0))],
        out_specs=pl.BlockSpec((1, toks, 2 * hd), lambda o: (o, 0, 0)),
        out_shape=jax.ShapeDtypeStruct((slots, toks, 2 * hd), jnp.bfloat16),
    )(qn, keys, vals, raw, da, gain)


def pick(a, i, axis=0):
    return lax.dynamic_index_in_dim(a, i, axis, keepdims=False)


def after(x, *others):
    return lax.optimization_barrier((x,) + others)[0]


def swap(x, axis):
    return lax.all_to_all(x, axis, 0, 0, tiled=True)


def share(x, axis):
    return swap(jnp.broadcast_to(x[None], (lax.axis_size(axis),) + x.shape), axis)


def per_device(
    text, order, lengths, image, in_gain, wq, wk, wv, wo, query_norm_gain, k_gain, gate, cot
):
    D, S, T = lax.axis_size("dp"), lax.axis_size("section"), lax.axis_size("tensor")
    R = T // D
    d, s, t = lax.axis_index("dp"), lax.axis_index("section"), lax.axis_index("tensor")
    slots, rows = text.shape[:2]
    width = in_gain.shape[1]
    hd = k_gain.shape[1]
    feats = width // T
    chunk = feats // D
    toks = image.shape[1] * S

    def onward(x):
        return lax.ppermute(x, "section", [(i, (i + 1) % S) for i in range(S)])

    def dp_flip(x, m):
        return lax.ppermute(x, "dp", [(i, i ^ m) for i in range(D)])

    def dp_all(x):
        across = dp_flip(x, 2)
        return [x, dp_flip(x, 1), across, dp_flip(across, 1)]

    def spread(x):
        a, c = t // R, t % D
        parts = jnp.stack(jnp.split(x, D, axis=-1))
        got = []
        for k in range(D):
            pairs = [(i * R + b, b * D + (i + k) % D) for i in range(D) for b in range(R)]
            got.append(lax.ppermute(pick(parts, (a + k) % D), "tensor", pairs))
        got = jnp.stack(got)
        return jnp.concatenate([pick(got, (c - (d ^ j)) % D) for j in range(D)], axis=-1)

    def unspread(x):
        a, c = t // R, t % D
        parts = jnp.stack(jnp.split(x, D, axis=-1))
        got = []
        for k in range(D):
            pairs = [(b * D + (i + k) % D, i * R + b) for i in range(D) for b in range(R)]
            got.append(lax.ppermute(pick(parts, ((c - k) % D) ^ d), "tensor", pairs))
        got = jnp.stack(got)
        return jnp.concatenate([pick(got, (j - a) % D) for j in range(D)], axis=-1)

    micro = order[0]
    lens = jnp.take(lengths[0], micro)
    alpha = jnp.tanh(gate)

    shared = share(jnp.take(image, micro, axis=0).reshape(-1, feats), "section")
    img = lax.all_gather(shared.reshape(slots * toks, feats), "tensor", axis=1, tiled=True)
    wkv = after(jnp.concatenate([wk[0], wv[0]], axis=1), img)
    wkv = lax.all_gather(wkv, "dp", axis=0, tiled=True)
    kv = jnp.dot(img, wkv, preferred_element_type=jnp.float32)
    kv = jnp.moveaxis(kv.reshape(S, slots, toks // S, 2 * hd), 0, 1).reshape(slots, toks, 2 * hd)
    k_raw, vals = kv[..., :hd], kv[..., hd:]
    keys = k_raw * lax.rsqrt(jnp.mean(k_raw * k_raw, axis=-1, keepdims=True) + EPS) * k_gain[0]

    wq_own = swap(after(wq[0].reshape(T, chunk, wq.shape[2]), shared), "tensor")
    wq_f = dp_all(wq_own)
    text_f = spread(after(jnp.take(text, micro, axis=0), wq_own))
    gain_f = pick(in_gain.reshape(D, T, chunk), t, 1)
    gain_f = jnp.concatenate([pick(gain_f, d ^ j) for j in range(D)])[None]
    wo_own = jnp.moveaxis(wo[0].reshape(wo.shape[1], T, chunk), 1, 0)
    wo_own = swap(after(wo_own, wq_own, wkv), "tensor")
    ints = jnp.concatenate([s.astype(jnp.int32)[None], lens])

    h = None
    all_qn, all_h = [], []
    for step in range(S + slots - 1):
        parts, hq = query(step, ints, text_f, gain_f, h, wq_f)
        p, qn = attend(step, ints, alpha, width, query_norm_gain, keys, swap(parts, "tensor"))
        all_qn.append(qn)
        if step == 0:
            vals16 = vals.astype(jnp.bfloat16).reshape(slots * toks, hd)
            vals16 = jnp.broadcast_to(vals16[None], (T,) + vals16.shape)
            both = swap(jnp.concatenate([p, vals16], axis=1), "tensor")
            probs = both[:, :rows]
            wo_own = after(wo_own, hq)
            across = dp_flip(wo_own, 2)
            wo_f = [wo_own, dp_flip(wo_own, 1), across, dp_flip(after(across, probs), 1)]
            vo = value_out(both[:, rows:], wo_f, slots)
        else:
            probs = swap(p, "tensor")
        if step == 1:
            wo_full = lax.all_gather(after(wo[0], p), "dp", axis=1, tiled=True)
        if step == 5:
            mask = (jnp.arange(rows)[None, :] < lens[:, None]).astype(jnp.float32)[:, :, None]
            d_attn = dot16(cot[0].reshape(slots * rows, width), wo_full, ROWS_ROWS)
            d_attn = alpha[0] * mask * d_attn.reshape(slots, rows, -1)
            probs, d_attn = lax.optimization_barrier((probs, d_attn))
        h = output(step, ints, probs, vo, hq)
        all_h.append(h)
        h = onward(h)

    states = unspread(lax.dynamic_slice_in_dim(jnp.stack(all_h), s, slots, 0))

    qn = lax.dynamic_slice_in_dim(jnp.stack(all_qn), s, slots, 0)
    d_kv = back(qn, keys, vals, k_raw, d_attn, k_gain).reshape(slots * toks, 2 * hd)
    grad = dot16(d_kv, wkv, ROWS_ROWS).astype(jnp.bfloat16)
    grad = swap(jnp.moveaxis(grad.reshape(slots * toks, T, feats), 1, 0), "tensor")
    grad = jnp.sum(grad.astype(jnp.float32), axis=0).astype(jnp.bfloat16)
    grad = swap(jnp.moveaxis(grad.reshape(slots, S, toks // S, feats), 1, 0), "section")
    grad = jnp.sum(grad.astype(jnp.float32), axis=0)
    grad = jnp.stack([pick(grad, jnp.argmax(micro == m)) for m in range(slots)])
    return (states[None], grad)


def solution(mesh):
    return jax.shard_map(
        per_device,
        mesh=mesh,
        in_specs=(
            P("dp", None, "tensor"),
            P("dp", None),
            P("dp", None),
            P("dp", "section", "tensor"),
            P("section", None),
            P("section", "dp", "tensor"),
            P("section", "dp", "tensor"),
            P("section", "dp", "tensor"),
            P("section", "tensor", "dp"),
            P("section", None),
            P("section", None),
            P("section"),
            P("section", "dp", None, None),
        ),
        out_specs=(P("section", "dp", None, "tensor"), P("dp", "section", "tensor")),
        check_vma=False,
    )
```

profile of v0, /device:TPU:32, one launch (start us, length us, event | category | flops | bytes accessed | tf_op | source)
XLA Modules:
  0.0 689.9 jit_solution(3047580472017339622)
XLA Ops:
  11.6 11.9 %all_to_all.115 = bf16[8,8,1024]{2,1,0:T(8,128)(2,1)} all-to-all(bf16[8,8,1024]{2,1,0:T(8,128)(2,1)S(1)} %broadcast_in_dim.56), channel_id=1, replica_groups=mesh['dp'=4,'section'=8,'tensor'=8] {'section'}, dimensions={0} | all-to-all | bytes 262144 | tf_op jit(solution)/shard_map/all_to_all | solution.py:228
  24.7 37.2 %all-gather.4.cloned.1.call-done = bf16[64,8192]{1,0:T(8,128)(2,1)} async-done(((bf16[64,1024]{1,0:T(8,128)(2,1)}), bf16[64,8192]{1,0:T(8,128)(2,1)}) %all-gather.4.cloned.1.call-update) | async-done | bytes 1048592 | tf_op jit(solution)/shard_map/all_gather | solution.py:283
  62.0 50.8 %all_to_all.116.refs_0_.refs_1_ = bf16[8,256,512]{2,1,0:T(8,128)(2,1)} all-to-all(bf16[8,256,512]{2,1,0:T(8,128)(2,1)} %bitcast.158), channel_id=1, replica_groups=mesh['dp'=4,'section'=8,'tensor'=8] {'tensor'}, dimensions={0} | all-to-all | bytes 4194304 | tf_op jit(solution)/shard_map/all_to_all | solution.py:228
  112.8 3.0 collective-permute-start.5
  115.8 3.9 copy.24
  119.7 3.9 copy.25
  123.6 5.8 all-to-all-start.4
  129.5 25.9 %collective-permute-done.5.refs_2_.refs_3_ = bf16[8,256,512]{2,1,0:T(8,128)(2,1)} collective-permute-done((bf16[8,256,512]{2,1,0:T(8,128)(2,1)}, bf16[8,256,512]{2,1,0:T(8,128)(2,1)}, u32[]{:S(2)}, u32[]{:S(2)}) %collective-permute-start.5) | collective-permute-done | bytes 2097184 | tf_op jit(solution)/shard_map/ppermute | solution.py:252
  162.3 5.7 collective-permute-start.2
  167.9 4.9 collective-permute-done
  172.9 4.0 collective-permute-start.1
  179.1 5.9 shard_map.140
  187.5 8.4 %all-to-all-start.2 = ((bf16[8,272,128]{2,1,0:T(8,128)(2,1)}), bf16[8,272,128]{2,1,0:T(8,128)(2,1)S(1)}, u32[]{:S(2)}, u32[]{:S(2)}) async-start(bf16[8,272,128]{2,1,0:T(8,128)(2,1)} %get-tuple-element.52), calls=%async_computation.2 | async-start | bytes 1114112 | tf_op jit(solution)/shard_map/all_to_all | solution.py:228
  195.9 3.3 fusion.24
  200.0 12.2 %all-to-all-done.2.q_ref = bf16[8,272,128]{2,1,0:T(8,128)(2,1)S(1)} async-done(((bf16[8,272,128]{2,1,0:T(8,128)(2,1)}), bf16[8,272,128]{2,1,0:T(8,128)(2,1)S(1)}, u32[]{:S(2)}, u32[]{:S(2)}) %all-to-all-start.2) | async-done | bytes 557088 | tf_op jit(solution)/shard_map/all_to_all | solution.py:228
  213.5 13.7 %all_to_all.117 = bf16[8,128,128]{2,1,0:T(8,128)(2,1)S(1)} all-to-all(bf16[8,128,128]{2,1,0:T(8,128)(2,1)S(1)} %pad_maximum_fusion.4), channel_id=1, replica_groups=mesh['dp'=4,'section'=8,'tensor'=8] {'tensor'}, dimensions={0} | all-to-all | bytes 524288 | tf_op jit(solution)/shard_map/all_to_all | solution.py:228
  227.4 5.3 collective-permute-done.8.refs_2_
  232.7 4.4 collective-permute-done.9.refs_3_
  237.0 4.6 shard_map.142.vo_ref
  245.0 6.2 collective-permute-done.10.refs_0_
  251.2 5.0 shard_map.144
  256.2 27.3 %all_to_all.118.q_ref = bf16[8,272,128]{2,1,0:T(8,128)(2,1)S(1)} all-to-all(bf16[8,272,128]{2,1,0:T(8,128)(2,1)S(1)} %get-tuple-element.58), channel_id=1, replica_groups=mesh['dp'=4,'section'=8,'tensor'=8] {'tensor'}, dimensions={0} | all-to-all | bytes 1114112 | tf_op jit(solution)/shard_map/all_to_all | solution.py:228
  284.8 11.7 %all_to_all.119.p_ref = bf16[8,64,128]{2,1,0:T(8,128)(2,1)S(1)} all-to-all(bf16[8,64,128]{2,1,0:T(8,128)(2,1)S(1)} %get-tuple-element.59), channel_id=1, replica_groups=mesh['dp'=4,'section'=8,'tensor'=8] {'tensor'}, dimensions={0} | all-to-all | bytes 262144 | tf_op jit(solution)/shard_map/all_to_all | solution.py:228
  300.1 9.9 %collective-permute-done.11.refs_0_ = bf16[64,1024]{1,0:T(8,128)(2,1)S(1)} collective-permute-done((bf16[64,1024]{1,0:T(8,128)(2,1)S(1)}, bf16[64,1024]{1,0:T(8,128)(2,1)S(1)}, u32[]{:S(2)}, u32[]{:S(2)}) %collective-permute-start.11) | collective-permute-done | bytes 131104 | tf_op jit(solution)/shard_map/ppermute | solution.py:249
  310.0 5.8 shard_map.147
  315.9 5.5 all-to-all-start.7
  322.7 13.1 %all-to-all-done.7 = bf16[8,272,128]{2,1,0:T(8,128)(2,1)} async-done(((bf16[8,272,128]{2,1,0:T(8,128)(2,1)}), bf16[8,272,128]{2,1,0:T(8,128)(2,1)}, u32[]{:S(2)}, u32[]{:S(2)}) %all-to-all-start.7) | async-done | bytes 557088 | tf_op jit(solution)/shard_map/all_to_all | solution.py:228
  338.0 11.5 %all_to_all.120.p_ref = bf16[8,64,128]{2,1,0:T(8,128)(2,1)S(1)} all-to-all(bf16[8,64,128]{2,1,0:T(8,128)(2,1)S(1)} %get-tuple-element.106), channel_id=1, replica_groups=mesh['dp'=4,'section'=8,'tensor'=8] {'tensor'}, dimensions={0} | all-to-all | bytes 262144 | tf_op jit(solution)/shard_map/all_to_all | solution.py:228
  352.8 7.1 %collective-permute-done.12.refs_0_ = bf16[64,1024]{1,0:T(8,128)(2,1)S(1)} collective-permute-done((bf16[64,1024]{1,0:T(8,128)(2,1)S(1)}, bf16[64,1024]{1,0:T(8,128)(2,1)S(1)}, u32[]{:S(2)}, u32[]{:S(2)}) %collective-permute-start.12) | collective-permute-done | bytes 131104 | tf_op jit(solution)/shard_map/ppermute | solution.py:249
  359.9 5.2 shard_map.149
  365.1 15.6 %all_to_all.121 = bf16[8,272,128]{2,1,0:T(8,128)(2,1)S(1)} all-to-all(bf16[8,272,128]{2,1,0:T(8,128)(2,1)S(1)} %get-tuple-element.64), channel_id=1, replica_groups=mesh['dp'=4,'section'=8,'tensor'=8] {'tensor'}, dimensions={0} | all-to-all | bytes 1114112 | tf_op jit(solution)/shard_map/all_to_all | solution.py:228
  382.4 11.8 %all_to_all.122.p_ref = bf16[8,64,128]{2,1,0:T(8,128)(2,1)S(1)} all-to-all(bf16[8,64,128]{2,1,0:T(8,128)(2,1)S(1)} %get-tuple-element.102), channel_id=1, replica_groups=mesh['dp'=4,'section'=8,'tensor'=8] {'tensor'}, dimensions={0} | all-to-all | bytes 262144 | tf_op jit(solution)/shard_map/all_to_all | solution.py:228
  395.4 7.1 %collective-permute-done.13.refs_0_ = bf16[64,1024]{1,0:T(8,128)(2,1)S(1)} collective-permute-done((bf16[64,1024]{1,0:T(8,128)(2,1)S(1)}, bf16[64,1024]{1,0:T(8,128)(2,1)S(1)}, u32[]{:S(2)}, u32[]{:S(2)}) %collective-permute-start.13) | collective-permute-done | bytes 131104 | tf_op jit(solution)/shard_map/ppermute | solution.py:249
  402.4 5.0 shard_map.151
  407.5 16.0 %all_to_all.123 = bf16[8,272,128]{2,1,0:T(8,128)(2,1)S(1)} all-to-all(bf16[8,272,128]{2,1,0:T(8,128)(2,1)S(1)} %get-tuple-element.67), channel_id=1, replica_groups=mesh['dp'=4,'section'=8,'tensor'=8] {'tensor'}, dimensions={0} | all-to-all | bytes 1114112 | tf_op jit(solution)/shard_map/all_to_all | solution.py:228
  425.2 11.4 %all_to_all.124.p_ref = bf16[8,64,128]{2,1,0:T(8,128)(2,1)S(1)} all-to-all(bf16[8,64,128]{2,1,0:T(8,128)(2,1)S(1)} %get-tuple-element.110), channel_id=1, replica_groups=mesh['dp'=4,'section'=8,'tensor'=8] {'tensor'}, dimensions={0} | all-to-all | bytes 262144 | tf_op jit(solution)/shard_map/all_to_all | solution.py:228
  437.8 7.1 %collective-permute-done.14.refs_0_ = bf16[64,1024]{1,0:T(8,128)(2,1)S(1)} collective-permute-done((bf16[64,1024]{1,0:T(8,128)(2,1)S(1)}, bf16[64,1024]{1,0:T(8,128)(2,1)S(1)}, u32[]{:S(2)}, u32[]{:S(2)}) %collective-permute-start.14) | collective-permute-done | bytes 131104 | tf_op jit(solution)/shard_map/ppermute | solution.py:249
  444.8 5.8 shard_map.153
  450.7 5.5 all-to-all-start.13
  456.3 12.2 %all-to-all-done.13 = bf16[8,272,128]{2,1,0:T(8,128)(2,1)} async-done(((bf16[8,272,128]{2,1,0:T(8,128)(2,1)}), bf16[8,272,128]{2,1,0:T(8,128)(2,1)}, u32[]{:S(2)}, u32[]{:S(2)}) %all-to-all-start.13) | async-done | bytes 557088 | tf_op jit(solution)/shard_map/all_to_all | solution.py:228
  470.9 14.7 %all-to-all-start.14 = ((bf16[8,64,128]{2,1,0:T(8,128)(2,1)}), bf16[8,64,128]{2,1,0:T(8,128)(2,1)S(1)}, u32[]{:S(2)}, u32[]{:S(2)}) async-start(bf16[8,64,128]{2,1,0:T(8,128)(2,1)} %get-tuple-element.122), calls=%async_computation.14 | async-start | bytes 262144 | tf_op jit(solution)/shard_map/all_to_all | solution.py:228
  485.7 6.3 fusion.25
  496.5 7.1 %collective-permute-done.15.refs_0_ = bf16[64,1024]{1,0:T(8,128)(2,1)S(1)} collective-permute-done((bf16[64,1024]{1,0:T(8,128)(2,1)S(1)}, bf16[64,1024]{1,0:T(8,128)(2,1)S(1)}, u32[]{:S(2)}, u32[]{:S(2)}) %collective-permute-start.15) | collective-permute-done | bytes 131104 | tf_op jit(solution)/shard_map/ppermute | solution.py:249
  503.6 5.2 shard_map.155
  508.8 20.2 %all_to_all.125 = bf16[8,272,128]{2,1,0:T(8,128)(2,1)S(1)} all-to-all(bf16[8,272,128]{2,1,0:T(8,128)(2,1)S(1)} %get-tuple-element.75), channel_id=1, replica_groups=mesh['dp'=4,'section'=8,'tensor'=8] {'tensor'}, dimensions={0} | all-to-all | bytes 1114112 | tf_op jit(solution)/shard_map/all_to_all | solution.py:228
  530.6 11.5 %all_to_all.126.p_ref = bf16[8,64,128]{2,1,0:T(8,128)(2,1)S(1)} all-to-all(bf16[8,64,128]{2,1,0:T(8,128)(2,1)S(1)} %get-tuple-element.98), channel_id=1, replica_groups=mesh['dp'=4,'section'=8,'tensor'=8] {'tensor'}, dimensions={0} | all-to-all | bytes 262144 | tf_op jit(solution)/shard_map/all_to_all | solution.py:228
  543.2 7.1 %collective-permute-done.16.refs_0_ = bf16[64,1024]{1,0:T(8,128)(2,1)S(1)} collective-permute-done((bf16[64,1024]{1,0:T(8,128)(2,1)S(1)}, bf16[64,1024]{1,0:T(8,128)(2,1)S(1)}, u32[]{:S(2)}, u32[]{:S(2)}) %collective-permute-start.16) | collective-permute-done | bytes 131104 | tf_op jit(solution)/shard_map/ppermute | solution.py:249
  550.3 5.0 shard_map.157
  555.3 16.0 %all_to_all.127 = bf16[8,272,128]{2,1,0:T(8,128)(2,1)S(1)} all-to-all(bf16[8,272,128]{2,1,0:T(8,128)(2,1)S(1)} %get-tuple-element.78), channel_id=1, replica_groups=mesh['dp'=4,'section'=8,'tensor'=8] {'tensor'}, dimensions={0} | all-to-all | bytes 1114112 | tf_op jit(solution)/shard_map/all_to_all | solution.py:228
  573.1 11.5 %all_to_all.128.p_ref = bf16[8,64,128]{2,1,0:T(8,128)(2,1)S(1)} all-to-all(bf16[8,64,128]{2,1,0:T(8,128)(2,1)S(1)} %get-tuple-element.114), channel_id=1, replica_groups=mesh['dp'=4,'section'=8,'tensor'=8] {'tensor'}, dimensions={0} | all-to-all | bytes 262144 | tf_op jit(solution)/shard_map/all_to_all | solution.py:228
  585.6 7.1 %collective-permute-done.17.refs_0_ = bf16[64,1024]{1,0:T(8,128)(2,1)S(1)} collective-permute-done((bf16[64,1024]{1,0:T(8,128)(2,1)S(1)}, bf16[64,1024]{1,0:T(8,128)(2,1)S(1)}, u32[]{:S(2)}, u32[]{:S(2)}) %collective-permute-start.17) | collective-permute-done | bytes 131104 | tf_op jit(solution)/shard_map/ppermute | solution.py:249
  592.7 5.8 shard_map.159
  599.2 5.7 all-to-all-start.19
  607.5 9.7 %all-to-all-done.19 = bf16[8,272,128]{2,1,0:T(8,128)(2,1)} async-done(((bf16[8,272,128]{2,1,0:T(8,128)(2,1)}), bf16[8,272,128]{2,1,0:T(8,128)(2,1)}, u32[]{:S(2)}, u32[]{:S(2)}) %all-to-all-start.19) | async-done | bytes 557088 | tf_op jit(solution)/shard_map/all_to_all | solution.py:228
  619.5 4.7 all-to-all-start.20
  625.9 5.5 shard_map.160
  631.4 3.6 convolution_convert_fusion
  636.9 6.5 all-to-all-start.21
  646.6 3.3 shard_map.168
  651.0 3.4 collective-permute-start.18
  654.4 5.5 collective-permute-start.21
  660.0 6.0 collective-permute-start.19
  672.6 3.4 all-to-all-start.22
  676.7 5.8 all-to-all-done.22
  (152 shorter events, 69.8 us)
Async XLA Ops:
  7.2 478.5 %copy-start = (bf16[1,2,64,8192]{3,2,1,0:T(8,128)(2,1)S(1)}, bf16[1,2,64,8192]{3,2,1,0:T(8,128)(2,1)}, u32[]{:S(2)}) copy-start(bf16[1,2,64,8192]{3,2,1,0:T(8,128)(2,1)} %param.25) | copy-start | bytes 6291460
  7.2 16.4 %copy-start.11 = (bf16[1,2048,128]{2,1,0:T(8,128)(2,1)S(1)}, bf16[1,2048,128]{2,1,0:T(8,128)(2,1)}, u32[]{:S(2)}) copy-start(bf16[1,2048,128]{2,1,0:T(8,128)(2,1)} %param.20) | copy-start | bytes 1572868
  7.2 16.4 %copy-start.12 = (bf16[1,2048,128]{2,1,0:T(8,128)(2,1)S(1)}, bf16[1,2048,128]{2,1,0:T(8,128)(2,1)}, u32[]{:S(2)}) copy-start(bf16[1,2048,128]{2,1,0:T(8,128)(2,1)} %param.19) | copy-start | bytes 1572868
  7.2 54.8 %all-gather.4.cloned.1.call-start = ((), (), s32[]{:S(2)}) async-start(), calls=%async_computation.23 | async-start | bytes 1179648 | tf_op jit(solution)/shard_map/all_gather | solution.py:283
  23.6 100.1 %all-gather.6.cloned.1.call-start = ((), (), s32[]{:S(2)}) async-start(), calls=%async_computation.24 | async-start | bytes 5242880 | tf_op jit(solution)/shard_map/all_gather | solution.py:285
  112.8 42.6 %collective-permute-start.5 = (bf16[8,256,512]{2,1,0:T(8,128)(2,1)}, bf16[8,256,512]{2,1,0:T(8,128)(2,1)}, u32[]{:S(2)}, u32[]{:S(2)}) collective-permute-start(bf16[8,256,512]{2,1,0:T(8,128)(2,1)} %all_to_all.116.refs_0_.refs_1_), channel_id=1, source_target_pairs={{0,128},{64,192},{128,0},{192,64},{1,129},{65,193},{129,1},{193,65... | collective-permute-start | bytes 6291464 | tf_op jit(solution)/shard_map/ppermute | solution.py:252
  123.6 32.2 %copy-start.14 = (f32[1,8192]{1,0:T(1,128)S(1)}, f32[1,8192]{1,0:T(1,128)}, u32[]{:S(2)}) copy-start(f32[1,8192]{1,0:T(1,128)} %param.17) | copy-start | bytes 98308
  123.6 33.0 %copy-start.13 = (bf16[2,64,1024]{2,1,0:T(8,128)(2,1)S(1)}, bf16[2,64,1024]{2,1,0:T(8,128)(2,1)}, u32[]{:S(2)}) copy-start(bf16[2,64,1024]{2,1,0:T(8,128)(2,1)} %param.13) | copy-start | bytes 786436
  123.6 61.4 %all-to-all-start.4 = ((bf16[8,512,256]{2,1,0:T(8,128)(2,1)}), bf16[8,512,256]{2,1,0:T(8,128)(2,1)}, u32[]{:S(2)}, u32[]{:S(2)}) async-start(bf16[8,512,256]{2,1,0:T(8,128)(2,1)} %bitcast.154), calls=%async_computation.4 | async-start | bytes 4194304 | tf_op jit(solution)/shard_map/all_to_all | solution.py:228
  129.5 49.7 %collective-permute-start.4 = (bf16[8,256,512]{2,1,0:T(8,128)(2,1)}, bf16[8,256,512]{2,1,0:T(8,128)(2,1)}, u32[]{:S(2)}, u32[]{:S(2)}) collective-permute-start(bf16[8,256,512]{2,1,0:T(8,128)(2,1)} %all_to_all.116.refs_0_.refs_1_), channel_id=1, source_target_pairs={{0,64},{64,0},{128,192},{192,128},{1,65},{65,1},{129,193},{193,129... | collective-permute-start | bytes 6291464 | tf_op jit(solution)/shard_map/ppermute | solution.py:252
  155.4 23.8 %collective-permute-start.6 = (bf16[8,256,512]{2,1,0:T(8,128)(2,1)}, bf16[8,256,512]{2,1,0:T(8,128)(2,1)}, u32[]{:S(2)}, u32[]{:S(2)}) collective-permute-start(bf16[8,256,512]{2,1,0:T(8,128)(2,1)} %collective-permute-done.5.refs_2_.refs_3_), channel_id=1, source_target_pairs={{0,64},{64,0},{128,192},{192,128},{1,65},{65,1},{129,193},{193,129... | collective-permute-start | bytes 6291464 | tf_op jit(solution)/shard_map/ppermute | solution.py:252
  157.5 15.4 %collective-permute-start = (bf16[2,64,256]{2,1,0:T(8,128)(2,1)S(1)}, bf16[2,64,256]{2,1,0:T(8,128)(2,1)S(1)}, u32[]{:S(2)}, u32[]{:S(2)}) collective-permute-start(bf16[2,64,256]{2,1,0:T(8,128)(2,1)S(1)} %get-tuple-element.144), channel_id=1, source_target_pairs={{0,0},{1,4},{2,1},{3,5},{4,2},{5,6},{6,3},{7,7},{8,8},{9,12},{10,9... | collective-permute-start | bytes 196616 | tf_op jit(solution)/shard_map/ppermute | solution.py:264
  160.3 16.9 %collective-permute-start.3 = (bf16[2,64,256]{2,1,0:T(8,128)(2,1)S(1)}, bf16[2,64,256]{2,1,0:T(8,128)(2,1)S(1)}, u32[]{:S(2)}, u32[]{:S(2)}) collective-permute-start(bf16[2,64,256]{2,1,0:T(8,128)(2,1)S(1)} %get-tuple-element.145), channel_id=1, source_target_pairs={{0,3},{1,7},{2,0},{3,4},{4,1},{5,5},{6,2},{7,6},{8,11},{9,15},{10,... | collective-permute-start | bytes 196616 | tf_op jit(solution)/shard_map/ppermute | solution.py:264
  162.3 15.0 %collective-permute-start.2 = (bf16[2,64,256]{2,1,0:T(8,128)(2,1)S(1)}, bf16[2,64,256]{2,1,0:T(8,128)(2,1)S(1)}, u32[]{:S(2)}, u32[]{:S(2)}) collective-permute-start(bf16[2,64,256]{2,1,0:T(8,128)(2,1)S(1)} %get-tuple-element.146), channel_id=1, source_target_pairs={{0,2},{1,6},{2,3},{3,7},{4,0},{5,4},{6,1},{7,5},{8,10},{9,14},{10,... | collective-permute-start | bytes 196616 | tf_op jit(solution)/shard_map/ppermute | solution.py:264
  172.9 6.1 collective-permute-start.1
  185.0 47.7 %collective-permute-start.8 = (bf16[8,512,256]{2,1,0:T(8,128)(2,1)}, bf16[8,512,256]{2,1,0:T(8,128)(2,1)}, u32[]{:S(2)}, u32[]{:S(2)}) collective-permute-start(bf16[8,512,256]{2,1,0:T(8,128)(2,1)} %all-to-all-done.4.refs_0_), channel_id=1, source_target_pairs={{0,128},{64,192},{128,0},{192,64},{1,129},{65,193},{129,1},{193,65... | collective-permute-start | bytes 6291464 | tf_op jit(solution)/shard_map/ppermute | solution.py:252
  187.5 24.7 %all-to-all-start.2 = ((bf16[8,272,128]{2,1,0:T(8,128)(2,1)}), bf16[8,272,128]{2,1,0:T(8,128)(2,1)S(1)}, u32[]{:S(2)}, u32[]{:S(2)}) async-start(bf16[8,272,128]{2,1,0:T(8,128)(2,1)} %get-tuple-element.52), calls=%async_computation.2 | async-start | bytes 1114112 | tf_op jit(solution)/shard_map/all_to_all | solution.py:228
  195.9 4.1 copy-start.15
  195.9 16.4 %copy-start.10 = (f32[1,128]{1,0:T(1,128)S(1)}, f32[1,128]{1,0:T(1,128)}, u32[]{:S(2)}) copy-start(f32[1,128]{1,0:T(1,128)} %gain_ref.11) | copy-start | bytes 1540
  195.9 289.8 %all-gather.8.cloned.1.call-start = ((), (), s32[]{:S(2)}) async-start(), calls=%async_computation.25 | async-start | bytes 10485760 | tf_op jit(solution)/shard_map/all_gather | solution.py:318
  200.0 417.1 %copy-start.7 = (f32[2,32,128]{2,1,0:T(8,128)}, f32[2,32,128]{2,1,0:T(8,128)S(1)}, u32[]{:S(2)}) copy-start(f32[2,32,128]{2,1,0:T(8,128)S(1)} %multiply_multiply_fusion.k_ref) | copy-start | bytes 98308
  227.3 5.4 collective-permute-start.7
  232.7 4.4 collective-permute-start.9
  241.6 1.9 copy-start.1
  243.6 7.7 %collective-permute-start.10 = (bf16[64,1024]{1,0:T(8,128)(2,1)S(1)}, bf16[64,1024]{1,0:T(8,128)(2,1)S(1)}, u32[]{:S(2)}, u32[]{:S(2)}) collective-permute-start(bf16[64,1024]{1,0:T(8,128)(2,1)S(1)} %shard_map.143), channel_id=1, source_target_pairs={{0,8},{8,16},{16,24},{24,32},{32,40},{40,48},{48,56},{56,0},{1,9},... | collective-permute-start | bytes 393224 | tf_op jit(solution)/shard_map/ppermute | solution.py:249
  296.5 2.3 copy-start.2
  299.8 10.2 %collective-permute-start.11 = (bf16[64,1024]{1,0:T(8,128)(2,1)S(1)}, bf16[64,1024]{1,0:T(8,128)(2,1)S(1)}, u32[]{:S(2)}, u32[]{:S(2)}) collective-permute-start(bf16[64,1024]{1,0:T(8,128)(2,1)S(1)} %shard_map.146), channel_id=1, source_target_pairs={{0,8},{8,16},{16,24},{24,32},{32,40},{40,48},{48,56},{56,0},{1,9},... | collective-permute-start | bytes 393224 | tf_op jit(solution)/shard_map/ppermute | solution.py:249
  315.9 20.0 %all-to-all-start.7 = ((bf16[8,272,128]{2,1,0:T(8,128)(2,1)}), bf16[8,272,128]{2,1,0:T(8,128)(2,1)}, u32[]{:S(2)}, u32[]{:S(2)}) async-start(bf16[8,272,128]{2,1,0:T(8,128)(2,1)} %get-tuple-element.61), calls=%async_computation.7 | async-start | bytes 1114112 | tf_op jit(solution)/shard_map/all_to_all | solution.py:228
  349.5 2.2 copy-start.3
  352.7 7.2 %collective-permute-start.12 = (bf16[64,1024]{1,0:T(8,128)(2,1)S(1)}, bf16[64,1024]{1,0:T(8,128)(2,1)S(1)}, u32[]{:S(2)}, u32[]{:S(2)}) collective-permute-start(bf16[64,1024]{1,0:T(8,128)(2,1)S(1)} %shard_map.148), channel_id=1, source_target_pairs={{0,8},{8,16},{16,24},{24,32},{32,40},{40,48},{48,56},{56,0},{1,9},... | collective-permute-start | bytes 393224 | tf_op jit(solution)/shard_map/ppermute | solution.py:249
  359.9 34.4 %copy-start.4 = (bf16[2,1024,1024]{2,1,0:T(8,128)(2,1)S(1)}, bf16[2,1024,1024]{2,1,0:T(8,128)(2,1)}, u32[]{:S(2)}) copy-start(bf16[2,1024,1024]{2,1,0:T(8,128)(2,1)} %copy-done.1) | copy-start | bytes 12582916
  395.3 7.2 %collective-permute-start.13 = (bf16[64,1024]{1,0:T(8,128)(2,1)S(1)}, bf16[64,1024]{1,0:T(8,128)(2,1)S(1)}, u32[]{:S(2)}, u32[]{:S(2)}) collective-permute-start(bf16[64,1024]{1,0:T(8,128)(2,1)S(1)} %shard_map.150), channel_id=1, source_target_pairs={{0,8},{8,16},{16,24},{24,32},{32,40},{40,48},{48,56},{56,0},{1,9},... | collective-permute-start | bytes 393224 | tf_op jit(solution)/shard_map/ppermute | solution.py:249
  437.7 7.2 %collective-permute-start.14 = (bf16[64,1024]{1,0:T(8,128)(2,1)S(1)}, bf16[64,1024]{1,0:T(8,128)(2,1)S(1)}, u32[]{:S(2)}, u32[]{:S(2)}) collective-permute-start(bf16[64,1024]{1,0:T(8,128)(2,1)S(1)} %shard_map.152), channel_id=1, source_target_pairs={{0,8},{8,16},{16,24},{24,32},{32,40},{40,48},{48,56},{56,0},{1,9},... | collective-permute-start | bytes 393224 | tf_op jit(solution)/shard_map/ppermute | solution.py:249
  450.7 17.8 %all-to-all-start.13 = ((bf16[8,272,128]{2,1,0:T(8,128)(2,1)}), bf16[8,272,128]{2,1,0:T(8,128)(2,1)}, u32[]{:S(2)}, u32[]{:S(2)}) async-start(bf16[8,272,128]{2,1,0:T(8,128)(2,1)} %get-tuple-element.70), calls=%async_computation.13 | async-start | bytes 1114112 | tf_op jit(solution)/shard_map/all_to_all | solution.py:228
  470.9 22.3 %all-to-all-start.14 = ((bf16[8,64,128]{2,1,0:T(8,128)(2,1)}), bf16[8,64,128]{2,1,0:T(8,128)(2,1)S(1)}, u32[]{:S(2)}, u32[]{:S(2)}) async-start(bf16[8,64,128]{2,1,0:T(8,128)(2,1)} %get-tuple-element.122), calls=%async_computation.14 | async-start | bytes 262144 | tf_op jit(solution)/shard_map/all_to_all | solution.py:228
  493.2 2.2 copy-start.5
  496.4 7.2 %collective-permute-start.15 = (bf16[64,1024]{1,0:T(8,128)(2,1)S(1)}, bf16[64,1024]{1,0:T(8,128)(2,1)S(1)}, u32[]{:S(2)}, u32[]{:S(2)}) collective-permute-start(bf16[64,1024]{1,0:T(8,128)(2,1)S(1)} %shard_map.154), channel_id=1, source_target_pairs={{0,8},{8,16},{16,24},{24,32},{32,40},{40,48},{48,56},{56,0},{1,9},... | collective-permute-start | bytes 393224 | tf_op jit(solution)/shard_map/ppermute | solution.py:249
  503.6 38.5 %copy-start.6 = (bf16[2,1024,1024]{2,1,0:T(8,128)(2,1)S(1)}, bf16[2,1024,1024]{2,1,0:T(8,128)(2,1)}, u32[]{:S(2)}) copy-start(bf16[2,1024,1024]{2,1,0:T(8,128)(2,1)} %copy-done.1) | copy-start | bytes 12582916
  543.1 7.2 %collective-permute-start.16 = (bf16[64,1024]{1,0:T(8,128)(2,1)S(1)}, bf16[64,1024]{1,0:T(8,128)(2,1)S(1)}, u32[]{:S(2)}, u32[]{:S(2)}) collective-permute-start(bf16[64,1024]{1,0:T(8,128)(2,1)S(1)} %shard_map.156), channel_id=1, source_target_pairs={{0,8},{8,16},{16,24},{24,32},{32,40},{40,48},{48,56},{56,0},{1,9},... | collective-permute-start | bytes 393224 | tf_op jit(solution)/shard_map/ppermute | solution.py:249
  585.5 7.2 %collective-permute-start.17 = (bf16[64,1024]{1,0:T(8,128)(2,1)S(1)}, bf16[64,1024]{1,0:T(8,128)(2,1)S(1)}, u32[]{:S(2)}, u32[]{:S(2)}) collective-permute-start(bf16[64,1024]{1,0:T(8,128)(2,1)S(1)} %shard_map.158), channel_id=1, source_target_pairs={{0,8},{8,16},{16,24},{24,32},{32,40},{40,48},{48,56},{56,0},{1,9},... | collective-permute-start | bytes 393224 | tf_op jit(solution)/shard_map/ppermute | solution.py:249
  598.5 0.6 copy-start.8
  599.2 5.7 copy-start.16
  599.2 18.0 %all-to-all-start.19 = ((bf16[8,272,128]{2,1,0:T(8,128)(2,1)}), bf16[8,272,128]{2,1,0:T(8,128)(2,1)}, u32[]{:S(2)}, u32[]{:S(2)}) async-start(bf16[8,272,128]{2,1,0:T(8,128)(2,1)} %get-tuple-element.81), calls=%async_computation.19 | async-start | bytes 1114112 | tf_op jit(solution)/shard_map/all_to_all | solution.py:228
  619.5 17.3 %all-to-all-start.20 = ((bf16[8,64,128]{2,1,0:T(8,128)(2,1)}), bf16[8,64,128]{2,1,0:T(8,128)(2,1)S(1)}, u32[]{:S(2)}, u32[]{:S(2)}) async-start(bf16[8,64,128]{2,1,0:T(8,128)(2,1)} %get-tuple-element.118), calls=%async_computation.20 | async-start | bytes 262144 | tf_op jit(solution)/shard_map/all_to_all | solution.py:228
  636.9 33.5 %all-to-all-start.21 = ((bf16[8,64,1024]{2,1,0:T(8,128)(2,1)}), bf16[8,64,1024]{2,1,0:T(8,128)(2,1)}, u32[]{:S(2)}, u32[]{:S(2)}) async-start(bf16[8,64,1024]{2,1,0:T(8,128)(2,1)} %bitcast.157), calls=%async_computation.21 | async-start | bytes 2097152 | tf_op jit(solution)/shard_map/all_to_all | solution.py:228
  643.3 3.3 copy-start.9
  651.0 19.3 %collective-permute-start.18 = (bf16[2,64,256]{2,1,0:T(8,128)(2,1)S(1)}, bf16[2,64,256]{2,1,0:T(8,128)(2,1)S(1)}, u32[]{:S(2)}, u32[]{:S(2)}) collective-permute-start(bf16[2,64,256]{2,1,0:T(8,128)(2,1)S(1)} %get-tuple-element.134), channel_id=1, source_target_pairs={{0,0},{4,1},{1,2},{5,3},{2,4},{6,5},{3,6},{7,7},{8,8},{12,9},{9,10... | collective-permute-start | bytes 196616 | tf_op jit(solution)/shard_map/ppermute | solution.py:274
  654.4 15.9 %collective-permute-start.21 = (bf16[2,64,256]{2,1,0:T(8,128)(2,1)S(1)}, bf16[2,64,256]{2,1,0:T(8,128)(2,1)S(1)}, u32[]{:S(2)}, u32[]{:S(2)}) collective-permute-start(bf16[2,64,256]{2,1,0:T(8,128)(2,1)S(1)} %get-tuple-element.135), channel_id=1, source_target_pairs={{3,0},{7,1},{0,2},{4,3},{1,4},{5,5},{2,6},{6,7},{11,8},{15,9},{8,1... | collective-permute-start | bytes 196616 | tf_op jit(solution)/shard_map/ppermute | solution.py:274
  659.8 10.4 %collective-permute-start.20 = (bf16[2,64,256]{2,1,0:T(8,128)(2,1)S(1)}, bf16[2,64,256]{2,1,0:T(8,128)(2,1)S(1)}, u32[]{:S(2)}, u32[]{:S(2)}) collective-permute-start(bf16[2,64,256]{2,1,0:T(8,128)(2,1)S(1)} %get-tuple-element.136), channel_id=1, source_target_pairs={{2,0},{6,1},{3,2},{7,3},{0,4},{4,5},{1,6},{5,7},{10,8},{14,9},{11,... | collective-permute-start | bytes 196616 | tf_op jit(solution)/shard_map/ppermute | solution.py:274
  660.0 10.3 %collective-permute-start.19 = (bf16[2,64,256]{2,1,0:T(8,128)(2,1)S(1)}, bf16[2,64,256]{2,1,0:T(8,128)(2,1)S(1)}, u32[]{:S(2)}, u32[]{:S(2)}) collective-permute-start(bf16[2,64,256]{2,1,0:T(8,128)(2,1)S(1)} %get-tuple-element.137), channel_id=1, source_target_pairs={{1,0},{5,1},{2,2},{6,3},{3,4},{7,5},{0,6},{4,7},{9,8},{13,9},{10,1... | collective-permute-start | bytes 196616 | tf_op jit(solution)/shard_map/ppermute | solution.py:274
  672.6 9.9 %all-to-all-start.22 = ((bf16[8,2,4,1024]{3,2,1,0:T(4,128)(2,1)}), bf16[8,2,4,1024]{3,2,1,0:T(4,128)(2,1)S(1)}, u32[]{:S(2)}, u32[]{:S(2)}) async-start(bf16[8,2,4,1024]{3,2,1,0:T(4,128)(2,1)} %copy.27), calls=%async_computation.22 | async-start | bytes 262144 | tf_op jit(solution)/shard_map/all_to_all | solution.py:228
Sparse Core Ops, SparseCore 0:
  23.7 38.2 all-gather.3
  63.8 40.0 all-gather.5
  284.9 58.6 all-gather.7
where the time goes:
time: 696 us; the launch traced here: 690 us
  blocking collectives  241 us (35%)
  waiting for transfers between devices  193 us (28%)
  starting transfers between devices  96.8 us (14%)
  Pallas kernels  69.5 us (10%)
  local copies, waits for them, and re-layouts  48.5 us (7%)
  between operations  18.9 us (3%)
  matrix products  13.2 us (2%)
  other arithmetic  9.45 us (1%)
    all_to_all x14, blocking collectives, swap(): return lax.all_to_all(x, axis, 0, 0, tiled=True)  241 us
    all_to_all x9, starting transfers between devices, swap(): return lax.all_to_all(x, axis, 0, 0, tiled=True)  60.1 us
    ppermute x8, waiting for transfers between devices, onward(): return lax.ppermute(x, 'section', [(i, (i + 1) % S) for i in range(S)])  58.4 us
    all_to_all x9, waiting for transfers between devices, swap(): return lax.all_to_all(x, axis, 0, 0, tiled=True)  54.3 us
    pallas_call x9, Pallas kernels, query(): pl.pallas_call(functools.partial(query_kernel, step), in_specs=[pl.BlockS...  48.8 us
    all_gather x1, waiting for transfers between devices, per_device(): lax.all_gather(shared.reshape(slots * toks, feats), 'tensor', axis=1, til...  37.2 us
    ppermute x6, waiting for transfers between devices, dp_flip(): return lax.ppermute(x, 'dp', [(i, i ^ m) for i in range(D)])  35.6 us
    unnamed x46, local copies, waits for them, and re-layouts  19.2 us
  transfers between devices with their start and end apart: 34, of which 22 were waited for; matrix products, arithmetic and copies ran while one was open for 7% of the time, Pallas kernels for 6%

commit v1 on v0

--- a/solution.py
+++ b/solution.py
@@ -30,8 +30,16 @@
 
 
 def query_kernel(step, ints, text_ref, gain_ref, *refs):
-    h_ref = refs[0] if len(refs) == 7 else None
-    w_refs, q_ref, hq_ref = refs[-6:-2], refs[-2], refs[-1]
+    h_ref = refs[0] if len(refs) == 9 else None
+    w_refs, q_ref, hq_ref, w_s, sems = refs[-8:-4], refs[-4], refs[-3], refs[-2], refs[-1]
+    n, chunk, cols = w_refs[0].shape
+    copies = []
+    for half in range(2):
+        at = pl.ds(half * (n // 2), n // 2)
+        for j in range(4):
+            copy = pltpu.make_async_copy(w_refs[j].at[at], w_s.at[j, at], sems.at[half, j])
+            copy.start()
+            copies.append(copy)
     h = text_ref[slot_of(step, ints, text_ref.shape[0])]
     if h_ref is not None:
         h = jnp.where(ints[0] == 0, h, h_ref[...])
@@ -45,11 +53,13 @@
     pair = jnp.where(own, jnp.where(lane < rows, hi, ss - hi), 0.0)
     pair = jnp.broadcast_to(jnp.sum(pair, axis=0, keepdims=True), (EXTRA, LANES))
     pair = pair.astype(jnp.bfloat16)
-    n, chunk, cols = w_refs[0].shape
     for k in range(n):
-        acc = dot16(x[:, :chunk], w_refs[0][k])
+        if k % (n // 2) == 0:
+            for copy in copies[k // (n // 2) * 4 :][:4]:
+                copy.wait()
+        acc = dot16(x[:, :chunk], w_s[0, k])
         for j in range(1, 4):
-            acc += dot16(x[:, j * chunk : (j + 1) * chunk], w_refs[j][k])
+            acc += dot16(x[:, j * chunk : (j + 1) * chunk], w_s[j, k])
         acc = acc.astype(jnp.bfloat16)
         for i in range(cols // LANES):
             q_ref[k, i * rows : (i + 1) * rows, :] = acc[:, i * LANES : (i + 1) * LANES]
@@ -58,36 +68,54 @@
 
 def query(step, ints, text, gain, h, w):
     rows, feats = text.shape[1:]
-    n, _, cols = w[0].shape
-    args = [text, gain] + ([] if h is None else [h]) + list(w)
+    n, chunk, cols = w[0].shape
+    args = [text, gain] + ([] if h is None else [h])
     return pl.pallas_call(
         functools.partial(query_kernel, step),
         in_specs=[pl.BlockSpec(memory_space=pltpu.SMEM)]
-        + [pl.BlockSpec(memory_space=pltpu.VMEM)] * len(args),
+        + [pl.BlockSpec(memory_space=pltpu.VMEM)] * len(args)
+        + [pl.BlockSpec(memory_space=pl.ANY)] * 4,
         out_specs=[pl.BlockSpec(memory_space=pltpu.VMEM)] * 2,
         out_shape=[
             jax.ShapeDtypeStruct((n, cols // LANES * rows + EXTRA, LANES), jnp.bfloat16),
             jax.ShapeDtypeStruct((rows, feats), jnp.bfloat16),
         ],
+        scratch_shapes=[
+            pltpu.VMEM((4, n, chunk, cols), jnp.bfloat16),
+            pltpu.SemaphoreType.DMA((2, 4)),
+        ],
         compiler_params=pltpu.CompilerParams(vmem_limit_bytes=VMEM_BYTES),
-    )(ints, *args)
-
-
-def output_kernel(step, ints, p_ref, vo_ref, h_ref, o_ref):
+    )(ints, *args, *w)
+
+
+def keep(step, ints, kept_ref, new, old_ref):
+    for o in range(kept_ref.shape[0]):
+        old = jnp.zeros(new.shape, new.dtype) if old_ref is None else old_ref[o]
+        kept_ref[o] = jnp.where(step - ints[0] == o, new, old)
+
+
+def output_kernel(step, ints, p_ref, vo_ref, h_ref, *refs):
+    o_ref, kept_ref = refs[-2:]
     probs = jnp.concatenate([p_ref[i] for i in range(p_ref.shape[0])], axis=1)
     new = h_ref[...].astype(jnp.float32) + dot16(probs, vo_ref[slot_of(step, ints, vo_ref.shape[0])])
-    o_ref[...] = new.astype(jnp.bfloat16)
-
-
-def output(step, ints, probs, vo, h):
+    new = new.astype(jnp.bfloat16)
+    o_ref[...] = new
+    keep(step, ints, kept_ref, new, refs[0] if len(refs) == 3 else None)
+
+
+def output(step, ints, probs, vo, h, kept):
+    args = [probs, vo, h] + ([] if kept is None else [kept])
     return pl.pallas_call(
         functools.partial(output_kernel, step),
         in_specs=[pl.BlockSpec(memory_space=pltpu.SMEM)]
-        + [pl.BlockSpec(memory_space=pltpu.VMEM)] * 3,
-        out_specs=pl.BlockSpec(memory_space=pltpu.VMEM),
-        out_shape=jax.ShapeDtypeStruct(h.shape, jnp.bfloat16),
+        + [pl.BlockSpec(memory_space=pltpu.VMEM)] * len(args),
+        out_specs=[pl.BlockSpec(memory_space=pltpu.VMEM)] * 2,
+        out_shape=[
+            jax.ShapeDtypeStruct(h.shape, jnp.bfloat16),
+            jax.ShapeDtypeStruct(vo.shape[:1] + h.shape, jnp.bfloat16),
+        ],
         compiler_params=pltpu.CompilerParams(vmem_limit_bytes=VMEM_BYTES),
-    )(ints, probs, vo, h)
+    )(ints, *args)
 
 
 def own_lanes(rows):
@@ -100,13 +128,14 @@
     return pl.BlockSpec(shape, lambda *_: (0,) * len(shape))
 
 
-def attend_kernel(step, width, ints, alpha_ref, gain_ref, k_ref, q_ref, p_ref, qn_ref):
+def attend_kernel(step, width, ints, alpha_ref, gain_ref, k_ref, q_ref, *refs):
+    p_ref, kept_ref = refs[-2:]
     slot = slot_of(step, ints, k_ref.shape[0])
     total = q_ref[0].astype(jnp.float32)
     for i in range(1, q_ref.shape[0]):
         total += q_ref[i].astype(jnp.float32)
     hd = gain_ref.shape[1]
-    rows, cols = qn_ref.shape
+    rows, cols = kept_ref.shape[1:]
     own, _ = own_lanes(rows)
     sums = jnp.broadcast_to(total[cols // hd * rows : cols // hd * rows + 1], (rows, LANES))
     ss = jnp.sum(jnp.where(own, sums, 0.0), axis=1, keepdims=True)
@@ -114,51 +143,57 @@
     keys = k_ref[slot]
     row = lax.broadcasted_iota(jnp.int32, (rows, keys.shape[0]), 0)
     scale = jnp.where(row < ints[1 + slot], alpha_ref[0], 0.0)
-    parts = []
+    parts, normed = [], []
     for h in range(cols // hd):
         q = total[h * rows : (h + 1) * rows] * rs
         r = lax.rsqrt(jnp.mean(q * q, axis=1, keepdims=True) + EPS)
         qn = q * r * gain_ref[...] * (1.0 / math.sqrt(hd))
-        qn_ref[:, h * hd : (h + 1) * hd] = qn
+        normed.append(qn)
         sc = dot32(qn, keys, ROWS_ROWS)
         e = jnp.exp(sc - jnp.max(sc, axis=1, keepdims=True))
         parts.append(scale * e / jnp.sum(e, axis=1, keepdims=True))
     p = jnp.concatenate(parts, axis=1).astype(jnp.bfloat16)
     for i in range(p_ref.shape[0]):
         p_ref[i] = p
-
-
-def attend(step, ints, alpha, width, gain, keys, parts):
+    old_ref = refs[0] if len(refs) == 3 else None
+    keep(step, ints, kept_ref, jnp.concatenate(normed, axis=1), old_ref)
+
+
+def attend(step, ints, alpha, width, gain, keys, parts, kept):
     hd = gain.shape[1]
     toks = keys.shape[1]
     heads = 4
     n = parts.shape[0]
     rows = (parts.shape[1] - EXTRA) // heads
+    args = [gain, keys, parts] + ([] if kept is None else [kept])
     return pl.pallas_call(
         functools.partial(attend_kernel, step, width),
         in_specs=[pl.BlockSpec(memory_space=pltpu.SMEM)] * 2
-        + [pl.BlockSpec(memory_space=pltpu.VMEM)] * 3,
+        + [pl.BlockSpec(memory_space=pltpu.VMEM)] * len(args),
         out_specs=[pl.BlockSpec(memory_space=pltpu.VMEM)] * 2,
         out_shape=[
             jax.ShapeDtypeStruct((n, rows, heads * toks), jnp.bfloat16),
-            jax.ShapeDtypeStruct((rows, heads * hd), jnp.float32),
+            jax.ShapeDtypeStruct(keys.shape[:1] + (rows, heads * hd), jnp.float32),
         ],
         compiler_params=pltpu.CompilerParams(vmem_limit_bytes=VMEM_BYTES),
-    )(ints, alpha, gain, keys, parts)
+    )(ints, alpha, *args)
 
 
 def value_out_kernel(slots, v_ref, *refs):
-    w_refs, o_ref = refs[:4], refs[4]
+    w_refs, o_ref = refs[:-1], refs[-1]
     n, vrows, hd = v_ref.shape
     toks = vrows // slots
-    heads, chunk = w_refs[0].shape[1] // hd, w_refs[0].shape[2]
+    part, chunk = w_refs[0].shape[1] // hd, w_refs[0].shape[2]
+    heads = part * len(w_refs) // 4
 
     def block(k, carry):
         v = v_ref[k]
         for h in range(heads):
             at = pl.multiple_of((k * heads + h) * toks, toks)
             for j in range(4):
-                r = dot16(v, w_refs[j][k, h * hd : (h + 1) * hd, :]).astype(jnp.bfloat16)
+                w_ref = w_refs[h // part * 4 + j]
+                i = h % part * hd
+                r = dot16(v, w_ref[k, i : i + hd, :]).astype(jnp.bfloat16)
                 for o in range(slots):
                     o_ref[o, pl.ds(at, toks), j * chunk : (j + 1) * chunk] = r[
                         o * toks : (o + 1) * toks
@@ -170,26 +205,26 @@
 
 def value_out(v, w, slots):
     n, vrows, hd = v.shape
-    heads = w[0].shape[1] // hd
+    heads = w[0].shape[1] * len(w) // 4 // hd
     chunk = w[0].shape[2]
     toks = vrows // slots
     return pl.pallas_call(
         functools.partial(value_out_kernel, slots),
-        in_specs=[pl.BlockSpec(memory_space=pltpu.VMEM)] * 5,
+        in_specs=[pl.BlockSpec(memory_space=pltpu.VMEM)] * (1 + len(w)),
         out_specs=pl.BlockSpec(memory_space=pltpu.VMEM),
         out_shape=jax.ShapeDtypeStruct((slots, n * heads * toks, 4 * chunk), jnp.bfloat16),
-        compiler_params=pltpu.CompilerParams(vmem_limit_bytes=VMEM_BYTES),
+        compiler_params=pltpu.CompilerParams(vmem_limit_bytes=2 * VMEM_BYTES),
     )(v, *w)
 
 
-def back_kernel(qn_ref, k_ref, v_ref, raw_ref, da_ref, gain_ref, o_ref):
-    keys, vals, raw, gain = k_ref[0], v_ref[0], raw_ref[0], gain_ref[...]
+def back_kernel(slot, qn_ref, k_ref, v_ref, raw_ref, da_ref, gain_ref, w_ref, o_ref):
+    keys, vals, raw, gain = k_ref[slot], v_ref[slot], raw_ref[slot], gain_ref[...]
     hd = keys.shape[1]
     d_kn = jnp.zeros(keys.shape, jnp.float32)
     d_v = jnp.zeros(keys.shape, jnp.float32)
     for h in range(qn_ref.shape[2] // hd):
-        qn = qn_ref[0, :, h * hd : (h + 1) * hd]
-        da = da_ref[0, :, h * hd : (h + 1) * hd]
+        qn = qn_ref[slot, :, h * hd : (h + 1) * hd]
+        da = da_ref[slot, :, h * hd : (h + 1) * hd]
         sc = dot32(qn, keys, ROWS_ROWS)
         e = jnp.exp(sc - jnp.max(sc, axis=1, keepdims=True))
         p = e / jnp.sum(e, axis=1, keepdims=True)
@@ -200,20 +235,22 @@
     r = lax.rsqrt(jnp.mean(raw * raw, axis=1, keepdims=True) + EPS)
     u = d_kn * gain
     d_k = r * u - raw * (r * r * r * jnp.mean(raw * u, axis=1, keepdims=True))
-    o_ref[0, :, :hd] = d_k.astype(jnp.bfloat16)
-    o_ref[0, :, hd:] = d_v.astype(jnp.bfloat16)
-
-
-def back(qn, keys, vals, raw, da, gain):
-    slots, toks, hd = keys.shape
-    one = lambda a: pl.BlockSpec((1,) + a.shape[1:], lambda o: (o, 0, 0))
+    d_kv = jnp.concatenate([d_k, d_v], axis=1).astype(jnp.bfloat16)
+    feats = o_ref.shape[2]
+    for i in range(o_ref.shape[0]):
+        part = dot16(d_kv, w_ref[i * feats : (i + 1) * feats], ROWS_ROWS)
+        o_ref[i] = part.astype(jnp.bfloat16)
+
+
+def back(slot, n, qn, keys, vals, raw, da, gain, w):
+    args = (qn, keys, vals, raw, da, gain, w)
     return pl.pallas_call(
-        back_kernel,
-        grid=(slots,),
-        in_specs=[one(qn), one(keys), one(vals), one(raw), one(da), pl.BlockSpec(gain.shape, lambda o: (0, 0))],
-        out_specs=pl.BlockSpec((1, toks, 2 * hd), lambda o: (o, 0, 0)),
-        out_shape=jax.ShapeDtypeStruct((slots, toks, 2 * hd), jnp.bfloat16),
-    )(qn, keys, vals, raw, da, gain)
+        functools.partial(back_kernel, slot),
+        in_specs=[pl.BlockSpec(memory_space=pltpu.VMEM)] * len(args),
+        out_specs=pl.BlockSpec(memory_space=pltpu.VMEM),
+        out_shape=jax.ShapeDtypeStruct((n, keys.shape[1], w.shape[0] // n), jnp.bfloat16),
+        compiler_params=pltpu.CompilerParams(vmem_limit_bytes=VMEM_BYTES),
+    )(*args)
 
 
 def pick(a, i, axis=0):
@@ -281,7 +318,7 @@
 
     shared = share(jnp.take(image, micro, axis=0).reshape(-1, feats), "section")
     img = lax.all_gather(shared.reshape(slots * toks, feats), "tensor", axis=1, tiled=True)
-    wkv = after(jnp.concatenate([wk[0], wv[0]], axis=1), img)
+    wkv = jnp.concatenate([wk[0], wv[0]], axis=1)
     wkv = lax.all_gather(wkv, "dp", axis=0, tiled=True)
     kv = jnp.dot(img, wkv, preferred_element_type=jnp.float32)
     kv = jnp.moveaxis(kv.reshape(S, slots, toks // S, 2 * hd), 0, 1).reshape(slots, toks, 2 * hd)
@@ -290,30 +327,39 @@
 
     wq_own = swap(after(wq[0].reshape(T, chunk, wq.shape[2]), shared), "tensor")
     wq_f = dp_all(wq_own)
-    text_f = spread(after(jnp.take(text, micro, axis=0), wq_own))
+    text_f = spread(after(jnp.take(text, micro, axis=0), shared))
     gain_f = pick(in_gain.reshape(D, T, chunk), t, 1)
     gain_f = jnp.concatenate([pick(gain_f, d ^ j) for j in range(D)])[None]
     wo_own = jnp.moveaxis(wo[0].reshape(wo.shape[1], T, chunk), 1, 0)
-    wo_own = swap(after(wo_own, wq_own, wkv), "tensor")
+    wo_own = after(wo_own, wq_own, wkv, img, text_f)
+    half = wo_own.shape[1] // 2
+    wo_a = swap(wo_own[:, :half], "tensor")
+    wo_b = swap(after(wo_own[:, half:], wo_a), "tensor")
     ints = jnp.concatenate([s.astype(jnp.int32)[None], lens])
 
-    h = None
-    all_qn, all_h = [], []
+    h = kept_qn = kept_h = None
+    grads = []
+
+    def image_part(slot):
+        part = back(slot, T, kept_qn, keys, vals, k_raw, d_attn, k_gain, wkv)
+        return jnp.sum(swap(part, "tensor").astype(jnp.float32), axis=0).astype(jnp.bfloat16)
+
     for step in range(S + slots - 1):
         parts, hq = query(step, ints, text_f, gain_f, h, wq_f)
-        p, qn = attend(step, ints, alpha, width, query_norm_gain, keys, swap(parts, "tensor"))
-        all_qn.append(qn)
+        swapped = swap(parts, "tensor")
+        p, kept_qn = attend(step, ints, alpha, width, query_norm_gain, keys, swapped, kept_qn)
         if step == 0:
             vals16 = vals.astype(jnp.bfloat16).reshape(slots * toks, hd)
             vals16 = jnp.broadcast_to(vals16[None], (T,) + vals16.shape)
             both = swap(jnp.concatenate([p, vals16], axis=1), "tensor")
             probs = both[:, :rows]
-            wo_own = after(wo_own, hq)
-            across = dp_flip(wo_own, 2)
-            wo_f = [wo_own, dp_flip(wo_own, 1), across, dp_flip(after(across, probs), 1)]
+            wo_f = []
+            for own in (wo_a, wo_b):
+                across = dp_flip(own, 2)
+                wo_f += [own, dp_flip(own, 1), across, dp_flip(after(across, probs), 1)]
             vo = value_out(both[:, rows:], wo_f, slots)
         else:
-            probs = swap(p, "tensor")
+            probs = swap(after(p, *grads), "tensor")
         if step == 1:
             wo_full = lax.all_gather(after(wo[0], p), "dp", axis=1, tiled=True)
         if step == 5:
@@ -321,18 +367,14 @@
             d_attn = dot16(cot[0].reshape(slots * rows, width), wo_full, ROWS_ROWS)
             d_attn = alpha[0] * mask * d_attn.reshape(slots, rows, -1)
             probs, d_attn = lax.optimization_barrier((probs, d_attn))
-        h = output(step, ints, probs, vo, hq)
-        all_h.append(h)
+        if step >= S - 1:
+            grads.append(image_part(step - S + 1))
+        h, kept_h = output(step, ints, probs, vo, hq, kept_h)
         h = onward(h)
 
-    states = unspread(lax.dynamic_slice_in_dim(jnp.stack(all_h), s, slots, 0))
-
-    qn = lax.dynamic_slice_in_dim(jnp.stack(all_qn), s, slots, 0)
-    d_kv = back(qn, keys, vals, k_raw, d_attn, k_gain).reshape(slots * toks, 2 * hd)
-    grad = dot16(d_kv, wkv, ROWS_ROWS).astype(jnp.bfloat16)
-    grad = swap(jnp.moveaxis(grad.reshape(slots * toks, T, feats), 1, 0), "tensor")
-    grad = jnp.sum(grad.astype(jnp.float32), axis=0).astype(jnp.bfloat16)
-    grad = swap(jnp.moveaxis(grad.reshape(slots, S, toks // S, feats), 1, 0), "section")
+    states = unspread(kept_h)
+    grad = jnp.stack(grads).reshape(slots, S, toks // S, feats)
+    grad = swap(jnp.moveaxis(grad, 1, 0), "section")
     grad = jnp.sum(grad.astype(jnp.float32), axis=0)
     grad = jnp.stack([pick(grad, jnp.argmax(micro == m)) for m in range(slots)])
     return (states[None], grad)

time: 696 us -> 740 us (1.063)
  waiting for transfers between devices: 193 us -> 268 us
  blocking collectives: 241 us -> 180 us
  starting transfers between devices: 96.8 us -> 112 us
  Pallas kernels: 69.5 us -> 81.6 us
    all_to_all x14 -> x12, blocking collectives: 241 us -> 180 us  [swap(): return lax.all_to_all(x, axis, 0, 0, tiled=True)]
    all_gather x1, waiting for transfers between devices: 0.01 us -> 51.2 us  [per_device(): wkv = lax.all_gather(wkv, 'dp', axis=0, tiled=True)]
    all_gather x1, waiting for transfers between devices: 37.2 us -> 0.02 us  [per_device(): lax.all_gather(shared.reshape(slots * toks, feats), 'tensor', axis=1, til...]
    all_to_all x9 -> x13, waiting for transfers between devices: 54.3 us -> 90.1 us  [swap(): return lax.all_to_all(x, axis, 0, 0, tiled=True)]
    ppermute x4, waiting for transfers between devices: 6.96 us -> 42.7 us  [spread(): got.append(lax.ppermute(pick(parts, (a + k) % D), 'tensor', pairs))]
    pallas_call x8 -> x0, local copies, waits for them, and re-layouts: 17.2 us -> none  [the longest x7 13.8 us: attend(): pl.pallas_call(functools.partial(attend_kernel, step, width), in_specs=[p...]
    all_to_all x9 -> x13, starting transfers between devices: 60.1 us -> 75.2 us  [swap(): return lax.all_to_all(x, axis, 0, 0, tiled=True)]
    ppermute x6 -> x9, waiting for transfers between devices: 35.6 us -> 24.1 us  [dp_flip(): return lax.ppermute(x, 'dp', [(i, i ^ m) for i in range(D)])]
  transfers between devices with their start and end apart: 34 -> 41, of which waited for: 22 -> 27; matrix products, arithmetic and copies ran while one was open for 7% -> 5% of each run, Pallas kernels for 6% -> 7%
where the time goes in v1:
time: 740 us; the launch traced here: 728 us
  waiting for transfers between devices  268 us (36%)
  blocking collectives  180 us (24%)
  starting transfers between devices  112 us (15%)
  Pallas kernels  81.6 us (11%)
  local copies, waits for them, and re-layouts  42.9 us (6%)
  between operations  19.8 us (3%)
  other arithmetic  14.7 us (2%)
  matrix products  10.3 us (1%)
    all_to_all x12, blocking collectives, swap(): return lax.all_to_all(x, axis, 0, 0, tiled=True)  180 us
    all_to_all x13, waiting for transfers between devices, swap(): return lax.all_to_all(x, axis, 0, 0, tiled=True)  90.1 us
    all_to_all x13, starting transfers between devices, swap(): return lax.all_to_all(x, axis, 0, 0, tiled=True)  75.2 us
    ppermute x8, waiting for transfers between devices, onward(): return lax.ppermute(x, 'section', [(i, (i + 1) % S) for i in range(S)])  58.7 us
    all_gather x1, waiting for transfers between devices, per_device(): wkv = lax.all_gather(wkv, 'dp', axis=0, tiled=True)  51.2 us
    pallas_call x9, Pallas kernels, query(): pl.pallas_call(functools.partial(query_kernel, step), in_specs=[pl.BlockS...  45.4 us
    ppermute x4, waiting for transfers between devices, spread(): got.append(lax.ppermute(pick(parts, (a + k) % D), 'tensor', pairs))  42.7 us
    unnamed x76, local copies, waits for them, and re-layouts  26.8 us
  transfers between devices with their start and end apart: 41, of which 27 were waited for; matrix products, arithmetic and copies ran while one was open for 5% of the time, Pallas kernels for 7%

profile of v1, /device:TPU:32, one launch (start us, length us, event | category | flops | bytes accessed | tf_op | source)
XLA Modules:
  0.0 728.3 jit_solution(15070613200181387983)
XLA Ops:
  11.6 11.9 %all_to_all.125 = bf16[8,8,1024]{2,1,0:T(8,128)(2,1)} all-to-all(bf16[8,8,1024]{2,1,0:T(8,128)(2,1)S(1)} %broadcast_in_dim.56), channel_id=1, replica_groups=mesh['dp'=4,'section'=8,'tensor'=8] {'section'}, dimensions={0} | all-to-all | bytes 262144 | tf_op jit(solution)/shard_map/all_to_all | solution.py:265
  25.8 8.7 %all-to-all-start.1 = ((bf16[8,256,512]{2,1,0:T(8,128)(2,1)}), bf16[8,256,512]{2,1,0:T(8,128)(2,1)}, u32[]{:S(2)}, u32[]{:S(2)}) async-start(bf16[8,256,512]{2,1,0:T(8,128)(2,1)} %bitcast.112), calls=%async_computation.1 | async-start | bytes 4194304 | tf_op jit(solution)/shard_map/all_to_all | solution.py:265
  35.4 6.4 collective-permute-start
  47.8 3.9 copy.20
  51.7 3.9 copy.21
  55.7 34.4 %collective-permute-done = bf16[2,64,256]{2,1,0:T(8,128)(2,1)S(1)} collective-permute-done((bf16[2,64,256]{2,1,0:T(8,128)(2,1)S(1)}, bf16[2,64,256]{2,1,0:T(8,128)(2,1)S(1)}, u32[]{:S(2)}, u32[]{:S(2)}) %collective-permute-start) | collective-permute-done | bytes 65568 | tf_op jit(solution)/shard_map/ppermute | solution.py:301
  90.1 3.3 collective-permute-done.1
  93.4 4.8 collective-permute-done.2
  101.3 51.2 %all-gather.6.cloned.1.call-done.w_ref = bf16[8192,256]{1,0:T(8,128)(2,1)} async-done(((bf16[2048,256]{1,0:T(8,128)(2,1)}), bf16[8192,256]{1,0:T(8,128)(2,1)}) %all-gather.6.cloned.1.call-update) | async-done | bytes 4194320 | tf_op jit(solution)/shard_map/all_gather | solution.py:322
  155.5 7.6 %all-to-all-start.4 = ((bf16[8,256,256]{2,1,0:T(8,128)(2,1)}), bf16[8,256,256]{2,1,0:T(8,128)(2,1)S(1)}, u32[]{:S(2)}, u32[]{:S(2)}) async-start(bf16[8,256,256]{2,1,0:T(8,128)(2,1)} %get-tuple-element.135), calls=%async_computation.4 | async-start | bytes 2097152 | tf_op jit(solution)/shard_map/all_to_all | solution.py:265
  166.2 24.6 %all-to-all-done.4.refs_0_ = bf16[8,256,256]{2,1,0:T(8,128)(2,1)S(1)} async-done(((bf16[8,256,256]{2,1,0:T(8,128)(2,1)}), bf16[8,256,256]{2,1,0:T(8,128)(2,1)S(1)}, u32[]{:S(2)}, u32[]{:S(2)}) %all-to-all-start.4) | async-done | bytes 1048608 | tf_op jit(solution)/shard_map/all_to_all | solution.py:265
  190.8 5.6 all-to-all-start.5
  198.5 4.9 shard_map.140
  204.9 19.4 %all-to-all-done.5.refs_4_ = bf16[8,256,256]{2,1,0:T(8,128)(2,1)} async-done(((bf16[8,256,256]{2,1,0:T(8,128)(2,1)}), bf16[8,256,256]{2,1,0:T(8,128)(2,1)}, u32[]{:S(2)}, u32[]{:S(2)}) %all-to-all-start.5) | async-done | bytes 1048608 | tf_op jit(solution)/shard_map/all_to_all | solution.py:265
  224.3 5.6 all-to-all-start.2
  229.9 4.0 fusion.4
  242.9 4.3 all-to-all-done.2.q_ref
  250.4 5.4 all-to-all-start.3
  255.8 11.0 %all-to-all-done.3 = bf16[8,128,128]{2,1,0:T(8,128)(2,1)} async-done(((bf16[8,128,128]{2,1,0:T(8,128)(2,1)}), bf16[8,128,128]{2,1,0:T(8,128)(2,1)}, u32[]{:S(2)}, u32[]{:S(2)}) %all-to-all-start.3) | async-done | bytes 262176 | tf_op jit(solution)/shard_map/all_to_all | solution.py:265
  268.4 18.2 %collective-permute-done.11.refs_6_ = bf16[8,256,256]{2,1,0:T(8,128)(2,1)} collective-permute-done((bf16[8,256,256]{2,1,0:T(8,128)(2,1)}, bf16[8,256,256]{2,1,0:T(8,128)(2,1)}, u32[]{:S(2)}, u32[]{:S(2)}) %collective-permute-start.11) | collective-permute-done | bytes 1048608 | tf_op jit(solution)/shard_map/ppermute | solution.py:289
  289.5 4.6 shard_map.142.vo_ref
  297.7 6.2 collective-permute-done.13.refs_0_
  303.9 4.9 shard_map.144
  308.8 23.3 %all_to_all.126.q_ref = bf16[8,272,128]{2,1,0:T(8,128)(2,1)S(1)} all-to-all(bf16[8,272,128]{2,1,0:T(8,128)(2,1)S(1)} %get-tuple-element.77), channel_id=1, replica_groups=mesh['dp'=4,'section'=8,'tensor'=8] {'tensor'}, dimensions={0} | all-to-all | bytes 1114112 | tf_op jit(solution)/shard_map/all_to_all | solution.py:265
  333.3 11.5 %all_to_all.127.p_ref = bf16[8,64,128]{2,1,0:T(8,128)(2,1)S(1)} all-to-all(bf16[8,64,128]{2,1,0:T(8,128)(2,1)S(1)} %get-tuple-element.79), channel_id=1, replica_groups=mesh['dp'=4,'section'=8,'tensor'=8] {'tensor'}, dimensions={0} | all-to-all | bytes 262144 | tf_op jit(solution)/shard_map/all_to_all | solution.py:265
  348.2 10.1 %collective-permute-done.14.refs_0_ = bf16[64,1024]{1,0:T(8,128)(2,1)S(1)} collective-permute-done((bf16[64,1024]{1,0:T(8,128)(2,1)S(1)}, bf16[64,1024]{1,0:T(8,128)(2,1)S(1)}, u32[]{:S(2)}, u32[]{:S(2)}) %collective-permute-start.14) | collective-permute-done | bytes 131104 | tf_op jit(solution)/shard_map/ppermute | solution.py:286
  358.3 5.2 shard_map.147
  363.5 17.7 %all_to_all.128.q_ref = bf16[8,272,128]{2,1,0:T(8,128)(2,1)S(1)} all-to-all(bf16[8,272,128]{2,1,0:T(8,128)(2,1)S(1)} %get-tuple-element.83), channel_id=1, replica_groups=mesh['dp'=4,'section'=8,'tensor'=8] {'tensor'}, dimensions={0} | all-to-all | bytes 1114112 | tf_op jit(solution)/shard_map/all_to_all | solution.py:265
  382.4 11.5 %all_to_all.129.p_ref = bf16[8,64,128]{2,1,0:T(8,128)(2,1)S(1)} all-to-all(bf16[8,64,128]{2,1,0:T(8,128)(2,1)S(1)} %get-tuple-element.85), channel_id=1, replica_groups=mesh['dp'=4,'section'=8,'tensor'=8] {'tensor'}, dimensions={0} | all-to-all | bytes 262144 | tf_op jit(solution)/shard_map/all_to_all | solution.py:265
  395.0 7.1 collective-permute-done.15.refs_0_
  402.1 4.9 shard_map.150
  407.0 16.6 %all_to_all.130.q_ref = bf16[8,272,128]{2,1,0:T(8,128)(2,1)S(1)} all-to-all(bf16[8,272,128]{2,1,0:T(8,128)(2,1)S(1)} %get-tuple-element.89), channel_id=1, replica_groups=mesh['dp'=4,'section'=8,'tensor'=8] {'tensor'}, dimensions={0} | all-to-all | bytes 1114112 | tf_op jit(solution)/shard_map/all_to_all | solution.py:265
  424.8 11.5 %all_to_all.131.p_ref = bf16[8,64,128]{2,1,0:T(8,128)(2,1)S(1)} all-to-all(bf16[8,64,128]{2,1,0:T(8,128)(2,1)S(1)} %get-tuple-element.91), channel_id=1, replica_groups=mesh['dp'=4,'section'=8,'tensor'=8] {'tensor'}, dimensions={0} | all-to-all | bytes 262144 | tf_op jit(solution)/shard_map/all_to_all | solution.py:265
  437.4 7.1 collective-permute-done.16.refs_0_
  444.4 4.9 shard_map.153
  449.4 16.0 %all_to_all.132.q_ref = bf16[8,272,128]{2,1,0:T(8,128)(2,1)S(1)} all-to-all(bf16[8,272,128]{2,1,0:T(8,128)(2,1)S(1)} %get-tuple-element.95), channel_id=1, replica_groups=mesh['dp'=4,'section'=8,'tensor'=8] {'tensor'}, dimensions={0} | all-to-all | bytes 1114112 | tf_op jit(solution)/shard_map/all_to_all | solution.py:265
  466.6 11.6 %all_to_all.133.p_ref = bf16[8,64,128]{2,1,0:T(8,128)(2,1)S(1)} all-to-all(bf16[8,64,128]{2,1,0:T(8,128)(2,1)S(1)} %get-tuple-element.97), channel_id=1, replica_groups=mesh['dp'=4,'section'=8,'tensor'=8] {'tensor'}, dimensions={0} | all-to-all | bytes 262144 | tf_op jit(solution)/shard_map/all_to_all | solution.py:265
  479.6 7.1 collective-permute-done.17.refs_0_
  486.6 5.7 shard_map.156
  493.0 4.9 all-to-all-start.14
  499.1 11.1 %all-to-all-done.14.q_ref = bf16[8,272,128]{2,1,0:T(8,128)(2,1)S(1)} async-done(((bf16[8,272,128]{2,1,0:T(8,128)(2,1)}), bf16[8,272,128]{2,1,0:T(8,128)(2,1)S(1)}, u32[]{:S(2)}, u32[]{:S(2)}) %all-to-all-start.14) | async-done | bytes 557088 | tf_op jit(solution)/shard_map/all_to_all | solution.py:265
  513.7 4.6 all-to-all-start.15
  518.4 6.3 fusion.5
  529.4 7.1 collective-permute-done.18.refs_0_
  536.4 5.2 shard_map.159
  541.6 19.5 %all_to_all.134.q_ref = bf16[8,272,128]{2,1,0:T(8,128)(2,1)S(1)} all-to-all(bf16[8,272,128]{2,1,0:T(8,128)(2,1)S(1)} %get-tuple-element.109), channel_id=1, replica_groups=mesh['dp'=4,'section'=8,'tensor'=8] {'tensor'}, dimensions={0} | all-to-all | bytes 1114112 | tf_op jit(solution)/shard_map/all_to_all | solution.py:265
  562.3 11.5 %all_to_all.135.p_ref = bf16[8,64,128]{2,1,0:T(8,128)(2,1)S(1)} all-to-all(bf16[8,64,128]{2,1,0:T(8,128)(2,1)S(1)} %get-tuple-element.111), channel_id=1, replica_groups=mesh['dp'=4,'section'=8,'tensor'=8] {'tensor'}, dimensions={0} | all-to-all | bytes 262144 | tf_op jit(solution)/shard_map/all_to_all | solution.py:265
  574.9 7.1 collective-permute-done.19.refs_0_
  582.0 4.9 shard_map.162
  586.9 17.4 %all_to_all.136.q_ref = bf16[8,272,128]{2,1,0:T(8,128)(2,1)S(1)} all-to-all(bf16[8,272,128]{2,1,0:T(8,128)(2,1)S(1)} %get-tuple-element.115), channel_id=1, replica_groups=mesh['dp'=4,'section'=8,'tensor'=8] {'tensor'}, dimensions={0} | all-to-all | bytes 1114112 | tf_op jit(solution)/shard_map/all_to_all | solution.py:265
  606.2 4.7 all-to-all-start.19
  613.1 4.0 shard_map.167
  618.6 5.7 all-to-all-start.21
  628.6 7.1 collective-permute-done.20.refs_0_
  635.6 4.9 shard_map.165
  642.0 7.2 all-to-all-start.20
  650.9 11.0 %all-to-all-done.20.q_ref = bf16[8,272,128]{2,1,0:T(8,128)(2,1)S(1)} async-done(((bf16[8,272,128]{2,1,0:T(8,128)(2,1)}), bf16[8,272,128]{2,1,0:T(8,128)(2,1)S(1)}, u32[]{:S(2)}, u32[]{:S(2)}) %all-to-all-start.20) | async-done | bytes 557088 | tf_op jit(solution)/shard_map/all_to_all | solution.py:265
  664.5 4.7 all-to-all-start.22
  673.8 4.0 shard_map.169
  677.9 7.0 all-to-all-start.23
  689.0 3.4 collective-permute-start.21
  694.3 7.2 collective-permute-start.23
  710.7 3.4 all-to-all-start.24
  714.8 5.8 all-to-all-done.24
  (195 shorter events, 102.7 us)
Async XLA Ops:
  7.2 511.2 %copy-start = (bf16[1,2,64,8192]{3,2,1,0:T(8,128)(2,1)S(1)}, bf16[1,2,64,8192]{3,2,1,0:T(8,128)(2,1)}, u32[]{:S(2)}) copy-start(bf16[1,2,64,8192]{3,2,1,0:T(8,128)(2,1)} %param.25) | copy-start | bytes 6291460
  7.2 94.1 %all-gather.4.cloned.1.call-start = ((), (), s32[]{:S(2)}) async-start(), calls=%async_computation.25 | async-start | bytes 1179648 | tf_op jit(solution)/shard_map/all_gather | solution.py:320
  10.0 188.4 %copy-start.35 = (s32[2]{0:T(128)}, s32[2]{0:T(128)S(1)}, u32[]{:S(2)}) copy-start(s32[2]{0:T(128)S(1)} %get-tuple-element.132) | copy-start | bytes 28
  23.5 129.0 %all-gather.6.cloned.1.call-start = ((), (), s32[]{:S(2)}) async-start(), calls=%async_computation.26 | async-start | bytes 5242880 | tf_op jit(solution)/shard_map/all_gather | solution.py:322
  25.8 8.7 %copy-start.32 = (bf16[2,64,1024]{2,1,0:T(8,128)(2,1)S(1)}, bf16[2,64,1024]{2,1,0:T(8,128)(2,1)}, u32[]{:S(2)}) copy-start(bf16[2,64,1024]{2,1,0:T(8,128)(2,1)} %param.13) | copy-start | bytes 786436
  25.8 72.5 %all-to-all-start.1 = ((bf16[8,256,512]{2,1,0:T(8,128)(2,1)}), bf16[8,256,512]{2,1,0:T(8,128)(2,1)}, u32[]{:S(2)}, u32[]{:S(2)}) async-start(bf16[8,256,512]{2,1,0:T(8,128)(2,1)} %bitcast.112), calls=%async_computation.1 | async-start | bytes 4194304 | tf_op jit(solution)/shard_map/all_to_all | solution.py:265
  35.4 54.7 %collective-permute-start = (bf16[2,64,256]{2,1,0:T(8,128)(2,1)S(1)}, bf16[2,64,256]{2,1,0:T(8,128)(2,1)S(1)}, u32[]{:S(2)}, u32[]{:S(2)}) collective-permute-start(bf16[2,64,256]{2,1,0:T(8,128)(2,1)S(1)} %get-tuple-element.154), channel_id=1, source_target_pairs={{0,0},{1,4},{2,1},{3,5},{4,2},{5,6},{6,3},{7,7},{8,8},{9,12},{10,9... | collective-permute-start | bytes 196616 | tf_op jit(solution)/shard_map/ppermute | solution.py:301
  41.8 51.7 %collective-permute-start.1 = (bf16[2,64,256]{2,1,0:T(8,128)(2,1)S(1)}, bf16[2,64,256]{2,1,0:T(8,128)(2,1)S(1)}, u32[]{:S(2)}, u32[]{:S(2)}) collective-permute-start(bf16[2,64,256]{2,1,0:T(8,128)(2,1)S(1)} %get-tuple-element.157), channel_id=1, source_target_pairs={{0,1},{1,5},{2,2},{3,6},{4,3},{5,7},{6,0},{7,4},{8,9},{9,13},{10,1... | collective-permute-start | bytes 196616 | tf_op jit(solution)/shard_map/ppermute | solution.py:301
  44.2 54.0 %collective-permute-start.2 = (bf16[2,64,256]{2,1,0:T(8,128)(2,1)S(1)}, bf16[2,64,256]{2,1,0:T(8,128)(2,1)S(1)}, u32[]{:S(2)}, u32[]{:S(2)}) collective-permute-start(bf16[2,64,256]{2,1,0:T(8,128)(2,1)S(1)} %get-tuple-element.156), channel_id=1, source_target_pairs={{0,2},{1,6},{2,3},{3,7},{4,0},{5,4},{6,1},{7,5},{8,10},{9,14},{10,... | collective-permute-start | bytes 196616 | tf_op jit(solution)/shard_map/ppermute | solution.py:301
  45.2 53.1 %collective-permute-start.3 = (bf16[2,64,256]{2,1,0:T(8,128)(2,1)S(1)}, bf16[2,64,256]{2,1,0:T(8,128)(2,1)S(1)}, u32[]{:S(2)}, u32[]{:S(2)}) collective-permute-start(bf16[2,64,256]{2,1,0:T(8,128)(2,1)S(1)} %get-tuple-element.155), channel_id=1, source_target_pairs={{0,3},{1,7},{2,0},{3,4},{4,1},{5,5},{6,2},{7,6},{8,11},{9,15},{10,... | collective-permute-start | bytes 196616 | tf_op jit(solution)/shard_map/ppermute | solution.py:301
  98.4 67.8 %collective-permute-start.5 = (bf16[8,256,512]{2,1,0:T(8,128)(2,1)}, bf16[8,256,512]{2,1,0:T(8,128)(2,1)}, u32[]{:S(2)}, u32[]{:S(2)}) collective-permute-start(bf16[8,256,512]{2,1,0:T(8,128)(2,1)} %all-to-all-done.1.refs_0_.refs_1_), channel_id=1, source_target_pairs={{0,128},{64,192},{128,0},{192,64},{1,129},{65,193},{129,1},{193,65... | collective-permute-start | bytes 6291464 | tf_op jit(solution)/shard_map/ppermute | solution.py:289
  155.5 41.4 %copy-start.33 = (f32[1,8192]{1,0:T(1,128)S(1)}, f32[1,8192]{1,0:T(1,128)}, u32[]{:S(2)}) copy-start(f32[1,8192]{1,0:T(1,128)} %param.17) | copy-start | bytes 98308
  155.5 35.3 %all-to-all-start.4 = ((bf16[8,256,256]{2,1,0:T(8,128)(2,1)}), bf16[8,256,256]{2,1,0:T(8,128)(2,1)S(1)}, u32[]{:S(2)}, u32[]{:S(2)}) async-start(bf16[8,256,256]{2,1,0:T(8,128)(2,1)} %get-tuple-element.135), calls=%async_computation.4 | async-start | bytes 2097152 | tf_op jit(solution)/shard_map/all_to_all | solution.py:265
  163.1 35.4 %collective-permute-start.4 = (bf16[8,256,512]{2,1,0:T(8,128)(2,1)}, bf16[8,256,512]{2,1,0:T(8,128)(2,1)}, u32[]{:S(2)}, u32[]{:S(2)}) collective-permute-start(bf16[8,256,512]{2,1,0:T(8,128)(2,1)} %all-to-all-done.1.refs_0_.refs_1_), channel_id=1, source_target_pairs={{0,64},{64,0},{128,192},{192,128},{1,65},{65,1},{129,193},{193,129... | collective-permute-start | bytes 6291464 | tf_op jit(solution)/shard_map/ppermute | solution.py:289
  166.2 32.3 %collective-permute-start.6 = (bf16[8,256,512]{2,1,0:T(8,128)(2,1)}, bf16[8,256,512]{2,1,0:T(8,128)(2,1)}, u32[]{:S(2)}, u32[]{:S(2)}) collective-permute-start(bf16[8,256,512]{2,1,0:T(8,128)(2,1)} %collective-permute-done.5.refs_2_.refs_3_), channel_id=1, source_target_pairs={{0,64},{64,0},{128,192},{192,128},{1,65},{65,1},{129,193},{193,129... | collective-permute-start | bytes 6291464 | tf_op jit(solution)/shard_map/ppermute | solution.py:289
  190.8 33.5 %all-to-all-start.5 = ((bf16[8,256,256]{2,1,0:T(8,128)(2,1)}), bf16[8,256,256]{2,1,0:T(8,128)(2,1)}, u32[]{:S(2)}, u32[]{:S(2)}) async-start(bf16[8,256,256]{2,1,0:T(8,128)(2,1)} %get-tuple-element.73), calls=%async_computation.5 | async-start | bytes 2097152 | tf_op jit(solution)/shard_map/all_to_all | solution.py:265
  224.3 22.9 %all-to-all-start.2 = ((bf16[8,272,128]{2,1,0:T(8,128)(2,1)}), bf16[8,272,128]{2,1,0:T(8,128)(2,1)}, u32[]{:S(2)}, u32[]{:S(2)}) async-start(bf16[8,272,128]{2,1,0:T(8,128)(2,1)} %copy-done.10), calls=%async_computation.2 | async-start | bytes 1114112 | tf_op jit(solution)/shard_map/all_to_all | solution.py:265
  229.9 12.2 %copy-start.31 = (f32[1,128]{1,0:T(1,128)S(1)}, f32[1,128]{1,0:T(1,128)}, u32[]{:S(2)}) copy-start(f32[1,128]{1,0:T(1,128)} %gain_ref.21) | copy-start | bytes 1540
  229.9 17.3 %copy-start.30 = (f32[1,128]{1,0:T(1,128)S(1)}, f32[1,128]{1,0:T(1,128)}, u32[]{:S(2)}) copy-start(f32[1,128]{1,0:T(1,128)} %gain_ref.19) | copy-start | bytes 1540
  237.7 30.2 %collective-permute-start.8 = (bf16[8,256,256]{2,1,0:T(8,128)(2,1)S(1)}, bf16[8,256,256]{2,1,0:T(8,128)(2,1)}, u32[]{:S(2)}, u32[]{:S(2)}) collective-permute-start(bf16[8,256,256]{2,1,0:T(8,128)(2,1)S(1)} %all-to-all-done.4.refs_0_), channel_id=1, source_target_pairs={{0,128},{64,192},{128,0},{192,64},{1,129},{65,193},{129,1},{193,65... | collective-permute-start | bytes 3145736 | tf_op jit(solution)/shard_map/ppermute | solution.py:289
  238.3 48.3 %collective-permute-start.11 = (bf16[8,256,256]{2,1,0:T(8,128)(2,1)}, bf16[8,256,256]{2,1,0:T(8,128)(2,1)}, u32[]{:S(2)}, u32[]{:S(2)}) collective-permute-start(bf16[8,256,256]{2,1,0:T(8,128)(2,1)} %all-to-all-done.5.refs_4_), channel_id=1, source_target_pairs={{0,128},{64,192},{128,0},{192,64},{1,129},{65,193},{129,1},{193,65... | collective-permute-start | bytes 3145736 | tf_op jit(solution)/shard_map/ppermute | solution.py:289
  250.4 16.4 %all-to-all-start.3 = ((bf16[8,128,128]{2,1,0:T(8,128)(2,1)}), bf16[8,128,128]{2,1,0:T(8,128)(2,1)}, u32[]{:S(2)}, u32[]{:S(2)}) async-start(bf16[8,128,128]{2,1,0:T(8,128)(2,1)} %pad_maximum_fusion.4), calls=%async_computation.3 | async-start | bytes 524288 | tf_op jit(solution)/shard_map/all_to_all | solution.py:265
  255.8 262.5 %all-gather.8.cloned.1.call-start = ((), (), s32[]{:S(2)}) async-start(), calls=%async_computation.27 | async-start | bytes 10485760 | tf_op jit(solution)/shard_map/all_gather | solution.py:364
  255.8 30.8 %collective-permute-start.7 = (bf16[8,256,256]{2,1,0:T(8,128)(2,1)S(1)}, bf16[8,256,256]{2,1,0:T(8,128)(2,1)}, u32[]{:S(2)}, u32[]{:S(2)}) collective-permute-start(bf16[8,256,256]{2,1,0:T(8,128)(2,1)S(1)} %all-to-all-done.4.refs_0_), channel_id=1, source_target_pairs={{0,64},{64,0},{128,192},{192,128},{1,65},{65,1},{129,193},{193,129... | collective-permute-start | bytes 3145736 | tf_op jit(solution)/shard_map/ppermute | solution.py:289
  267.8 18.8 %collective-permute-start.9 = (bf16[8,256,256]{2,1,0:T(8,128)(2,1)}, bf16[8,256,256]{2,1,0:T(8,128)(2,1)S(1)}, u32[]{:S(2)}, u32[]{:S(2)}) collective-permute-start(bf16[8,256,256]{2,1,0:T(8,128)(2,1)} %collective-permute-done.8.refs_2_), channel_id=1, source_target_pairs={{0,64},{64,0},{128,192},{192,128},{1,65},{65,1},{129,193},{193,129... | collective-permute-start | bytes 3145736 | tf_op jit(solution)/shard_map/ppermute | solution.py:289
  267.9 18.7 %collective-permute-start.10 = (bf16[8,256,256]{2,1,0:T(8,128)(2,1)}, bf16[8,256,256]{2,1,0:T(8,128)(2,1)S(1)}, u32[]{:S(2)}, u32[]{:S(2)}) collective-permute-start(bf16[8,256,256]{2,1,0:T(8,128)(2,1)} %all-to-all-done.5.refs_4_), channel_id=1, source_target_pairs={{0,64},{64,0},{128,192},{192,128},{1,65},{65,1},{129,193},{193,129... | collective-permute-start | bytes 3145736 | tf_op jit(solution)/shard_map/ppermute | solution.py:289
  286.6 2.9 collective-permute-start.12
  289.5 4.6 copy-start.25
  296.0 36.0 %copy-start.17 = (f32[2,64,512]{2,1,0:T(8,128)S(1)}, f32[2,64,512]{2,1,0:T(8,128)}, u32[]{:S(2)}) copy-start(f32[2,64,512]{2,1,0:T(8,128)} %copy-done.16) | copy-start | bytes 786436
  296.0 7.8 %collective-permute-start.13 = (bf16[64,1024]{1,0:T(8,128)(2,1)S(1)}, bf16[64,1024]{1,0:T(8,128)(2,1)S(1)}, u32[]{:S(2)}, u32[]{:S(2)}) collective-permute-start(bf16[64,1024]{1,0:T(8,128)(2,1)S(1)} %get-tuple-element.76), channel_id=1, source_target_pairs={{0,8},{8,16},{16,24},{24,32},{32,40},{40,48},{48,56},{56,0},{1,9},... | collective-permute-start | bytes 393224 | tf_op jit(solution)/shard_map/ppermute | solution.py:286
  344.8 2.2 copy-start.2
  348.1 10.2 %collective-permute-start.14 = (bf16[64,1024]{1,0:T(8,128)(2,1)S(1)}, bf16[64,1024]{1,0:T(8,128)(2,1)S(1)}, u32[]{:S(2)}, u32[]{:S(2)}) collective-permute-start(bf16[64,1024]{1,0:T(8,128)(2,1)S(1)} %get-tuple-element.82), channel_id=1, source_target_pairs={{0,8},{8,16},{16,24},{24,32},{32,40},{40,48},{48,56},{56,0},{1,9},... | collective-permute-start | bytes 393224 | tf_op jit(solution)/shard_map/ppermute | solution.py:286
  358.3 35.6 %copy-start.3 = (bf16[2,1024,1024]{2,1,0:T(8,128)(2,1)S(1)}, bf16[2,1024,1024]{2,1,0:T(8,128)(2,1)}, u32[]{:S(2)}) copy-start(bf16[2,1024,1024]{2,1,0:T(8,128)(2,1)} %copy-done.1) | copy-start | bytes 12582916
  394.9 7.2 collective-permute-start.15
  437.3 7.2 collective-permute-start.16
  466.6 11.6 %copy-start.20 = (f32[2,64,512]{2,1,0:T(8,128)}, f32[2,64,512]{2,1,0:T(8,128)S(1)}, u32[]{:S(2)}) copy-start(f32[2,64,512]{2,1,0:T(8,128)S(1)} %get-tuple-element.102.refs_0_) | copy-start | bytes 786436
  479.2 7.4 %collective-permute-start.17 = (bf16[64,1024]{1,0:T(8,128)(2,1)S(1)}, bf16[64,1024]{1,0:T(8,128)(2,1)S(1)}, u32[]{:S(2)}, u32[]{:S(2)}) collective-permute-start(bf16[64,1024]{1,0:T(8,128)(2,1)S(1)} %get-tuple-element.100), channel_id=1, source_target_pairs={{0,8},{8,16},{16,24},{24,32},{32,40},{40,48},{48,56},{56,0},{1,9},... | collective-permute-start | bytes 393224 | tf_op jit(solution)/shard_map/ppermute | solution.py:286
  493.0 17.2 %all-to-all-start.14 = ((bf16[8,272,128]{2,1,0:T(8,128)(2,1)}), bf16[8,272,128]{2,1,0:T(8,128)(2,1)S(1)}, u32[]{:S(2)}, u32[]{:S(2)}) async-start(bf16[8,272,128]{2,1,0:T(8,128)(2,1)} %get-tuple-element.101), calls=%async_computation.14 | async-start | bytes 1114112 | tf_op jit(solution)/shard_map/all_to_all | solution.py:265
  513.7 12.3 %all-to-all-start.15 = ((bf16[8,64,128]{2,1,0:T(8,128)(2,1)}), bf16[8,64,128]{2,1,0:T(8,128)(2,1)S(1)}, u32[]{:S(2)}, u32[]{:S(2)}) async-start(bf16[8,64,128]{2,1,0:T(8,128)(2,1)} %get-tuple-element.103), calls=%async_computation.15 | async-start | bytes 262144 | tf_op jit(solution)/shard_map/all_to_all | solution.py:265
  518.4 6.4 copy-start.34
  518.4 7.6 %copy-start.27 = (bf16[64,1024]{1,0:T(8,128)(2,1)S(1)}, bf16[64,1024]{1,0:T(8,128)(2,1)}, u32[]{:S(2)}) copy-start(bf16[64,1024]{1,0:T(8,128)(2,1)} %copy-done.26) | copy-start | bytes 393220
  526.0 2.2 copy-start.4
  529.3 31.8 %copy-start.19 = (f32[2,64,512]{2,1,0:T(8,128)S(1)}, f32[2,64,512]{2,1,0:T(8,128)}, u32[]{:S(2)}) copy-start(f32[2,64,512]{2,1,0:T(8,128)} %copy-done.18) | copy-start | bytes 786436
  529.3 7.2 collective-permute-start.18
  536.4 37.4 %copy-start.5 = (bf16[2,1024,1024]{2,1,0:T(8,128)(2,1)S(1)}, bf16[2,1024,1024]{2,1,0:T(8,128)(2,1)}, u32[]{:S(2)}) copy-start(bf16[2,1024,1024]{2,1,0:T(8,128)(2,1)} %copy-done.1) | copy-start | bytes 12582916
  574.8 7.2 collective-permute-start.19
  586.9 19.3 %copy-start.28 = (bf16[64,1024]{1,0:T(8,128)(2,1)}, bf16[64,1024]{1,0:T(8,128)(2,1)S(1)}, u32[]{:S(2)}) copy-start(bf16[64,1024]{1,0:T(8,128)(2,1)S(1)} %get-tuple-element.118.h_ref) | copy-start | bytes 393220
  606.2 12.4 %all-to-all-start.19 = ((bf16[8,64,128]{2,1,0:T(8,128)(2,1)}), bf16[8,64,128]{2,1,0:T(8,128)(2,1)S(1)}, u32[]{:S(2)}, u32[]{:S(2)}) async-start(bf16[8,64,128]{2,1,0:T(8,128)(2,1)} %get-tuple-element.117), calls=%async_computation.19 | async-start | bytes 262144 | tf_op jit(solution)/shard_map/all_to_all | solution.py:265
  613.1 11.2 %copy-start.29 = (bf16[64,1024]{1,0:T(8,128)(2,1)S(1)}, bf16[64,1024]{1,0:T(8,128)(2,1)}, u32[]{:S(2)}) copy-start(bf16[64,1024]{1,0:T(8,128)(2,1)} %copy-done.28) | copy-start | bytes 393220
  618.6 23.4 %all-to-all-start.21 = ((bf16[8,32,1024]{2,1,0:T(8,128)(2,1)}), bf16[8,32,1024]{2,1,0:T(8,128)(2,1)}, u32[]{:S(2)}, u32[]{:S(2)}) async-start(bf16[8,32,1024]{2,1,0:T(8,128)(2,1)} %shard_map.167), calls=%async_computation.21 | async-start | bytes 1048576 | tf_op jit(solution)/shard_map/all_to_all | solution.py:265
  624.4 2.2 copy-start.6
  628.3 7.3 %collective-permute-start.20 = (bf16[64,1024]{1,0:T(8,128)(2,1)S(1)}, bf16[64,1024]{1,0:T(8,128)(2,1)S(1)}, u32[]{:S(2)}, u32[]{:S(2)}) collective-permute-start(bf16[64,1024]{1,0:T(8,128)(2,1)S(1)} %get-tuple-element.120), channel_id=1, source_target_pairs={{0,8},{8,16},{16,24},{24,32},{32,40},{40,48},{48,56},{56,0},{1,9},... | collective-permute-start | bytes 393224 | tf_op jit(solution)/shard_map/ppermute | solution.py:286
  642.0 20.0 %all-to-all-start.20 = ((bf16[8,272,128]{2,1,0:T(8,128)(2,1)}), bf16[8,272,128]{2,1,0:T(8,128)(2,1)S(1)}, u32[]{:S(2)}, u32[]{:S(2)}) async-start(bf16[8,272,128]{2,1,0:T(8,128)(2,1)} %copy-done.11), calls=%async_computation.20 | async-start | bytes 1114112 | tf_op jit(solution)/shard_map/all_to_all | solution.py:265
  664.5 13.4 %all-to-all-start.22 = ((bf16[8,64,128]{2,1,0:T(8,128)(2,1)}), bf16[8,64,128]{2,1,0:T(8,128)(2,1)S(1)}, u32[]{:S(2)}, u32[]{:S(2)}) async-start(bf16[8,64,128]{2,1,0:T(8,128)(2,1)} %get-tuple-element.125), calls=%async_computation.22 | async-start | bytes 262144 | tf_op jit(solution)/shard_map/all_to_all | solution.py:265
  673.8 11.2 %copy-start.13 = (bf16[2,64,1024]{2,1,0:T(8,128)(2,1)S(1)}, bf16[2,64,1024]{2,1,0:T(8,128)(2,1)}, u32[]{:S(2)}) copy-start(bf16[2,64,1024]{2,1,0:T(8,128)(2,1)} %copy-done.12) | copy-start | bytes 786436
  673.8 11.2 %copy-start.23 = (bf16[64,1024]{1,0:T(8,128)(2,1)S(1)}, bf16[64,1024]{1,0:T(8,128)(2,1)}, u32[]{:S(2)}) copy-start(bf16[64,1024]{1,0:T(8,128)(2,1)} %copy-done.22) | copy-start | bytes 393220
  677.9 31.9 %all-to-all-start.23 = ((bf16[8,32,1024]{2,1,0:T(8,128)(2,1)}), bf16[8,32,1024]{2,1,0:T(8,128)(2,1)S(1)}, u32[]{:S(2)}, u32[]{:S(2)}) async-start(bf16[8,32,1024]{2,1,0:T(8,128)(2,1)} %shard_map.169), calls=%async_computation.23 | async-start | bytes 1048576 | tf_op jit(solution)/shard_map/all_to_all | solution.py:265
  685.0 2.2 copy-start.7
  687.1 16.3 %copy-start.36 = (s32[1,2]{1,0:T(1,128)S(1)}, s32[1,2]{1,0:T(1,128)}, u32[]{:S(2)}) copy-start(s32[1,2]{1,0:T(1,128)} %param.14) | copy-start | bytes 28
  689.0 20.0 %collective-permute-start.21 = (bf16[2,64,256]{2,1,0:T(8,128)(2,1)S(1)}, bf16[2,64,256]{2,1,0:T(8,128)(2,1)S(1)}, u32[]{:S(2)}, u32[]{:S(2)}) collective-permute-start(bf16[2,64,256]{2,1,0:T(8,128)(2,1)S(1)} %get-tuple-element.140), channel_id=1, source_target_pairs={{0,0},{4,1},{1,2},{5,3},{2,4},{6,5},{3,6},{7,7},{8,8},{12,9},{9,10... | collective-permute-start | bytes 196616 | tf_op jit(solution)/shard_map/ppermute | solution.py:311
  692.3 16.7 %collective-permute-start.22 = (bf16[2,64,256]{2,1,0:T(8,128)(2,1)S(1)}, bf16[2,64,256]{2,1,0:T(8,128)(2,1)S(1)}, u32[]{:S(2)}, u32[]{:S(2)}) collective-permute-start(bf16[2,64,256]{2,1,0:T(8,128)(2,1)S(1)} %get-tuple-element.143), channel_id=1, source_target_pairs={{1,0},{5,1},{2,2},{6,3},{3,4},{7,5},{0,6},{4,7},{9,8},{13,9},{10,1... | collective-permute-start | bytes 196616 | tf_op jit(solution)/shard_map/ppermute | solution.py:311
  694.3 14.8 %collective-permute-start.23 = (bf16[2,64,256]{2,1,0:T(8,128)(2,1)S(1)}, bf16[2,64,256]{2,1,0:T(8,128)(2,1)S(1)}, u32[]{:S(2)}, u32[]{:S(2)}) collective-permute-start(bf16[2,64,256]{2,1,0:T(8,128)(2,1)S(1)} %get-tuple-element.142), channel_id=1, source_target_pairs={{2,0},{6,1},{3,2},{7,3},{0,4},{4,5},{1,6},{5,7},{10,8},{14,9},{11,... | collective-permute-start | bytes 196616 | tf_op jit(solution)/shard_map/ppermute | solution.py:311
  701.5 8.3 %collective-permute-start.24 = (bf16[2,64,256]{2,1,0:T(8,128)(2,1)S(1)}, bf16[2,64,256]{2,1,0:T(8,128)(2,1)S(1)}, u32[]{:S(2)}, u32[]{:S(2)}) collective-permute-start(bf16[2,64,256]{2,1,0:T(8,128)(2,1)S(1)} %get-tuple-element.141), channel_id=1, source_target_pairs={{3,0},{7,1},{0,2},{4,3},{1,4},{5,5},{2,6},{6,7},{11,8},{15,9},{8,1... | collective-permute-start | bytes 196616 | tf_op jit(solution)/shard_map/ppermute | solution.py:311
  710.7 9.9 %all-to-all-start.24 = ((bf16[8,2,4,1024]{3,2,1,0:T(4,128)(2,1)}), bf16[8,2,4,1024]{3,2,1,0:T(4,128)(2,1)S(1)}, u32[]{:S(2)}, u32[]{:S(2)}) async-start(bf16[8,2,4,1024]{3,2,1,0:T(4,128)(2,1)} %maximum_bitcast_fusion.1), calls=%async_computation.24 | async-start | bytes 262144 | tf_op jit(solution)/shard_map/all_to_all | solution.py:265
  (14 other events, 14.6 us)
Sparse Core Ops, SparseCore 0:
  23.6 54.4 all-gather.3
  79.9 72.5 all-gather.5
  333.4 58.0 all-gather.7

commit v2 on v1

--- a/solution.py
+++ b/solution.py
@@ -213,7 +213,7 @@
         in_specs=[pl.BlockSpec(memory_space=pltpu.VMEM)] * (1 + len(w)),
         out_specs=pl.BlockSpec(memory_space=pltpu.VMEM),
         out_shape=jax.ShapeDtypeStruct((slots, n * heads * toks, 4 * chunk), jnp.bfloat16),
-        compiler_params=pltpu.CompilerParams(vmem_limit_bytes=2 * VMEM_BYTES),
+        compiler_params=pltpu.CompilerParams(vmem_limit_bytes=VMEM_BYTES),
     )(v, *w)
 
 
@@ -316,25 +316,26 @@
     lens = jnp.take(lengths[0], micro)
     alpha = jnp.tanh(gate)
 
-    shared = share(jnp.take(image, micro, axis=0).reshape(-1, feats), "section")
-    img = lax.all_gather(shared.reshape(slots * toks, feats), "tensor", axis=1, tiled=True)
     wkv = jnp.concatenate([wk[0], wv[0]], axis=1)
+    shared = share(after(jnp.take(image, micro, axis=0), wkv).reshape(-1, feats), "section")
     wkv = lax.all_gather(wkv, "dp", axis=0, tiled=True)
+
+    wq_own = swap(after(wq[0].reshape(T, chunk, wq.shape[2]), shared), "tensor")
+    wq_f = dp_all(wq_own)
+    text_f = spread(after(jnp.take(text, micro, axis=0), shared))
+    img = after(shared, wq_own).reshape(slots * toks, feats)
+    img = lax.all_gather(img, "tensor", axis=1, tiled=True)
+    gain_f = pick(in_gain.reshape(D, T, chunk), t, 1)
+    gain_f = jnp.concatenate([pick(gain_f, d ^ j) for j in range(D)])[None]
+    wo_own = jnp.moveaxis(wo[0].reshape(wo.shape[1], T, chunk), 1, 0)
+    wo_own = after(wo_own, wq_own, wkv, text_f)
+    half = wo_own.shape[1] // 2
+    wo_a = swap(wo_own[:, :half], "tensor")
+    wo_b = swap(after(wo_own[:, half:], wo_a, img), "tensor")
     kv = jnp.dot(img, wkv, preferred_element_type=jnp.float32)
     kv = jnp.moveaxis(kv.reshape(S, slots, toks // S, 2 * hd), 0, 1).reshape(slots, toks, 2 * hd)
     k_raw, vals = kv[..., :hd], kv[..., hd:]
     keys = k_raw * lax.rsqrt(jnp.mean(k_raw * k_raw, axis=-1, keepdims=True) + EPS) * k_gain[0]
-
-    wq_own = swap(after(wq[0].reshape(T, chunk, wq.shape[2]), shared), "tensor")
-    wq_f = dp_all(wq_own)
-    text_f = spread(after(jnp.take(text, micro, axis=0), shared))
-    gain_f = pick(in_gain.reshape(D, T, chunk), t, 1)
-    gain_f = jnp.concatenate([pick(gain_f, d ^ j) for j in range(D)])[None]
-    wo_own = jnp.moveaxis(wo[0].reshape(wo.shape[1], T, chunk), 1, 0)
-    wo_own = after(wo_own, wq_own, wkv, img, text_f)
-    half = wo_own.shape[1] // 2
-    wo_a = swap(wo_own[:, :half], "tensor")
-    wo_b = swap(after(wo_own[:, half:], wo_a), "tensor")
     ints = jnp.concatenate([s.astype(jnp.int32)[None], lens])
 
     h = kept_qn = kept_h = None

time: 740 us -> 681 us (0.920)
  waiting for transfers between devices: 268 us -> 216 us
    all_gather x1, waiting for transfers between devices: 51.2 us -> 0.02 us  [per_device(): wkv = lax.all_gather(wkv, 'dp', axis=0, tiled=True)]
    ppermute x9, waiting for transfers between devices: 24.1 us -> 53.3 us  [dp_flip(): return lax.ppermute(x, 'dp', [(i, i ^ m) for i in range(D)])]
    all_to_all x13, waiting for transfers between devices: 90.1 us -> 68.3 us  [swap(): return lax.all_to_all(x, axis, 0, 0, tiled=True)]
    ppermute x4, waiting for transfers between devices: 42.7 us -> 32.9 us  [spread(): got.append(lax.ppermute(pick(parts, (a + k) % D), 'tensor', pairs))]
    unnamed x76 -> x84, local copies, waits for them, and re-layouts: 26.8 us -> 27 us
  transfers between devices with their start and end apart: 41 -> 41, of which waited for: 27 -> 27; matrix products, arithmetic and copies ran while one was open for 5% -> 6% of each run, Pallas kernels for 7% -> 8%
where the time goes in v2:
time: 681 us; the launch traced here: 670 us
  waiting for transfers between devices  216 us (32%)
  blocking collectives  179 us (26%)
  starting transfers between devices  109 us (16%)
  Pallas kernels  81.6 us (12%)
  local copies, waits for them, and re-layouts  40.8 us (6%)
  between operations  19.5 us (3%)
  other arithmetic  13.3 us (2%)
  matrix products  10.3 us (2%)
    all_to_all x12, blocking collectives, swap(): return lax.all_to_all(x, axis, 0, 0, tiled=True)  179 us
    all_to_all x13, starting transfers between devices, swap(): return lax.all_to_all(x, axis, 0, 0, tiled=True)  73.6 us
    all_to_all x13, waiting for transfers between devices, swap(): return lax.all_to_all(x, axis, 0, 0, tiled=True)  68.3 us
    ppermute x8, waiting for transfers between devices, onward(): return lax.ppermute(x, 'section', [(i, (i + 1) % S) for i in range(S)])  59.5 us
    ppermute x9, waiting for transfers between devices, dp_flip(): return lax.ppermute(x, 'dp', [(i, i ^ m) for i in range(D)])  53.3 us
    pallas_call x9, Pallas kernels, query(): pl.pallas_call(functools.partial(query_kernel, step), in_specs=[pl.BlockS...  45.4 us
    ppermute x4, waiting for transfers between devices, spread(): got.append(lax.ppermute(pick(parts, (a + k) % D), 'tensor', pairs))  32.9 us
    unnamed x84, local copies, waits for them, and re-layouts  27 us
  transfers between devices with their start and end apart: 41, of which 27 were waited for; matrix products, arithmetic and copies ran while one was open for 6% of the time, Pallas kernels for 8%

profile of v2, /device:TPU:32, one launch (start us, length us, event | category | flops | bytes accessed | tf_op | source)
XLA Modules:
  0.0 669.9 jit_solution(18155467958920669868)
XLA Ops:
  11.1 11.9 %all_to_all.125 = bf16[8,8,1024]{2,1,0:T(8,128)(2,1)} all-to-all(bf16[8,8,1024]{2,1,0:T(8,128)(2,1)S(1)} %broadcast_in_dim.53), channel_id=1, replica_groups=mesh['dp'=4,'section'=8,'tensor'=8] {'section'}, dimensions={0} | all-to-all | bytes 262144 | tf_op jit(solution)/shard_map/all_to_all | solution.py:265
  23.0 8.7 %all-to-all-start.1 = ((bf16[8,256,512]{2,1,0:T(8,128)(2,1)}), bf16[8,256,512]{2,1,0:T(8,128)(2,1)}, u32[]{:S(2)}, u32[]{:S(2)}) async-start(bf16[8,256,512]{2,1,0:T(8,128)(2,1)} %bitcast.112), calls=%async_computation.1 | async-start | bytes 4194304 | tf_op jit(solution)/shard_map/all_to_all | solution.py:265
  32.5 6.4 collective-permute-start
  44.9 3.9 copy.20
  48.9 3.9 copy.21
  52.8 24.9 %collective-permute-done = bf16[2,64,256]{2,1,0:T(8,128)(2,1)S(1)} collective-permute-done((bf16[2,64,256]{2,1,0:T(8,128)(2,1)S(1)}, bf16[2,64,256]{2,1,0:T(8,128)(2,1)S(1)}, u32[]{:S(2)}, u32[]{:S(2)}) %collective-permute-start) | collective-permute-done | bytes 65568 | tf_op jit(solution)/shard_map/ppermute | solution.py:301
  77.7 3.0 collective-permute-done.1
  80.7 4.8 collective-permute-done.2
  88.6 3.1 fusion.1
  91.7 4.9 all-to-all-start.4
  96.6 32.2 %collective-permute-done.5.refs_2_.refs_3_ = bf16[8,256,512]{2,1,0:T(8,128)(2,1)} collective-permute-done((bf16[8,256,512]{2,1,0:T(8,128)(2,1)}, bf16[8,256,512]{2,1,0:T(8,128)(2,1)}, u32[]{:S(2)}, u32[]{:S(2)}) %collective-permute-start.5) | collective-permute-done | bytes 2097184 | tf_op jit(solution)/shard_map/ppermute | solution.py:289
  131.3 6.7 all-to-all-start.5
  140.0 4.9 shard_map.140
  146.4 19.9 %all-to-all-done.5.refs_4_ = bf16[8,256,256]{2,1,0:T(8,128)(2,1)} async-done(((bf16[8,256,256]{2,1,0:T(8,128)(2,1)}), bf16[8,256,256]{2,1,0:T(8,128)(2,1)}, u32[]{:S(2)}, u32[]{:S(2)}) %all-to-all-start.5) | async-done | bytes 1048608 | tf_op jit(solution)/shard_map/all_to_all | solution.py:265
  166.3 5.6 all-to-all-start.2
  171.9 4.0 fusion.4
  184.9 4.4 all-to-all-done.2.q_ref
  192.4 5.4 all-to-all-start.3
  197.8 11.0 %all-to-all-done.3 = bf16[8,128,128]{2,1,0:T(8,128)(2,1)} async-done(((bf16[8,128,128]{2,1,0:T(8,128)(2,1)}), bf16[8,128,128]{2,1,0:T(8,128)(2,1)}, u32[]{:S(2)}, u32[]{:S(2)}) %all-to-all-start.3) | async-done | bytes 262176 | tf_op jit(solution)/shard_map/all_to_all | solution.py:265
  210.5 18.2 %collective-permute-done.11.refs_6_ = bf16[8,256,256]{2,1,0:T(8,128)(2,1)} collective-permute-done((bf16[8,256,256]{2,1,0:T(8,128)(2,1)}, bf16[8,256,256]{2,1,0:T(8,128)(2,1)}, u32[]{:S(2)}, u32[]{:S(2)}) %collective-permute-start.11) | collective-permute-done | bytes 1048608 | tf_op jit(solution)/shard_map/ppermute | solution.py:289
  231.6 4.6 shard_map.142.vo_ref
  238.7 7.2 %collective-permute-done.13.refs_0_ = bf16[64,1024]{1,0:T(8,128)(2,1)S(1)} collective-permute-done((bf16[64,1024]{1,0:T(8,128)(2,1)S(1)}, bf16[64,1024]{1,0:T(8,128)(2,1)S(1)}, u32[]{:S(2)}, u32[]{:S(2)}) %collective-permute-start.13) | collective-permute-done | bytes 131104 | tf_op jit(solution)/shard_map/ppermute | solution.py:286
  245.9 4.9 shard_map.144
  250.8 23.3 %all_to_all.126.q_ref = bf16[8,272,128]{2,1,0:T(8,128)(2,1)S(1)} all-to-all(bf16[8,272,128]{2,1,0:T(8,128)(2,1)S(1)} %get-tuple-element.81), channel_id=1, replica_groups=mesh['dp'=4,'section'=8,'tensor'=8] {'tensor'}, dimensions={0} | all-to-all | bytes 1114112 | tf_op jit(solution)/shard_map/all_to_all | solution.py:265
  275.3 11.5 %all_to_all.127.p_ref = bf16[8,64,128]{2,1,0:T(8,128)(2,1)S(1)} all-to-all(bf16[8,64,128]{2,1,0:T(8,128)(2,1)S(1)} %get-tuple-element.83), channel_id=1, replica_groups=mesh['dp'=4,'section'=8,'tensor'=8] {'tensor'}, dimensions={0} | all-to-all | bytes 262144 | tf_op jit(solution)/shard_map/all_to_all | solution.py:265
  290.4 9.9 %collective-permute-done.14.refs_0_ = bf16[64,1024]{1,0:T(8,128)(2,1)S(1)} collective-permute-done((bf16[64,1024]{1,0:T(8,128)(2,1)S(1)}, bf16[64,1024]{1,0:T(8,128)(2,1)S(1)}, u32[]{:S(2)}, u32[]{:S(2)}) %collective-permute-start.14) | collective-permute-done | bytes 131104 | tf_op jit(solution)/shard_map/ppermute | solution.py:286
  300.4 5.2 shard_map.147
  305.6 18.1 %all_to_all.128.q_ref = bf16[8,272,128]{2,1,0:T(8,128)(2,1)S(1)} all-to-all(bf16[8,272,128]{2,1,0:T(8,128)(2,1)S(1)} %get-tuple-element.87), channel_id=1, replica_groups=mesh['dp'=4,'section'=8,'tensor'=8] {'tensor'}, dimensions={0} | all-to-all | bytes 1114112 | tf_op jit(solution)/shard_map/all_to_all | solution.py:265
  324.9 11.5 %all_to_all.129.p_ref = bf16[8,64,128]{2,1,0:T(8,128)(2,1)S(1)} all-to-all(bf16[8,64,128]{2,1,0:T(8,128)(2,1)S(1)} %get-tuple-element.89), channel_id=1, replica_groups=mesh['dp'=4,'section'=8,'tensor'=8] {'tensor'}, dimensions={0} | all-to-all | bytes 262144 | tf_op jit(solution)/shard_map/all_to_all | solution.py:265
  337.5 7.1 %collective-permute-done.15.refs_0_ = bf16[64,1024]{1,0:T(8,128)(2,1)S(1)} collective-permute-done((bf16[64,1024]{1,0:T(8,128)(2,1)S(1)}, bf16[64,1024]{1,0:T(8,128)(2,1)S(1)}, u32[]{:S(2)}, u32[]{:S(2)}) %collective-permute-start.15) | collective-permute-done | bytes 131104 | tf_op jit(solution)/shard_map/ppermute | solution.py:286
  344.6 4.9 shard_map.150
  349.5 16.2 %all_to_all.130.q_ref = bf16[8,272,128]{2,1,0:T(8,128)(2,1)S(1)} all-to-all(bf16[8,272,128]{2,1,0:T(8,128)(2,1)S(1)} %get-tuple-element.93), channel_id=1, replica_groups=mesh['dp'=4,'section'=8,'tensor'=8] {'tensor'}, dimensions={0} | all-to-all | bytes 1114112 | tf_op jit(solution)/shard_map/all_to_all | solution.py:265
  366.9 11.5 %all_to_all.131.p_ref = bf16[8,64,128]{2,1,0:T(8,128)(2,1)S(1)} all-to-all(bf16[8,64,128]{2,1,0:T(8,128)(2,1)S(1)} %get-tuple-element.95), channel_id=1, replica_groups=mesh['dp'=4,'section'=8,'tensor'=8] {'tensor'}, dimensions={0} | all-to-all | bytes 262144 | tf_op jit(solution)/shard_map/all_to_all | solution.py:265
  379.6 7.1 %collective-permute-done.16.refs_0_ = bf16[64,1024]{1,0:T(8,128)(2,1)S(1)} collective-permute-done((bf16[64,1024]{1,0:T(8,128)(2,1)S(1)}, bf16[64,1024]{1,0:T(8,128)(2,1)S(1)}, u32[]{:S(2)}, u32[]{:S(2)}) %collective-permute-start.16) | collective-permute-done | bytes 131104 | tf_op jit(solution)/shard_map/ppermute | solution.py:286
  386.6 4.9 shard_map.153
  391.5 16.0 %all_to_all.132.q_ref = bf16[8,272,128]{2,1,0:T(8,128)(2,1)S(1)} all-to-all(bf16[8,272,128]{2,1,0:T(8,128)(2,1)S(1)} %get-tuple-element.99), channel_id=1, replica_groups=mesh['dp'=4,'section'=8,'tensor'=8] {'tensor'}, dimensions={0} | all-to-all | bytes 1114112 | tf_op jit(solution)/shard_map/all_to_all | solution.py:265
  408.8 11.4 %all_to_all.133.p_ref = bf16[8,64,128]{2,1,0:T(8,128)(2,1)S(1)} all-to-all(bf16[8,64,128]{2,1,0:T(8,128)(2,1)S(1)} %get-tuple-element.101), channel_id=1, replica_groups=mesh['dp'=4,'section'=8,'tensor'=8] {'tensor'}, dimensions={0} | all-to-all | bytes 262144 | tf_op jit(solution)/shard_map/all_to_all | solution.py:265
  421.6 7.1 %collective-permute-done.17.refs_0_ = bf16[64,1024]{1,0:T(8,128)(2,1)S(1)} collective-permute-done((bf16[64,1024]{1,0:T(8,128)(2,1)S(1)}, bf16[64,1024]{1,0:T(8,128)(2,1)S(1)}, u32[]{:S(2)}, u32[]{:S(2)}) %collective-permute-start.17) | collective-permute-done | bytes 131104 | tf_op jit(solution)/shard_map/ppermute | solution.py:286
  428.7 5.7 shard_map.156
  435.1 4.9 all-to-all-start.14
  441.2 11.1 %all-to-all-done.14.q_ref = bf16[8,272,128]{2,1,0:T(8,128)(2,1)S(1)} async-done(((bf16[8,272,128]{2,1,0:T(8,128)(2,1)}), bf16[8,272,128]{2,1,0:T(8,128)(2,1)S(1)}, u32[]{:S(2)}, u32[]{:S(2)}) %all-to-all-start.14) | async-done | bytes 557088 | tf_op jit(solution)/shard_map/all_to_all | solution.py:265
  455.8 4.7 all-to-all-start.15
  460.6 6.3 fusion.5
  471.5 7.1 %collective-permute-done.18.refs_0_ = bf16[64,1024]{1,0:T(8,128)(2,1)S(1)} collective-permute-done((bf16[64,1024]{1,0:T(8,128)(2,1)S(1)}, bf16[64,1024]{1,0:T(8,128)(2,1)S(1)}, u32[]{:S(2)}, u32[]{:S(2)}) %collective-permute-start.18) | collective-permute-done | bytes 131104 | tf_op jit(solution)/shard_map/ppermute | solution.py:286
  478.6 5.2 shard_map.159
  483.8 19.5 %all_to_all.134.q_ref = bf16[8,272,128]{2,1,0:T(8,128)(2,1)S(1)} all-to-all(bf16[8,272,128]{2,1,0:T(8,128)(2,1)S(1)} %get-tuple-element.113), channel_id=1, replica_groups=mesh['dp'=4,'section'=8,'tensor'=8] {'tensor'}, dimensions={0} | all-to-all | bytes 1114112 | tf_op jit(solution)/shard_map/all_to_all | solution.py:265
  504.5 11.5 %all_to_all.135.p_ref = bf16[8,64,128]{2,1,0:T(8,128)(2,1)S(1)} all-to-all(bf16[8,64,128]{2,1,0:T(8,128)(2,1)S(1)} %get-tuple-element.115), channel_id=1, replica_groups=mesh['dp'=4,'section'=8,'tensor'=8] {'tensor'}, dimensions={0} | all-to-all | bytes 262144 | tf_op jit(solution)/shard_map/all_to_all | solution.py:265
  517.1 7.1 %collective-permute-done.19.refs_0_ = bf16[64,1024]{1,0:T(8,128)(2,1)S(1)} collective-permute-done((bf16[64,1024]{1,0:T(8,128)(2,1)S(1)}, bf16[64,1024]{1,0:T(8,128)(2,1)S(1)}, u32[]{:S(2)}, u32[]{:S(2)}) %collective-permute-start.19) | collective-permute-done | bytes 131104 | tf_op jit(solution)/shard_map/ppermute | solution.py:286
  524.2 4.9 shard_map.162
  529.1 16.9 %all_to_all.136.q_ref = bf16[8,272,128]{2,1,0:T(8,128)(2,1)S(1)} all-to-all(bf16[8,272,128]{2,1,0:T(8,128)(2,1)S(1)} %get-tuple-element.119), channel_id=1, replica_groups=mesh['dp'=4,'section'=8,'tensor'=8] {'tensor'}, dimensions={0} | all-to-all | bytes 1114112 | tf_op jit(solution)/shard_map/all_to_all | solution.py:265
  547.9 4.7 all-to-all-start.19
  554.8 4.0 shard_map.167
  560.3 5.7 all-to-all-start.21
  570.3 7.1 %collective-permute-done.20.refs_0_ = bf16[64,1024]{1,0:T(8,128)(2,1)S(1)} collective-permute-done((bf16[64,1024]{1,0:T(8,128)(2,1)S(1)}, bf16[64,1024]{1,0:T(8,128)(2,1)S(1)}, u32[]{:S(2)}, u32[]{:S(2)}) %collective-permute-start.20) | collective-permute-done | bytes 131104 | tf_op jit(solution)/shard_map/ppermute | solution.py:286
  577.3 4.9 shard_map.165
  583.7 7.2 %all-to-all-start.20 = ((bf16[8,272,128]{2,1,0:T(8,128)(2,1)}), bf16[8,272,128]{2,1,0:T(8,128)(2,1)S(1)}, u32[]{:S(2)}, u32[]{:S(2)}) async-start(bf16[8,272,128]{2,1,0:T(8,128)(2,1)} %copy-done.11), calls=%async_computation.20 | async-start | bytes 1114112 | tf_op jit(solution)/shard_map/all_to_all | solution.py:265
  592.6 11.0 %all-to-all-done.20.q_ref = bf16[8,272,128]{2,1,0:T(8,128)(2,1)S(1)} async-done(((bf16[8,272,128]{2,1,0:T(8,128)(2,1)}), bf16[8,272,128]{2,1,0:T(8,128)(2,1)S(1)}, u32[]{:S(2)}, u32[]{:S(2)}) %all-to-all-start.20) | async-done | bytes 557088 | tf_op jit(solution)/shard_map/all_to_all | solution.py:265
  606.2 4.7 all-to-all-start.22
  615.3 4.0 shard_map.169
  619.6 6.9 %all-to-all-start.23 = ((bf16[8,32,1024]{2,1,0:T(8,128)(2,1)}), bf16[8,32,1024]{2,1,0:T(8,128)(2,1)S(1)}, u32[]{:S(2)}, u32[]{:S(2)}) async-start(bf16[8,32,1024]{2,1,0:T(8,128)(2,1)} %shard_map.169), calls=%async_computation.23 | async-start | bytes 1048576 | tf_op jit(solution)/shard_map/all_to_all | solution.py:265
  630.6 3.4 collective-permute-start.21
  635.9 7.2 %collective-permute-start.23 = (bf16[2,64,256]{2,1,0:T(8,128)(2,1)S(1)}, bf16[2,64,256]{2,1,0:T(8,128)(2,1)S(1)}, u32[]{:S(2)}, u32[]{:S(2)}) collective-permute-start(bf16[2,64,256]{2,1,0:T(8,128)(2,1)S(1)} %get-tuple-element.146), channel_id=1, source_target_pairs={{2,0},{6,1},{3,2},{7,3},{0,4},{4,5},{1,6},{5,7},{10,8},{14,9},{11,... | collective-permute-start | bytes 196616 | tf_op jit(solution)/shard_map/ppermute | solution.py:311
  652.3 3.4 all-to-all-start.24
  656.4 5.8 all-to-all-done.24
  (201 shorter events, 95.6 us)
Async XLA Ops:
  7.2 453.4 %copy-start = (bf16[1,2,64,8192]{3,2,1,0:T(8,128)(2,1)S(1)}, bf16[1,2,64,8192]{3,2,1,0:T(8,128)(2,1)}, u32[]{:S(2)}) copy-start(bf16[1,2,64,8192]{3,2,1,0:T(8,128)(2,1)} %param.25) | copy-start | bytes 6291460
  7.2 2.5 copy-start.39
  7.2 2.5 copy-start.32
  7.2 3.2 copy-start.36
  7.2 81.4 %all-gather.6.cloned.1.call-start = ((), (), s32[]{:S(2)}) async-start(), calls=%async_computation.26 | async-start | bytes 5242880 | tf_op jit(solution)/shard_map/all_gather | solution.py:321
  11.0 128.9 %copy-start.38 = (s32[2]{0:T(128)}, s32[2]{0:T(128)S(1)}, u32[]{:S(2)}) copy-start(s32[2]{0:T(128)S(1)} %get-tuple-element.136) | copy-start | bytes 28
  23.0 8.7 %copy-start.33 = (bf16[2,64,1024]{2,1,0:T(8,128)(2,1)S(1)}, bf16[2,64,1024]{2,1,0:T(8,128)(2,1)}, u32[]{:S(2)}) copy-start(bf16[2,64,1024]{2,1,0:T(8,128)(2,1)} %param.13) | copy-start | bytes 786436
  23.0 62.7 %all-to-all-start.1 = ((bf16[8,256,512]{2,1,0:T(8,128)(2,1)}), bf16[8,256,512]{2,1,0:T(8,128)(2,1)}, u32[]{:S(2)}, u32[]{:S(2)}) async-start(bf16[8,256,512]{2,1,0:T(8,128)(2,1)} %bitcast.112), calls=%async_computation.1 | async-start | bytes 4194304 | tf_op jit(solution)/shard_map/all_to_all | solution.py:265
  31.7 97.4 %all-gather.4.cloned.1.call-start = ((), (), s32[]{:S(2)}) async-start(), calls=%async_computation.25 | async-start | bytes 1179648 | tf_op jit(solution)/shard_map/all_gather | solution.py:327
  32.5 45.2 %collective-permute-start = (bf16[2,64,256]{2,1,0:T(8,128)(2,1)S(1)}, bf16[2,64,256]{2,1,0:T(8,128)(2,1)S(1)}, u32[]{:S(2)}, u32[]{:S(2)}) collective-permute-start(bf16[2,64,256]{2,1,0:T(8,128)(2,1)S(1)} %get-tuple-element.158), channel_id=1, source_target_pairs={{0,0},{1,4},{2,1},{3,5},{4,2},{5,6},{6,3},{7,7},{8,8},{9,12},{10,9... | collective-permute-start | bytes 196616 | tf_op jit(solution)/shard_map/ppermute | solution.py:301
  38.9 41.8 %collective-permute-start.1 = (bf16[2,64,256]{2,1,0:T(8,128)(2,1)S(1)}, bf16[2,64,256]{2,1,0:T(8,128)(2,1)S(1)}, u32[]{:S(2)}, u32[]{:S(2)}) collective-permute-start(bf16[2,64,256]{2,1,0:T(8,128)(2,1)S(1)} %get-tuple-element.161), channel_id=1, source_target_pairs={{0,1},{1,5},{2,2},{3,6},{4,3},{5,7},{6,0},{7,4},{8,9},{9,13},{10,1... | collective-permute-start | bytes 196616 | tf_op jit(solution)/shard_map/ppermute | solution.py:301
  41.4 44.2 %collective-permute-start.2 = (bf16[2,64,256]{2,1,0:T(8,128)(2,1)S(1)}, bf16[2,64,256]{2,1,0:T(8,128)(2,1)S(1)}, u32[]{:S(2)}, u32[]{:S(2)}) collective-permute-start(bf16[2,64,256]{2,1,0:T(8,128)(2,1)S(1)} %get-tuple-element.160), channel_id=1, source_target_pairs={{0,2},{1,6},{2,3},{3,7},{4,0},{5,4},{6,1},{7,5},{8,10},{9,14},{10,... | collective-permute-start | bytes 196616 | tf_op jit(solution)/shard_map/ppermute | solution.py:301
  42.4 43.3 %collective-permute-start.3 = (bf16[2,64,256]{2,1,0:T(8,128)(2,1)S(1)}, bf16[2,64,256]{2,1,0:T(8,128)(2,1)S(1)}, u32[]{:S(2)}, u32[]{:S(2)}) collective-permute-start(bf16[2,64,256]{2,1,0:T(8,128)(2,1)S(1)} %get-tuple-element.159), channel_id=1, source_target_pairs={{0,3},{1,7},{2,0},{3,4},{4,1},{5,5},{6,2},{7,6},{8,11},{9,15},{10,... | collective-permute-start | bytes 196616 | tf_op jit(solution)/shard_map/ppermute | solution.py:301
  85.7 43.1 %collective-permute-start.5 = (bf16[8,256,512]{2,1,0:T(8,128)(2,1)}, bf16[8,256,512]{2,1,0:T(8,128)(2,1)}, u32[]{:S(2)}, u32[]{:S(2)}) collective-permute-start(bf16[8,256,512]{2,1,0:T(8,128)(2,1)} %all-to-all-done.1.refs_0_.refs_1_), channel_id=1, source_target_pairs={{0,128},{64,192},{128,0},{192,64},{1,129},{65,193},{129,1},{193,65... | collective-permute-start | bytes 6291464 | tf_op jit(solution)/shard_map/ppermute | solution.py:289
  91.7 46.8 %copy-start.35 = (f32[1,8192]{1,0:T(1,128)S(1)}, f32[1,8192]{1,0:T(1,128)}, u32[]{:S(2)}) copy-start(f32[1,8192]{1,0:T(1,128)} %param.17) | copy-start | bytes 98308
  91.7 39.6 %all-to-all-start.4 = ((bf16[8,256,256]{2,1,0:T(8,128)(2,1)}), bf16[8,256,256]{2,1,0:T(8,128)(2,1)S(1)}, u32[]{:S(2)}, u32[]{:S(2)}) async-start(bf16[8,256,256]{2,1,0:T(8,128)(2,1)} %get-tuple-element.139), calls=%async_computation.4 | async-start | bytes 2097152 | tf_op jit(solution)/shard_map/all_to_all | solution.py:265
  96.6 43.4 %collective-permute-start.4 = (bf16[8,256,512]{2,1,0:T(8,128)(2,1)}, bf16[8,256,512]{2,1,0:T(8,128)(2,1)}, u32[]{:S(2)}, u32[]{:S(2)}) collective-permute-start(bf16[8,256,512]{2,1,0:T(8,128)(2,1)} %all-to-all-done.1.refs_0_.refs_1_), channel_id=1, source_target_pairs={{0,64},{64,0},{128,192},{192,128},{1,65},{65,1},{129,193},{193,129... | collective-permute-start | bytes 6291464 | tf_op jit(solution)/shard_map/ppermute | solution.py:289
  128.8 11.2 %collective-permute-start.6 = (bf16[8,256,512]{2,1,0:T(8,128)(2,1)}, bf16[8,256,512]{2,1,0:T(8,128)(2,1)}, u32[]{:S(2)}, u32[]{:S(2)}) collective-permute-start(bf16[8,256,512]{2,1,0:T(8,128)(2,1)} %collective-permute-done.5.refs_2_.refs_3_), channel_id=1, source_target_pairs={{0,64},{64,0},{128,192},{192,128},{1,65},{65,1},{129,193},{193,129... | collective-permute-start | bytes 6291464 | tf_op jit(solution)/shard_map/ppermute | solution.py:289
  131.3 35.0 %all-to-all-start.5 = ((bf16[8,256,256]{2,1,0:T(8,128)(2,1)}), bf16[8,256,256]{2,1,0:T(8,128)(2,1)}, u32[]{:S(2)}, u32[]{:S(2)}) async-start(bf16[8,256,256]{2,1,0:T(8,128)(2,1)} %get-tuple-element.77), calls=%async_computation.5 | async-start | bytes 2097152 | tf_op jit(solution)/shard_map/all_to_all | solution.py:265
  166.3 22.9 %all-to-all-start.2 = ((bf16[8,272,128]{2,1,0:T(8,128)(2,1)}), bf16[8,272,128]{2,1,0:T(8,128)(2,1)}, u32[]{:S(2)}, u32[]{:S(2)}) async-start(bf16[8,272,128]{2,1,0:T(8,128)(2,1)} %copy-done.10), calls=%async_computation.2 | async-start | bytes 1114112 | tf_op jit(solution)/shard_map/all_to_all | solution.py:265
  171.9 12.2 %copy-start.31 = (f32[1,128]{1,0:T(1,128)S(1)}, f32[1,128]{1,0:T(1,128)}, u32[]{:S(2)}) copy-start(f32[1,128]{1,0:T(1,128)} %gain_ref.21) | copy-start | bytes 1540
  171.9 17.4 %copy-start.30 = (f32[1,128]{1,0:T(1,128)S(1)}, f32[1,128]{1,0:T(1,128)}, u32[]{:S(2)}) copy-start(f32[1,128]{1,0:T(1,128)} %gain_ref.19) | copy-start | bytes 1540
  179.7 30.2 %collective-permute-start.8 = (bf16[8,256,256]{2,1,0:T(8,128)(2,1)S(1)}, bf16[8,256,256]{2,1,0:T(8,128)(2,1)}, u32[]{:S(2)}, u32[]{:S(2)}) collective-permute-start(bf16[8,256,256]{2,1,0:T(8,128)(2,1)S(1)} %all-to-all-done.4.refs_0_), channel_id=1, source_target_pairs={{0,128},{64,192},{128,0},{192,64},{1,129},{65,193},{129,1},{193,65... | collective-permute-start | bytes 3145736 | tf_op jit(solution)/shard_map/ppermute | solution.py:289
  182.5 46.2 %collective-permute-start.11 = (bf16[8,256,256]{2,1,0:T(8,128)(2,1)}, bf16[8,256,256]{2,1,0:T(8,128)(2,1)}, u32[]{:S(2)}, u32[]{:S(2)}) collective-permute-start(bf16[8,256,256]{2,1,0:T(8,128)(2,1)} %all-to-all-done.5.refs_4_), channel_id=1, source_target_pairs={{0,128},{64,192},{128,0},{192,64},{1,129},{65,193},{129,1},{193,65... | collective-permute-start | bytes 3145736 | tf_op jit(solution)/shard_map/ppermute | solution.py:289
  192.4 16.4 %all-to-all-start.3 = ((bf16[8,128,128]{2,1,0:T(8,128)(2,1)}), bf16[8,128,128]{2,1,0:T(8,128)(2,1)}, u32[]{:S(2)}, u32[]{:S(2)}) async-start(bf16[8,128,128]{2,1,0:T(8,128)(2,1)} %pad_maximum_fusion.4), calls=%async_computation.3 | async-start | bytes 524288 | tf_op jit(solution)/shard_map/all_to_all | solution.py:265
  197.8 262.7 %all-gather.8.cloned.1.call-start = ((), (), s32[]{:S(2)}) async-start(), calls=%async_computation.27 | async-start | bytes 10485760 | tf_op jit(solution)/shard_map/all_gather | solution.py:365
  197.8 30.8 %collective-permute-start.7 = (bf16[8,256,256]{2,1,0:T(8,128)(2,1)S(1)}, bf16[8,256,256]{2,1,0:T(8,128)(2,1)}, u32[]{:S(2)}, u32[]{:S(2)}) collective-permute-start(bf16[8,256,256]{2,1,0:T(8,128)(2,1)S(1)} %all-to-all-done.4.refs_0_), channel_id=1, source_target_pairs={{0,64},{64,0},{128,192},{192,128},{1,65},{65,1},{129,193},{193,129... | collective-permute-start | bytes 3145736 | tf_op jit(solution)/shard_map/ppermute | solution.py:289
  209.9 18.8 %collective-permute-start.9 = (bf16[8,256,256]{2,1,0:T(8,128)(2,1)}, bf16[8,256,256]{2,1,0:T(8,128)(2,1)S(1)}, u32[]{:S(2)}, u32[]{:S(2)}) collective-permute-start(bf16[8,256,256]{2,1,0:T(8,128)(2,1)} %collective-permute-done.8.refs_2_), channel_id=1, source_target_pairs={{0,64},{64,0},{128,192},{192,128},{1,65},{65,1},{129,193},{193,129... | collective-permute-start | bytes 3145736 | tf_op jit(solution)/shard_map/ppermute | solution.py:289
  210.0 18.7 %collective-permute-start.10 = (bf16[8,256,256]{2,1,0:T(8,128)(2,1)}, bf16[8,256,256]{2,1,0:T(8,128)(2,1)S(1)}, u32[]{:S(2)}, u32[]{:S(2)}) collective-permute-start(bf16[8,256,256]{2,1,0:T(8,128)(2,1)} %all-to-all-done.5.refs_4_), channel_id=1, source_target_pairs={{0,64},{64,0},{128,192},{192,128},{1,65},{65,1},{129,193},{193,129... | collective-permute-start | bytes 3145736 | tf_op jit(solution)/shard_map/ppermute | solution.py:289
  228.7 2.9 collective-permute-start.12
  231.6 4.6 copy-start.25
  238.1 36.0 %copy-start.17 = (f32[2,64,512]{2,1,0:T(8,128)S(1)}, f32[2,64,512]{2,1,0:T(8,128)}, u32[]{:S(2)}) copy-start(f32[2,64,512]{2,1,0:T(8,128)} %copy-done.16) | copy-start | bytes 786436
  238.1 7.8 %collective-permute-start.13 = (bf16[64,1024]{1,0:T(8,128)(2,1)S(1)}, bf16[64,1024]{1,0:T(8,128)(2,1)S(1)}, u32[]{:S(2)}, u32[]{:S(2)}) collective-permute-start(bf16[64,1024]{1,0:T(8,128)(2,1)S(1)} %get-tuple-element.80), channel_id=1, source_target_pairs={{0,8},{8,16},{16,24},{24,32},{32,40},{40,48},{48,56},{56,0},{1,9},... | collective-permute-start | bytes 393224 | tf_op jit(solution)/shard_map/ppermute | solution.py:286
  290.4 10.0 %collective-permute-start.14 = (bf16[64,1024]{1,0:T(8,128)(2,1)S(1)}, bf16[64,1024]{1,0:T(8,128)(2,1)S(1)}, u32[]{:S(2)}, u32[]{:S(2)}) collective-permute-start(bf16[64,1024]{1,0:T(8,128)(2,1)S(1)} %get-tuple-element.86), channel_id=1, source_target_pairs={{0,8},{8,16},{16,24},{24,32},{32,40},{40,48},{48,56},{56,0},{1,9},... | collective-permute-start | bytes 393224 | tf_op jit(solution)/shard_map/ppermute | solution.py:286
  300.4 36.0 %copy-start.3 = (bf16[2,1024,1024]{2,1,0:T(8,128)(2,1)S(1)}, bf16[2,1024,1024]{2,1,0:T(8,128)(2,1)}, u32[]{:S(2)}) copy-start(bf16[2,1024,1024]{2,1,0:T(8,128)(2,1)} %copy-done.1) | copy-start | bytes 12582916
  337.4 7.2 %collective-permute-start.15 = (bf16[64,1024]{1,0:T(8,128)(2,1)S(1)}, bf16[64,1024]{1,0:T(8,128)(2,1)S(1)}, u32[]{:S(2)}, u32[]{:S(2)}) collective-permute-start(bf16[64,1024]{1,0:T(8,128)(2,1)S(1)} %get-tuple-element.92), channel_id=1, source_target_pairs={{0,8},{8,16},{16,24},{24,32},{32,40},{40,48},{48,56},{56,0},{1,9},... | collective-permute-start | bytes 393224 | tf_op jit(solution)/shard_map/ppermute | solution.py:286
  379.5 7.2 %collective-permute-start.16 = (bf16[64,1024]{1,0:T(8,128)(2,1)S(1)}, bf16[64,1024]{1,0:T(8,128)(2,1)S(1)}, u32[]{:S(2)}, u32[]{:S(2)}) collective-permute-start(bf16[64,1024]{1,0:T(8,128)(2,1)S(1)} %get-tuple-element.98), channel_id=1, source_target_pairs={{0,8},{8,16},{16,24},{24,32},{32,40},{40,48},{48,56},{56,0},{1,9},... | collective-permute-start | bytes 393224 | tf_op jit(solution)/shard_map/ppermute | solution.py:286
  408.8 11.5 %copy-start.20 = (f32[2,64,512]{2,1,0:T(8,128)}, f32[2,64,512]{2,1,0:T(8,128)S(1)}, u32[]{:S(2)}) copy-start(f32[2,64,512]{2,1,0:T(8,128)S(1)} %get-tuple-element.106.refs_0_) | copy-start | bytes 786436
  421.3 7.4 %collective-permute-start.17 = (bf16[64,1024]{1,0:T(8,128)(2,1)S(1)}, bf16[64,1024]{1,0:T(8,128)(2,1)S(1)}, u32[]{:S(2)}, u32[]{:S(2)}) collective-permute-start(bf16[64,1024]{1,0:T(8,128)(2,1)S(1)} %get-tuple-element.104), channel_id=1, source_target_pairs={{0,8},{8,16},{16,24},{24,32},{32,40},{40,48},{48,56},{56,0},{1,9},... | collective-permute-start | bytes 393224 | tf_op jit(solution)/shard_map/ppermute | solution.py:286
  435.1 17.2 %all-to-all-start.14 = ((bf16[8,272,128]{2,1,0:T(8,128)(2,1)}), bf16[8,272,128]{2,1,0:T(8,128)(2,1)S(1)}, u32[]{:S(2)}, u32[]{:S(2)}) async-start(bf16[8,272,128]{2,1,0:T(8,128)(2,1)} %get-tuple-element.105), calls=%async_computation.14 | async-start | bytes 1114112 | tf_op jit(solution)/shard_map/all_to_all | solution.py:265
  455.8 12.4 %all-to-all-start.15 = ((bf16[8,64,128]{2,1,0:T(8,128)(2,1)}), bf16[8,64,128]{2,1,0:T(8,128)(2,1)S(1)}, u32[]{:S(2)}, u32[]{:S(2)}) async-start(bf16[8,64,128]{2,1,0:T(8,128)(2,1)} %get-tuple-element.107), calls=%async_computation.15 | async-start | bytes 262144 | tf_op jit(solution)/shard_map/all_to_all | solution.py:265
  460.5 6.4 copy-start.37
  460.6 7.6 %copy-start.27 = (bf16[64,1024]{1,0:T(8,128)(2,1)S(1)}, bf16[64,1024]{1,0:T(8,128)(2,1)}, u32[]{:S(2)}) copy-start(bf16[64,1024]{1,0:T(8,128)(2,1)} %copy-done.26) | copy-start | bytes 393220
  471.4 31.8 %copy-start.19 = (f32[2,64,512]{2,1,0:T(8,128)S(1)}, f32[2,64,512]{2,1,0:T(8,128)}, u32[]{:S(2)}) copy-start(f32[2,64,512]{2,1,0:T(8,128)} %copy-done.18) | copy-start | bytes 786436
  471.5 7.2 %collective-permute-start.18 = (bf16[64,1024]{1,0:T(8,128)(2,1)S(1)}, bf16[64,1024]{1,0:T(8,128)(2,1)S(1)}, u32[]{:S(2)}, u32[]{:S(2)}) collective-permute-start(bf16[64,1024]{1,0:T(8,128)(2,1)S(1)} %get-tuple-element.112), channel_id=1, source_target_pairs={{0,8},{8,16},{16,24},{24,32},{32,40},{40,48},{48,56},{56,0},{1,9},... | collective-permute-start | bytes 393224 | tf_op jit(solution)/shard_map/ppermute | solution.py:286
  478.6 37.4 %copy-start.5 = (bf16[2,1024,1024]{2,1,0:T(8,128)(2,1)S(1)}, bf16[2,1024,1024]{2,1,0:T(8,128)(2,1)}, u32[]{:S(2)}) copy-start(bf16[2,1024,1024]{2,1,0:T(8,128)(2,1)} %copy-done.1) | copy-start | bytes 12582916
  517.0 7.2 %collective-permute-start.19 = (bf16[64,1024]{1,0:T(8,128)(2,1)S(1)}, bf16[64,1024]{1,0:T(8,128)(2,1)S(1)}, u32[]{:S(2)}, u32[]{:S(2)}) collective-permute-start(bf16[64,1024]{1,0:T(8,128)(2,1)S(1)} %get-tuple-element.118), channel_id=1, source_target_pairs={{0,8},{8,16},{16,24},{24,32},{32,40},{40,48},{48,56},{56,0},{1,9},... | collective-permute-start | bytes 393224 | tf_op jit(solution)/shard_map/ppermute | solution.py:286
  529.1 18.9 %copy-start.28 = (bf16[64,1024]{1,0:T(8,128)(2,1)}, bf16[64,1024]{1,0:T(8,128)(2,1)S(1)}, u32[]{:S(2)}) copy-start(bf16[64,1024]{1,0:T(8,128)(2,1)S(1)} %get-tuple-element.122.h_ref) | copy-start | bytes 393220
  547.9 12.4 %all-to-all-start.19 = ((bf16[8,64,128]{2,1,0:T(8,128)(2,1)}), bf16[8,64,128]{2,1,0:T(8,128)(2,1)S(1)}, u32[]{:S(2)}, u32[]{:S(2)}) async-start(bf16[8,64,128]{2,1,0:T(8,128)(2,1)} %get-tuple-element.121), calls=%async_computation.19 | async-start | bytes 262144 | tf_op jit(solution)/shard_map/all_to_all | solution.py:265
  554.8 11.2 %copy-start.29 = (bf16[64,1024]{1,0:T(8,128)(2,1)S(1)}, bf16[64,1024]{1,0:T(8,128)(2,1)}, u32[]{:S(2)}) copy-start(bf16[64,1024]{1,0:T(8,128)(2,1)} %copy-done.28) | copy-start | bytes 393220
  560.3 23.4 %all-to-all-start.21 = ((bf16[8,32,1024]{2,1,0:T(8,128)(2,1)}), bf16[8,32,1024]{2,1,0:T(8,128)(2,1)}, u32[]{:S(2)}, u32[]{:S(2)}) async-start(bf16[8,32,1024]{2,1,0:T(8,128)(2,1)} %shard_map.167), calls=%async_computation.21 | async-start | bytes 1048576 | tf_op jit(solution)/shard_map/all_to_all | solution.py:265
  570.0 7.3 %collective-permute-start.20 = (bf16[64,1024]{1,0:T(8,128)(2,1)S(1)}, bf16[64,1024]{1,0:T(8,128)(2,1)S(1)}, u32[]{:S(2)}, u32[]{:S(2)}) collective-permute-start(bf16[64,1024]{1,0:T(8,128)(2,1)S(1)} %get-tuple-element.124), channel_id=1, source_target_pairs={{0,8},{8,16},{16,24},{24,32},{32,40},{40,48},{48,56},{56,0},{1,9},... | collective-permute-start | bytes 393224 | tf_op jit(solution)/shard_map/ppermute | solution.py:286
  583.7 19.9 %all-to-all-start.20 = ((bf16[8,272,128]{2,1,0:T(8,128)(2,1)}), bf16[8,272,128]{2,1,0:T(8,128)(2,1)S(1)}, u32[]{:S(2)}, u32[]{:S(2)}) async-start(bf16[8,272,128]{2,1,0:T(8,128)(2,1)} %copy-done.11), calls=%async_computation.20 | async-start | bytes 1114112 | tf_op jit(solution)/shard_map/all_to_all | solution.py:265
  606.2 13.4 %all-to-all-start.22 = ((bf16[8,64,128]{2,1,0:T(8,128)(2,1)}), bf16[8,64,128]{2,1,0:T(8,128)(2,1)S(1)}, u32[]{:S(2)}, u32[]{:S(2)}) async-start(bf16[8,64,128]{2,1,0:T(8,128)(2,1)} %get-tuple-element.129), calls=%async_computation.22 | async-start | bytes 262144 | tf_op jit(solution)/shard_map/all_to_all | solution.py:265
  615.3 11.2 %copy-start.13 = (bf16[2,64,1024]{2,1,0:T(8,128)(2,1)S(1)}, bf16[2,64,1024]{2,1,0:T(8,128)(2,1)}, u32[]{:S(2)}) copy-start(bf16[2,64,1024]{2,1,0:T(8,128)(2,1)} %copy-done.12) | copy-start | bytes 786436
  615.3 11.2 %copy-start.23 = (bf16[64,1024]{1,0:T(8,128)(2,1)S(1)}, bf16[64,1024]{1,0:T(8,128)(2,1)}, u32[]{:S(2)}) copy-start(bf16[64,1024]{1,0:T(8,128)(2,1)} %copy-done.22) | copy-start | bytes 393220
  619.6 31.8 %all-to-all-start.23 = ((bf16[8,32,1024]{2,1,0:T(8,128)(2,1)}), bf16[8,32,1024]{2,1,0:T(8,128)(2,1)S(1)}, u32[]{:S(2)}, u32[]{:S(2)}) async-start(bf16[8,32,1024]{2,1,0:T(8,128)(2,1)} %shard_map.169), calls=%async_computation.23 | async-start | bytes 1048576 | tf_op jit(solution)/shard_map/all_to_all | solution.py:265
  628.7 16.3 %copy-start.40 = (s32[1,2]{1,0:T(1,128)S(1)}, s32[1,2]{1,0:T(1,128)}, u32[]{:S(2)}) copy-start(s32[1,2]{1,0:T(1,128)} %param.14) | copy-start | bytes 28
  628.7 20.6 %copy-start.34 = (bf16[32,1024]{1,0:T(8,128)(2,1)S(1)}, bf16[32,1024]{1,0:T(8,128)(2,1)}, u32[]{:S(2)}) copy-start(bf16[32,1024]{1,0:T(8,128)(2,1)} %reduce_sum.43) | copy-start | bytes 196612
  630.6 18.9 %collective-permute-start.21 = (bf16[2,64,256]{2,1,0:T(8,128)(2,1)S(1)}, bf16[2,64,256]{2,1,0:T(8,128)(2,1)S(1)}, u32[]{:S(2)}, u32[]{:S(2)}) collective-permute-start(bf16[2,64,256]{2,1,0:T(8,128)(2,1)S(1)} %get-tuple-element.144), channel_id=1, source_target_pairs={{0,0},{4,1},{1,2},{5,3},{2,4},{6,5},{3,6},{7,7},{8,8},{12,9},{9,10... | collective-permute-start | bytes 196616 | tf_op jit(solution)/shard_map/ppermute | solution.py:311
  633.9 15.5 %collective-permute-start.22 = (bf16[2,64,256]{2,1,0:T(8,128)(2,1)S(1)}, bf16[2,64,256]{2,1,0:T(8,128)(2,1)S(1)}, u32[]{:S(2)}, u32[]{:S(2)}) collective-permute-start(bf16[2,64,256]{2,1,0:T(8,128)(2,1)S(1)} %get-tuple-element.147), channel_id=1, source_target_pairs={{1,0},{5,1},{2,2},{6,3},{3,4},{7,5},{0,6},{4,7},{9,8},{13,9},{10,1... | collective-permute-start | bytes 196616 | tf_op jit(solution)/shard_map/ppermute | solution.py:311
  635.9 13.6 %collective-permute-start.23 = (bf16[2,64,256]{2,1,0:T(8,128)(2,1)S(1)}, bf16[2,64,256]{2,1,0:T(8,128)(2,1)S(1)}, u32[]{:S(2)}, u32[]{:S(2)}) collective-permute-start(bf16[2,64,256]{2,1,0:T(8,128)(2,1)S(1)} %get-tuple-element.146), channel_id=1, source_target_pairs={{2,0},{6,1},{3,2},{7,3},{0,4},{4,5},{1,6},{5,7},{10,8},{14,9},{11,... | collective-permute-start | bytes 196616 | tf_op jit(solution)/shard_map/ppermute | solution.py:311
  643.1 8.3 %collective-permute-start.24 = (bf16[2,64,256]{2,1,0:T(8,128)(2,1)S(1)}, bf16[2,64,256]{2,1,0:T(8,128)(2,1)S(1)}, u32[]{:S(2)}, u32[]{:S(2)}) collective-permute-start(bf16[2,64,256]{2,1,0:T(8,128)(2,1)S(1)} %get-tuple-element.145), channel_id=1, source_target_pairs={{3,0},{7,1},{0,2},{4,3},{1,4},{5,5},{2,6},{6,7},{11,8},{15,9},{8,1... | collective-permute-start | bytes 196616 | tf_op jit(solution)/shard_map/ppermute | solution.py:311
  652.3 9.9 %all-to-all-start.24 = ((bf16[8,2,4,1024]{3,2,1,0:T(4,128)(2,1)}), bf16[8,2,4,1024]{3,2,1,0:T(4,128)(2,1)S(1)}, u32[]{:S(2)}, u32[]{:S(2)}) async-start(bf16[8,2,4,1024]{3,2,1,0:T(4,128)(2,1)} %maximum_bitcast_fusion.1), calls=%async_computation.24 | async-start | bytes 262144 | tf_op jit(solution)/shard_map/all_to_all | solution.py:265
  (18 other events, 23.6 us)
Sparse Core Ops, SparseCore 0:
  9.9 43.6 all-gather.5
  88.7 40.3 all-gather.3
  275.5 59.2 all-gather.7

commit v3 on v2

--- a/solution.py
+++ b/solution.py
@@ -347,17 +347,19 @@
 
     for step in range(S + slots - 1):
         parts, hq = query(step, ints, text_f, gain_f, h, wq_f)
+        if step == 0:
+            across = [dp_flip(own, 2) for own in (wo_a, wo_b)]
+            parts = after(parts, across[0])
         swapped = swap(parts, "tensor")
         p, kept_qn = attend(step, ints, alpha, width, query_norm_gain, keys, swapped, kept_qn)
         if step == 0:
             vals16 = vals.astype(jnp.bfloat16).reshape(slots * toks, hd)
             vals16 = jnp.broadcast_to(vals16[None], (T,) + vals16.shape)
-            both = swap(jnp.concatenate([p, vals16], axis=1), "tensor")
+            both = swap(jnp.concatenate([after(p, across[1]), vals16], axis=1), "tensor")
             probs = both[:, :rows]
             wo_f = []
-            for own in (wo_a, wo_b):
-                across = dp_flip(own, 2)
-                wo_f += [own, dp_flip(own, 1), across, dp_flip(after(across, probs), 1)]
+            for own, far in zip((wo_a, wo_b), across):
+                wo_f += [own, dp_flip(own, 1), far, dp_flip(far, 1)]
             vo = value_out(both[:, rows:], wo_f, slots)
         else:
             probs = swap(after(p, *grads), "tensor")

time: 681 us -> 659 us (0.968)
  waiting for transfers between devices: 216 us -> 187 us
  blocking collectives: 179 us -> 192 us
    ppermute x9, waiting for transfers between devices: 53.3 us -> 0.02 us  [dp_flip(): return lax.ppermute(x, 'dp', [(i, i ^ m) for i in range(D)])]
    all_gather x1, waiting for transfers between devices: 0.27 us -> 31.5 us  [per_device(): img = lax.all_gather(img, 'tensor', axis=1, tiled=True)]
    all_to_all x12 -> x13, blocking collectives: 179 us -> 192 us  [swap(): return lax.all_to_all(x, axis, 0, 0, tiled=True)]
    all_to_all x13 -> x12, starting transfers between devices: 73.6 us -> 67.1 us  [swap(): return lax.all_to_all(x, axis, 0, 0, tiled=True)]
    all_to_all x13 -> x12, waiting for transfers between devices: 68.3 us -> 63.7 us  [swap(): return lax.all_to_all(x, axis, 0, 0, tiled=True)]
    unnamed x84 -> x80, local copies, waits for them, and re-layouts: 27 us -> 26.2 us
  transfers between devices with their start and end apart: 41 -> 40, of which waited for: 27 -> 23; matrix products, arithmetic and copies ran while one was open for 6% -> 6% of each run, Pallas kernels for 8% -> 8%
where the time goes in v3:
time: 659 us; the launch traced here: 648 us
  blocking collectives  192 us (29%)
  waiting for transfers between devices  187 us (28%)
  starting transfers between devices  105 us (16%)
  Pallas kernels  82.5 us (13%)
  local copies, waits for them, and re-layouts  39 us (6%)
  between operations  19.9 us (3%)
  other arithmetic  12.6 us (2%)
  matrix products  10.3 us (2%)
    all_to_all x13, blocking collectives, swap(): return lax.all_to_all(x, axis, 0, 0, tiled=True)  192 us
    all_to_all x12, starting transfers between devices, swap(): return lax.all_to_all(x, axis, 0, 0, tiled=True)  67.1 us
    all_to_all x12, waiting for transfers between devices, swap(): return lax.all_to_all(x, axis, 0, 0, tiled=True)  63.7 us
    ppermute x8, waiting for transfers between devices, onward(): return lax.ppermute(x, 'section', [(i, (i + 1) % S) for i in range(S)])  56.9 us
    pallas_call x9, Pallas kernels, query(): pl.pallas_call(functools.partial(query_kernel, step), in_specs=[pl.BlockS...  45.4 us
    ppermute x4, waiting for transfers between devices, spread(): got.append(lax.ppermute(pick(parts, (a + k) % D), 'tensor', pairs))  32.9 us
    all_gather x1, waiting for transfers between devices, per_device(): img = lax.all_gather(img, 'tensor', axis=1, tiled=True)  31.5 us
    unnamed x80, local copies, waits for them, and re-layouts  26.2 us
  transfers between devices with their start and end apart: 40, of which 23 were waited for; matrix products, arithmetic and copies ran while one was open for 6% of the time, Pallas kernels for 8%

profile of v3, /device:TPU:32, one launch (start us, length us, event | category | flops | bytes accessed | tf_op | source)
XLA Modules:
  0.0 647.9 jit_solution(12925070586963633321)
XLA Ops:
  11.1 11.9 %all_to_all.125 = bf16[8,8,1024]{2,1,0:T(8,128)(2,1)} all-to-all(bf16[8,8,1024]{2,1,0:T(8,128)(2,1)S(1)} %broadcast_in_dim.53), channel_id=1, replica_groups=mesh['dp'=4,'section'=8,'tensor'=8] {'section'}, dimensions={0} | all-to-all | bytes 262144 | tf_op jit(solution)/shard_map/all_to_all | solution.py:265
  23.0 8.7 %all-to-all-start.1 = ((bf16[8,256,512]{2,1,0:T(8,128)(2,1)}), bf16[8,256,512]{2,1,0:T(8,128)(2,1)}, u32[]{:S(2)}, u32[]{:S(2)}) async-start(bf16[8,256,512]{2,1,0:T(8,128)(2,1)} %bitcast.112), calls=%async_computation.1 | async-start | bytes 4194304 | tf_op jit(solution)/shard_map/all_to_all | solution.py:265
  32.5 6.4 collective-permute-start
  44.9 3.9 copy.20
  48.9 3.9 copy.21
  52.8 24.9 %collective-permute-done = bf16[2,64,256]{2,1,0:T(8,128)(2,1)S(1)} collective-permute-done((bf16[2,64,256]{2,1,0:T(8,128)(2,1)S(1)}, bf16[2,64,256]{2,1,0:T(8,128)(2,1)S(1)}, u32[]{:S(2)}, u32[]{:S(2)}) %collective-permute-start) | collective-permute-done | bytes 65568 | tf_op jit(solution)/shard_map/ppermute | solution.py:301
  77.7 3.0 collective-permute-done.1
  80.7 4.8 collective-permute-done.2
  85.8 2.8 collective-permute-start.5
  88.6 3.1 fusion.1
  91.7 4.9 all-to-all-start.2
  96.6 31.5 %all-gather.4.cloned.1.call-done = bf16[64,8192]{1,0:T(8,128)(2,1)} async-done(((bf16[64,1024]{1,0:T(8,128)(2,1)}), bf16[64,8192]{1,0:T(8,128)(2,1)}) %all-gather.4.cloned.1.call-update) | async-done | bytes 1048592 | tf_op jit(solution)/shard_map/all_gather | solution.py:327
  128.1 2.9 all-to-all-done.2.refs_0_
  131.0 5.6 all-to-all-start.4
  137.9 23.6 %all-to-all-done.4.refs_4_ = bf16[8,256,256]{2,1,0:T(8,128)(2,1)} async-done(((bf16[8,256,256]{2,1,0:T(8,128)(2,1)}), bf16[8,256,256]{2,1,0:T(8,128)(2,1)}, u32[]{:S(2)}, u32[]{:S(2)}) %all-to-all-start.4) | async-done | bytes 1048608 | tf_op jit(solution)/shard_map/all_to_all | solution.py:265
  165.9 4.9 shard_map.140
  172.2 5.6 all-to-all-start.3
  177.9 3.9 fusion.4
  188.4 6.5 %all-to-all-done.3.q_ref = bf16[8,272,128]{2,1,0:T(8,128)(2,1)} async-done(((bf16[8,272,128]{2,1,0:T(8,128)(2,1)}), bf16[8,272,128]{2,1,0:T(8,128)(2,1)}, u32[]{:S(2)}, u32[]{:S(2)}) %all-to-all-start.3) | async-done | bytes 557088 | tf_op jit(solution)/shard_map/all_to_all | solution.py:265
  196.7 14.7 %all_to_all.126 = bf16[8,128,128]{2,1,0:T(8,128)(2,1)S(1)} all-to-all(bf16[8,128,128]{2,1,0:T(8,128)(2,1)S(1)} %pad_maximum_fusion.4), channel_id=1, replica_groups=mesh['dp'=4,'section'=8,'tensor'=8] {'tensor'}, dimensions={0} | all-to-all | bytes 524288 | tf_op jit(solution)/shard_map/all_to_all | solution.py:265
  211.5 5.5 shard_map.142.vo_ref
  221.4 4.8 collective-permute-done.13.refs_0_
  226.2 4.9 shard_map.144
  231.1 20.2 %all_to_all.127.q_ref = bf16[8,272,128]{2,1,0:T(8,128)(2,1)S(1)} all-to-all(bf16[8,272,128]{2,1,0:T(8,128)(2,1)S(1)} %get-tuple-element.81), channel_id=1, replica_groups=mesh['dp'=4,'section'=8,'tensor'=8] {'tensor'}, dimensions={0} | all-to-all | bytes 1114112 | tf_op jit(solution)/shard_map/all_to_all | solution.py:265
  252.6 11.5 %all_to_all.128.p_ref = bf16[8,64,128]{2,1,0:T(8,128)(2,1)S(1)} all-to-all(bf16[8,64,128]{2,1,0:T(8,128)(2,1)S(1)} %get-tuple-element.83), channel_id=1, replica_groups=mesh['dp'=4,'section'=8,'tensor'=8] {'tensor'}, dimensions={0} | all-to-all | bytes 262144 | tf_op jit(solution)/shard_map/all_to_all | solution.py:265
  267.9 9.7 %collective-permute-done.14.refs_0_ = bf16[64,1024]{1,0:T(8,128)(2,1)S(1)} collective-permute-done((bf16[64,1024]{1,0:T(8,128)(2,1)S(1)}, bf16[64,1024]{1,0:T(8,128)(2,1)S(1)}, u32[]{:S(2)}, u32[]{:S(2)}) %collective-permute-start.14) | collective-permute-done | bytes 131104 | tf_op jit(solution)/shard_map/ppermute | solution.py:286
  277.6 5.2 shard_map.147
  282.8 18.1 %all_to_all.129.q_ref = bf16[8,272,128]{2,1,0:T(8,128)(2,1)S(1)} all-to-all(bf16[8,272,128]{2,1,0:T(8,128)(2,1)S(1)} %get-tuple-element.87), channel_id=1, replica_groups=mesh['dp'=4,'section'=8,'tensor'=8] {'tensor'}, dimensions={0} | all-to-all | bytes 1114112 | tf_op jit(solution)/shard_map/all_to_all | solution.py:265
  302.1 11.5 %all_to_all.130.p_ref = bf16[8,64,128]{2,1,0:T(8,128)(2,1)S(1)} all-to-all(bf16[8,64,128]{2,1,0:T(8,128)(2,1)S(1)} %get-tuple-element.89), channel_id=1, replica_groups=mesh['dp'=4,'section'=8,'tensor'=8] {'tensor'}, dimensions={0} | all-to-all | bytes 262144 | tf_op jit(solution)/shard_map/all_to_all | solution.py:265
  314.7 7.1 %collective-permute-done.15.refs_0_ = bf16[64,1024]{1,0:T(8,128)(2,1)S(1)} collective-permute-done((bf16[64,1024]{1,0:T(8,128)(2,1)S(1)}, bf16[64,1024]{1,0:T(8,128)(2,1)S(1)}, u32[]{:S(2)}, u32[]{:S(2)}) %collective-permute-start.15) | collective-permute-done | bytes 131104 | tf_op jit(solution)/shard_map/ppermute | solution.py:286
  321.7 4.9 shard_map.150
  326.7 16.4 %all_to_all.131.q_ref = bf16[8,272,128]{2,1,0:T(8,128)(2,1)S(1)} all-to-all(bf16[8,272,128]{2,1,0:T(8,128)(2,1)S(1)} %get-tuple-element.93), channel_id=1, replica_groups=mesh['dp'=4,'section'=8,'tensor'=8] {'tensor'}, dimensions={0} | all-to-all | bytes 1114112 | tf_op jit(solution)/shard_map/all_to_all | solution.py:265
  344.3 11.5 %all_to_all.132.p_ref = bf16[8,64,128]{2,1,0:T(8,128)(2,1)S(1)} all-to-all(bf16[8,64,128]{2,1,0:T(8,128)(2,1)S(1)} %get-tuple-element.95), channel_id=1, replica_groups=mesh['dp'=4,'section'=8,'tensor'=8] {'tensor'}, dimensions={0} | all-to-all | bytes 262144 | tf_op jit(solution)/shard_map/all_to_all | solution.py:265
  357.0 7.1 %collective-permute-done.16.refs_0_ = bf16[64,1024]{1,0:T(8,128)(2,1)S(1)} collective-permute-done((bf16[64,1024]{1,0:T(8,128)(2,1)S(1)}, bf16[64,1024]{1,0:T(8,128)(2,1)S(1)}, u32[]{:S(2)}, u32[]{:S(2)}) %collective-permute-start.16) | collective-permute-done | bytes 131104 | tf_op jit(solution)/shard_map/ppermute | solution.py:286
  364.0 4.9 shard_map.153
  368.9 16.0 %all_to_all.133.q_ref = bf16[8,272,128]{2,1,0:T(8,128)(2,1)S(1)} all-to-all(bf16[8,272,128]{2,1,0:T(8,128)(2,1)S(1)} %get-tuple-element.99), channel_id=1, replica_groups=mesh['dp'=4,'section'=8,'tensor'=8] {'tensor'}, dimensions={0} | all-to-all | bytes 1114112 | tf_op jit(solution)/shard_map/all_to_all | solution.py:265
  386.2 11.6 %all_to_all.134.p_ref = bf16[8,64,128]{2,1,0:T(8,128)(2,1)S(1)} all-to-all(bf16[8,64,128]{2,1,0:T(8,128)(2,1)S(1)} %get-tuple-element.101), channel_id=1, replica_groups=mesh['dp'=4,'section'=8,'tensor'=8] {'tensor'}, dimensions={0} | all-to-all | bytes 262144 | tf_op jit(solution)/shard_map/all_to_all | solution.py:265
  399.1 7.1 %collective-permute-done.17.refs_0_ = bf16[64,1024]{1,0:T(8,128)(2,1)S(1)} collective-permute-done((bf16[64,1024]{1,0:T(8,128)(2,1)S(1)}, bf16[64,1024]{1,0:T(8,128)(2,1)S(1)}, u32[]{:S(2)}, u32[]{:S(2)}) %collective-permute-start.17) | collective-permute-done | bytes 131104 | tf_op jit(solution)/shard_map/ppermute | solution.py:286
  406.2 5.7 shard_map.156
  412.6 4.9 all-to-all-start.14
  418.7 11.1 %all-to-all-done.14.q_ref = bf16[8,272,128]{2,1,0:T(8,128)(2,1)S(1)} async-done(((bf16[8,272,128]{2,1,0:T(8,128)(2,1)}), bf16[8,272,128]{2,1,0:T(8,128)(2,1)S(1)}, u32[]{:S(2)}, u32[]{:S(2)}) %all-to-all-start.14) | async-done | bytes 557088 | tf_op jit(solution)/shard_map/all_to_all | solution.py:265
  433.3 4.6 all-to-all-start.15
  438.0 6.3 fusion.5
  449.0 7.1 %collective-permute-done.18.refs_0_ = bf16[64,1024]{1,0:T(8,128)(2,1)S(1)} collective-permute-done((bf16[64,1024]{1,0:T(8,128)(2,1)S(1)}, bf16[64,1024]{1,0:T(8,128)(2,1)S(1)}, u32[]{:S(2)}, u32[]{:S(2)}) %collective-permute-start.18) | collective-permute-done | bytes 131104 | tf_op jit(solution)/shard_map/ppermute | solution.py:286
  456.0 5.2 shard_map.159
  461.2 19.5 %all_to_all.135.q_ref = bf16[8,272,128]{2,1,0:T(8,128)(2,1)S(1)} all-to-all(bf16[8,272,128]{2,1,0:T(8,128)(2,1)S(1)} %get-tuple-element.113), channel_id=1, replica_groups=mesh['dp'=4,'section'=8,'tensor'=8] {'tensor'}, dimensions={0} | all-to-all | bytes 1114112 | tf_op jit(solution)/shard_map/all_to_all | solution.py:265
  481.9 11.5 %all_to_all.136.p_ref = bf16[8,64,128]{2,1,0:T(8,128)(2,1)S(1)} all-to-all(bf16[8,64,128]{2,1,0:T(8,128)(2,1)S(1)} %get-tuple-element.115), channel_id=1, replica_groups=mesh['dp'=4,'section'=8,'tensor'=8] {'tensor'}, dimensions={0} | all-to-all | bytes 262144 | tf_op jit(solution)/shard_map/all_to_all | solution.py:265
  494.5 7.1 %collective-permute-done.19.refs_0_ = bf16[64,1024]{1,0:T(8,128)(2,1)S(1)} collective-permute-done((bf16[64,1024]{1,0:T(8,128)(2,1)S(1)}, bf16[64,1024]{1,0:T(8,128)(2,1)S(1)}, u32[]{:S(2)}, u32[]{:S(2)}) %collective-permute-start.19) | collective-permute-done | bytes 131104 | tf_op jit(solution)/shard_map/ppermute | solution.py:286
  501.6 4.9 shard_map.162
  506.5 17.4 %all_to_all.137.q_ref = bf16[8,272,128]{2,1,0:T(8,128)(2,1)S(1)} all-to-all(bf16[8,272,128]{2,1,0:T(8,128)(2,1)S(1)} %get-tuple-element.119), channel_id=1, replica_groups=mesh['dp'=4,'section'=8,'tensor'=8] {'tensor'}, dimensions={0} | all-to-all | bytes 1114112 | tf_op jit(solution)/shard_map/all_to_all | solution.py:265
  525.8 4.7 all-to-all-start.19
  532.7 4.0 shard_map.167
  538.2 5.7 all-to-all-start.21
  548.1 7.1 %collective-permute-done.20.refs_0_ = bf16[64,1024]{1,0:T(8,128)(2,1)S(1)} collective-permute-done((bf16[64,1024]{1,0:T(8,128)(2,1)S(1)}, bf16[64,1024]{1,0:T(8,128)(2,1)S(1)}, u32[]{:S(2)}, u32[]{:S(2)}) %collective-permute-start.20) | collective-permute-done | bytes 131104 | tf_op jit(solution)/shard_map/ppermute | solution.py:286
  555.2 4.9 shard_map.165
  561.6 7.2 %all-to-all-start.20 = ((bf16[8,272,128]{2,1,0:T(8,128)(2,1)}), bf16[8,272,128]{2,1,0:T(8,128)(2,1)S(1)}, u32[]{:S(2)}, u32[]{:S(2)}) async-start(bf16[8,272,128]{2,1,0:T(8,128)(2,1)} %copy-done.11), calls=%async_computation.20 | async-start | bytes 1114112 | tf_op jit(solution)/shard_map/all_to_all | solution.py:265
  570.5 11.0 %all-to-all-done.20.q_ref = bf16[8,272,128]{2,1,0:T(8,128)(2,1)S(1)} async-done(((bf16[8,272,128]{2,1,0:T(8,128)(2,1)}), bf16[8,272,128]{2,1,0:T(8,128)(2,1)S(1)}, u32[]{:S(2)}, u32[]{:S(2)}) %all-to-all-start.20) | async-done | bytes 557088 | tf_op jit(solution)/shard_map/all_to_all | solution.py:265
  584.1 4.7 all-to-all-start.22
  593.4 4.0 shard_map.169
  597.5 7.0 %all-to-all-start.23 = ((bf16[8,32,1024]{2,1,0:T(8,128)(2,1)}), bf16[8,32,1024]{2,1,0:T(8,128)(2,1)S(1)}, u32[]{:S(2)}, u32[]{:S(2)}) async-start(bf16[8,32,1024]{2,1,0:T(8,128)(2,1)} %shard_map.169), calls=%async_computation.23 | async-start | bytes 1048576 | tf_op jit(solution)/shard_map/all_to_all | solution.py:265
  608.6 3.4 collective-permute-start.21
  613.9 7.2 %collective-permute-start.23 = (bf16[2,64,256]{2,1,0:T(8,128)(2,1)S(1)}, bf16[2,64,256]{2,1,0:T(8,128)(2,1)S(1)}, u32[]{:S(2)}, u32[]{:S(2)}) collective-permute-start(bf16[2,64,256]{2,1,0:T(8,128)(2,1)S(1)} %get-tuple-element.146), channel_id=1, source_target_pairs={{2,0},{6,1},{3,2},{7,3},{0,4},{4,5},{1,6},{5,7},{10,8},{14,9},{11,... | collective-permute-start | bytes 196616 | tf_op jit(solution)/shard_map/ppermute | solution.py:311
  630.3 3.4 all-to-all-start.24
  634.4 5.8 all-to-all-done.24
  (196 shorter events, 87.3 us)
Async XLA Ops:
  7.2 430.8 %copy-start = (bf16[1,2,64,8192]{3,2,1,0:T(8,128)(2,1)S(1)}, bf16[1,2,64,8192]{3,2,1,0:T(8,128)(2,1)}, u32[]{:S(2)}) copy-start(bf16[1,2,64,8192]{3,2,1,0:T(8,128)(2,1)} %param.25) | copy-start | bytes 6291460
  7.2 2.5 copy-start.37
  7.2 2.5 copy-start.30
  7.2 3.2 copy-start.34
  7.2 81.4 %all-gather.6.cloned.1.call-start = ((), (), s32[]{:S(2)}) async-start(), calls=%async_computation.26 | async-start | bytes 5242880 | tf_op jit(solution)/shard_map/all_gather | solution.py:321
  11.0 154.8 %copy-start.36 = (s32[2]{0:T(128)}, s32[2]{0:T(128)S(1)}, u32[]{:S(2)}) copy-start(s32[2]{0:T(128)S(1)} %get-tuple-element.136) | copy-start | bytes 28
  23.0 8.7 %copy-start.31 = (bf16[2,64,1024]{2,1,0:T(8,128)(2,1)S(1)}, bf16[2,64,1024]{2,1,0:T(8,128)(2,1)}, u32[]{:S(2)}) copy-start(bf16[2,64,1024]{2,1,0:T(8,128)(2,1)} %param.13) | copy-start | bytes 786436
  23.0 62.8 %all-to-all-start.1 = ((bf16[8,256,512]{2,1,0:T(8,128)(2,1)}), bf16[8,256,512]{2,1,0:T(8,128)(2,1)}, u32[]{:S(2)}, u32[]{:S(2)}) async-start(bf16[8,256,512]{2,1,0:T(8,128)(2,1)} %bitcast.112), calls=%async_computation.1 | async-start | bytes 4194304 | tf_op jit(solution)/shard_map/all_to_all | solution.py:265
  31.7 96.4 %all-gather.4.cloned.1.call-start = ((), (), s32[]{:S(2)}) async-start(), calls=%async_computation.25 | async-start | bytes 1179648 | tf_op jit(solution)/shard_map/all_gather | solution.py:327
  32.5 45.2 %collective-permute-start = (bf16[2,64,256]{2,1,0:T(8,128)(2,1)S(1)}, bf16[2,64,256]{2,1,0:T(8,128)(2,1)S(1)}, u32[]{:S(2)}, u32[]{:S(2)}) collective-permute-start(bf16[2,64,256]{2,1,0:T(8,128)(2,1)S(1)} %get-tuple-element.158), channel_id=1, source_target_pairs={{0,0},{1,4},{2,1},{3,5},{4,2},{5,6},{6,3},{7,7},{8,8},{9,12},{10,9... | collective-permute-start | bytes 196616 | tf_op jit(solution)/shard_map/ppermute | solution.py:301
  38.9 41.8 %collective-permute-start.1 = (bf16[2,64,256]{2,1,0:T(8,128)(2,1)S(1)}, bf16[2,64,256]{2,1,0:T(8,128)(2,1)S(1)}, u32[]{:S(2)}, u32[]{:S(2)}) collective-permute-start(bf16[2,64,256]{2,1,0:T(8,128)(2,1)S(1)} %get-tuple-element.161), channel_id=1, source_target_pairs={{0,1},{1,5},{2,2},{3,6},{4,3},{5,7},{6,0},{7,4},{8,9},{9,13},{10,1... | collective-permute-start | bytes 196616 | tf_op jit(solution)/shard_map/ppermute | solution.py:301
  41.4 44.2 %collective-permute-start.2 = (bf16[2,64,256]{2,1,0:T(8,128)(2,1)S(1)}, bf16[2,64,256]{2,1,0:T(8,128)(2,1)S(1)}, u32[]{:S(2)}, u32[]{:S(2)}) collective-permute-start(bf16[2,64,256]{2,1,0:T(8,128)(2,1)S(1)} %get-tuple-element.160), channel_id=1, source_target_pairs={{0,2},{1,6},{2,3},{3,7},{4,0},{5,4},{6,1},{7,5},{8,10},{9,14},{10,... | collective-permute-start | bytes 196616 | tf_op jit(solution)/shard_map/ppermute | solution.py:301
  42.4 43.3 %collective-permute-start.3 = (bf16[2,64,256]{2,1,0:T(8,128)(2,1)S(1)}, bf16[2,64,256]{2,1,0:T(8,128)(2,1)S(1)}, u32[]{:S(2)}, u32[]{:S(2)}) collective-permute-start(bf16[2,64,256]{2,1,0:T(8,128)(2,1)S(1)} %get-tuple-element.159), channel_id=1, source_target_pairs={{0,3},{1,7},{2,0},{3,4},{4,1},{5,5},{6,2},{7,6},{8,11},{9,15},{10,... | collective-permute-start | bytes 196616 | tf_op jit(solution)/shard_map/ppermute | solution.py:301
  85.8 50.8 %collective-permute-start.5 = (bf16[8,256,512]{2,1,0:T(8,128)(2,1)}, bf16[8,256,512]{2,1,0:T(8,128)(2,1)}, u32[]{:S(2)}, u32[]{:S(2)}) collective-permute-start(bf16[8,256,512]{2,1,0:T(8,128)(2,1)} %all-to-all-done.1.refs_0_.refs_1_), channel_id=1, source_target_pairs={{0,128},{64,192},{128,0},{192,64},{1,129},{65,193},{129,1},{193,65... | collective-permute-start | bytes 6291464 | tf_op jit(solution)/shard_map/ppermute | solution.py:289
  91.7 72.7 %copy-start.33 = (f32[1,8192]{1,0:T(1,128)S(1)}, f32[1,8192]{1,0:T(1,128)}, u32[]{:S(2)}) copy-start(f32[1,8192]{1,0:T(1,128)} %param.17) | copy-start | bytes 98308
  91.7 39.3 %all-to-all-start.2 = ((bf16[8,256,256]{2,1,0:T(8,128)(2,1)}), bf16[8,256,256]{2,1,0:T(8,128)(2,1)S(1)}, u32[]{:S(2)}, u32[]{:S(2)}) async-start(bf16[8,256,256]{2,1,0:T(8,128)(2,1)} %get-tuple-element.139), calls=%async_computation.2 | async-start | bytes 2097152 | tf_op jit(solution)/shard_map/all_to_all | solution.py:265
  131.0 30.6 %all-to-all-start.4 = ((bf16[8,256,256]{2,1,0:T(8,128)(2,1)}), bf16[8,256,256]{2,1,0:T(8,128)(2,1)}, u32[]{:S(2)}, u32[]{:S(2)}) async-start(bf16[8,256,256]{2,1,0:T(8,128)(2,1)} %get-tuple-element.77), calls=%async_computation.4 | async-start | bytes 2097152 | tf_op jit(solution)/shard_map/all_to_all | solution.py:265
  136.5 29.3 %collective-permute-start.4 = (bf16[8,256,512]{2,1,0:T(8,128)(2,1)}, bf16[8,256,512]{2,1,0:T(8,128)(2,1)}, u32[]{:S(2)}, u32[]{:S(2)}) collective-permute-start(bf16[8,256,512]{2,1,0:T(8,128)(2,1)} %all-to-all-done.1.refs_0_.refs_1_), channel_id=1, source_target_pairs={{0,64},{64,0},{128,192},{192,128},{1,65},{65,1},{129,193},{193,129... | collective-permute-start | bytes 6291464 | tf_op jit(solution)/shard_map/ppermute | solution.py:289
  136.5 29.3 %collective-permute-start.6 = (bf16[8,256,512]{2,1,0:T(8,128)(2,1)}, bf16[8,256,512]{2,1,0:T(8,128)(2,1)}, u32[]{:S(2)}, u32[]{:S(2)}) collective-permute-start(bf16[8,256,512]{2,1,0:T(8,128)(2,1)} %collective-permute-done.5.refs_2_.refs_3_), channel_id=1, source_target_pairs={{0,64},{64,0},{128,192},{192,128},{1,65},{65,1},{129,193},{193,129... | collective-permute-start | bytes 6291464 | tf_op jit(solution)/shard_map/ppermute | solution.py:289
  137.0 35.2 %collective-permute-start.7 = (bf16[8,256,256]{2,1,0:T(8,128)(2,1)S(1)}, bf16[8,256,256]{2,1,0:T(8,128)(2,1)}, u32[]{:S(2)}, u32[]{:S(2)}) collective-permute-start(bf16[8,256,256]{2,1,0:T(8,128)(2,1)S(1)} %all-to-all-done.2.refs_0_), channel_id=1, source_target_pairs={{0,128},{64,192},{128,0},{192,64},{1,129},{65,193},{129,1},{193,65... | collective-permute-start | bytes 3145736 | tf_op jit(solution)/shard_map/ppermute | solution.py:289
  161.5 24.8 %collective-permute-start.8 = (bf16[8,256,256]{2,1,0:T(8,128)(2,1)}, bf16[8,256,256]{2,1,0:T(8,128)(2,1)}, u32[]{:S(2)}, u32[]{:S(2)}) collective-permute-start(bf16[8,256,256]{2,1,0:T(8,128)(2,1)} %all-to-all-done.4.refs_4_), channel_id=1, source_target_pairs={{0,128},{64,192},{128,0},{192,64},{1,129},{65,193},{129,1},{193,65... | collective-permute-start | bytes 3145736 | tf_op jit(solution)/shard_map/ppermute | solution.py:289
  172.2 22.6 %all-to-all-start.3 = ((bf16[8,272,128]{2,1,0:T(8,128)(2,1)}), bf16[8,272,128]{2,1,0:T(8,128)(2,1)}, u32[]{:S(2)}, u32[]{:S(2)}) async-start(bf16[8,272,128]{2,1,0:T(8,128)(2,1)} %copy-done.10), calls=%async_computation.3 | async-start | bytes 1114112 | tf_op jit(solution)/shard_map/all_to_all | solution.py:265
  177.8 9.7 %copy-start.29 = (f32[1,128]{1,0:T(1,128)S(1)}, f32[1,128]{1,0:T(1,128)}, u32[]{:S(2)}) copy-start(f32[1,128]{1,0:T(1,128)} %gain_ref.21) | copy-start | bytes 1540
  177.8 17.1 %copy-start.28 = (f32[1,128]{1,0:T(1,128)S(1)}, f32[1,128]{1,0:T(1,128)}, u32[]{:S(2)}) copy-start(f32[1,128]{1,0:T(1,128)} %gain_ref.19) | copy-start | bytes 1540
  177.8 260.1 %all-gather.8.cloned.1.call-start = ((), (), s32[]{:S(2)}) async-start(), calls=%async_computation.27 | async-start | bytes 10485760 | tf_op jit(solution)/shard_map/all_gather | solution.py:367
  185.6 25.8 %collective-permute-start.9 = (bf16[8,256,256]{2,1,0:T(8,128)(2,1)S(1)}, bf16[8,256,256]{2,1,0:T(8,128)(2,1)}, u32[]{:S(2)}, u32[]{:S(2)}) collective-permute-start(bf16[8,256,256]{2,1,0:T(8,128)(2,1)S(1)} %all-to-all-done.2.refs_0_), channel_id=1, source_target_pairs={{0,64},{64,0},{128,192},{192,128},{1,65},{65,1},{129,193},{193,129... | collective-permute-start | bytes 3145736 | tf_op jit(solution)/shard_map/ppermute | solution.py:289
  185.7 25.7 %collective-permute-start.10 = (bf16[8,256,256]{2,1,0:T(8,128)(2,1)}, bf16[8,256,256]{2,1,0:T(8,128)(2,1)}, u32[]{:S(2)}, u32[]{:S(2)}) collective-permute-start(bf16[8,256,256]{2,1,0:T(8,128)(2,1)} %collective-permute-done.7.refs_2_), channel_id=1, source_target_pairs={{0,64},{64,0},{128,192},{192,128},{1,65},{65,1},{129,193},{193,129... | collective-permute-start | bytes 3145736 | tf_op jit(solution)/shard_map/ppermute | solution.py:289
  186.2 25.2 %collective-permute-start.11 = (bf16[8,256,256]{2,1,0:T(8,128)(2,1)}, bf16[8,256,256]{2,1,0:T(8,128)(2,1)}, u32[]{:S(2)}, u32[]{:S(2)}) collective-permute-start(bf16[8,256,256]{2,1,0:T(8,128)(2,1)} %all-to-all-done.4.refs_4_), channel_id=1, source_target_pairs={{0,64},{64,0},{128,192},{192,128},{1,65},{65,1},{129,193},{193,129... | collective-permute-start | bytes 3145736 | tf_op jit(solution)/shard_map/ppermute | solution.py:289
  186.3 25.1 %collective-permute-start.12 = (bf16[8,256,256]{2,1,0:T(8,128)(2,1)}, bf16[8,256,256]{2,1,0:T(8,128)(2,1)}, u32[]{:S(2)}, u32[]{:S(2)}) collective-permute-start(bf16[8,256,256]{2,1,0:T(8,128)(2,1)} %collective-permute-done.8.refs_6_), channel_id=1, source_target_pairs={{0,64},{64,0},{128,192},{192,128},{1,65},{65,1},{129,193},{193,129... | collective-permute-start | bytes 3145736 | tf_op jit(solution)/shard_map/ppermute | solution.py:289
  211.5 5.5 copy-start.23
  219.0 7.2 %collective-permute-start.13 = (bf16[64,1024]{1,0:T(8,128)(2,1)S(1)}, bf16[64,1024]{1,0:T(8,128)(2,1)S(1)}, u32[]{:S(2)}, u32[]{:S(2)}) collective-permute-start(bf16[64,1024]{1,0:T(8,128)(2,1)S(1)} %get-tuple-element.80), channel_id=1, source_target_pairs={{0,8},{8,16},{16,24},{24,32},{32,40},{40,48},{48,56},{56,0},{1,9},... | collective-permute-start | bytes 393224 | tf_op jit(solution)/shard_map/ppermute | solution.py:286
  264.1 2.3 copy-start.2
  267.4 10.2 %collective-permute-start.14 = (bf16[64,1024]{1,0:T(8,128)(2,1)S(1)}, bf16[64,1024]{1,0:T(8,128)(2,1)S(1)}, u32[]{:S(2)}, u32[]{:S(2)}) collective-permute-start(bf16[64,1024]{1,0:T(8,128)(2,1)S(1)} %get-tuple-element.86), channel_id=1, source_target_pairs={{0,8},{8,16},{16,24},{24,32},{32,40},{40,48},{48,56},{56,0},{1,9},... | collective-permute-start | bytes 393224 | tf_op jit(solution)/shard_map/ppermute | solution.py:286
  277.6 35.9 %copy-start.3 = (bf16[2,1024,1024]{2,1,0:T(8,128)(2,1)S(1)}, bf16[2,1024,1024]{2,1,0:T(8,128)(2,1)}, u32[]{:S(2)}) copy-start(bf16[2,1024,1024]{2,1,0:T(8,128)(2,1)} %copy-done.1) | copy-start | bytes 12582916
  314.6 7.2 %collective-permute-start.15 = (bf16[64,1024]{1,0:T(8,128)(2,1)S(1)}, bf16[64,1024]{1,0:T(8,128)(2,1)S(1)}, u32[]{:S(2)}, u32[]{:S(2)}) collective-permute-start(bf16[64,1024]{1,0:T(8,128)(2,1)S(1)} %get-tuple-element.92), channel_id=1, source_target_pairs={{0,8},{8,16},{16,24},{24,32},{32,40},{40,48},{48,56},{56,0},{1,9},... | collective-permute-start | bytes 393224 | tf_op jit(solution)/shard_map/ppermute | solution.py:286
  356.9 7.2 %collective-permute-start.16 = (bf16[64,1024]{1,0:T(8,128)(2,1)S(1)}, bf16[64,1024]{1,0:T(8,128)(2,1)S(1)}, u32[]{:S(2)}, u32[]{:S(2)}) collective-permute-start(bf16[64,1024]{1,0:T(8,128)(2,1)S(1)} %get-tuple-element.98), channel_id=1, source_target_pairs={{0,8},{8,16},{16,24},{24,32},{32,40},{40,48},{48,56},{56,0},{1,9},... | collective-permute-start | bytes 393224 | tf_op jit(solution)/shard_map/ppermute | solution.py:286
  386.2 11.6 %copy-start.18 = (f32[2,64,512]{2,1,0:T(8,128)}, f32[2,64,512]{2,1,0:T(8,128)S(1)}, u32[]{:S(2)}) copy-start(f32[2,64,512]{2,1,0:T(8,128)S(1)} %get-tuple-element.106.refs_0_) | copy-start | bytes 786436
  398.8 7.4 %collective-permute-start.17 = (bf16[64,1024]{1,0:T(8,128)(2,1)S(1)}, bf16[64,1024]{1,0:T(8,128)(2,1)S(1)}, u32[]{:S(2)}, u32[]{:S(2)}) collective-permute-start(bf16[64,1024]{1,0:T(8,128)(2,1)S(1)} %get-tuple-element.104), channel_id=1, source_target_pairs={{0,8},{8,16},{16,24},{24,32},{32,40},{40,48},{48,56},{56,0},{1,9},... | collective-permute-start | bytes 393224 | tf_op jit(solution)/shard_map/ppermute | solution.py:286
  412.6 17.2 %all-to-all-start.14 = ((bf16[8,272,128]{2,1,0:T(8,128)(2,1)}), bf16[8,272,128]{2,1,0:T(8,128)(2,1)S(1)}, u32[]{:S(2)}, u32[]{:S(2)}) async-start(bf16[8,272,128]{2,1,0:T(8,128)(2,1)} %get-tuple-element.105), calls=%async_computation.14 | async-start | bytes 1114112 | tf_op jit(solution)/shard_map/all_to_all | solution.py:265
  433.3 12.3 %all-to-all-start.15 = ((bf16[8,64,128]{2,1,0:T(8,128)(2,1)}), bf16[8,64,128]{2,1,0:T(8,128)(2,1)S(1)}, u32[]{:S(2)}, u32[]{:S(2)}) async-start(bf16[8,64,128]{2,1,0:T(8,128)(2,1)} %get-tuple-element.107), calls=%async_computation.15 | async-start | bytes 262144 | tf_op jit(solution)/shard_map/all_to_all | solution.py:265
  437.9 6.4 copy-start.35
  438.0 7.6 %copy-start.25 = (bf16[64,1024]{1,0:T(8,128)(2,1)S(1)}, bf16[64,1024]{1,0:T(8,128)(2,1)}, u32[]{:S(2)}) copy-start(bf16[64,1024]{1,0:T(8,128)(2,1)} %copy-done.24) | copy-start | bytes 393220
  445.6 2.2 copy-start.4
  448.8 31.8 %copy-start.17 = (f32[2,64,512]{2,1,0:T(8,128)S(1)}, f32[2,64,512]{2,1,0:T(8,128)}, u32[]{:S(2)}) copy-start(f32[2,64,512]{2,1,0:T(8,128)} %copy-done.16) | copy-start | bytes 786436
  448.9 7.2 %collective-permute-start.18 = (bf16[64,1024]{1,0:T(8,128)(2,1)S(1)}, bf16[64,1024]{1,0:T(8,128)(2,1)S(1)}, u32[]{:S(2)}, u32[]{:S(2)}) collective-permute-start(bf16[64,1024]{1,0:T(8,128)(2,1)S(1)} %get-tuple-element.112), channel_id=1, source_target_pairs={{0,8},{8,16},{16,24},{24,32},{32,40},{40,48},{48,56},{56,0},{1,9},... | collective-permute-start | bytes 393224 | tf_op jit(solution)/shard_map/ppermute | solution.py:286
  456.0 37.3 %copy-start.5 = (bf16[2,1024,1024]{2,1,0:T(8,128)(2,1)S(1)}, bf16[2,1024,1024]{2,1,0:T(8,128)(2,1)}, u32[]{:S(2)}) copy-start(bf16[2,1024,1024]{2,1,0:T(8,128)(2,1)} %copy-done.1) | copy-start | bytes 12582916
  494.4 7.2 %collective-permute-start.19 = (bf16[64,1024]{1,0:T(8,128)(2,1)S(1)}, bf16[64,1024]{1,0:T(8,128)(2,1)S(1)}, u32[]{:S(2)}, u32[]{:S(2)}) collective-permute-start(bf16[64,1024]{1,0:T(8,128)(2,1)S(1)} %get-tuple-element.118), channel_id=1, source_target_pairs={{0,8},{8,16},{16,24},{24,32},{32,40},{40,48},{48,56},{56,0},{1,9},... | collective-permute-start | bytes 393224 | tf_op jit(solution)/shard_map/ppermute | solution.py:286
  506.5 19.3 %copy-start.26 = (bf16[64,1024]{1,0:T(8,128)(2,1)}, bf16[64,1024]{1,0:T(8,128)(2,1)S(1)}, u32[]{:S(2)}) copy-start(bf16[64,1024]{1,0:T(8,128)(2,1)S(1)} %get-tuple-element.122.h_ref) | copy-start | bytes 393220
  525.8 12.4 %all-to-all-start.19 = ((bf16[8,64,128]{2,1,0:T(8,128)(2,1)}), bf16[8,64,128]{2,1,0:T(8,128)(2,1)S(1)}, u32[]{:S(2)}, u32[]{:S(2)}) async-start(bf16[8,64,128]{2,1,0:T(8,128)(2,1)} %get-tuple-element.121), calls=%async_computation.19 | async-start | bytes 262144 | tf_op jit(solution)/shard_map/all_to_all | solution.py:265
  532.7 11.2 %copy-start.27 = (bf16[64,1024]{1,0:T(8,128)(2,1)S(1)}, bf16[64,1024]{1,0:T(8,128)(2,1)}, u32[]{:S(2)}) copy-start(bf16[64,1024]{1,0:T(8,128)(2,1)} %copy-done.26) | copy-start | bytes 393220
  538.2 23.4 %all-to-all-start.21 = ((bf16[8,32,1024]{2,1,0:T(8,128)(2,1)}), bf16[8,32,1024]{2,1,0:T(8,128)(2,1)}, u32[]{:S(2)}, u32[]{:S(2)}) async-start(bf16[8,32,1024]{2,1,0:T(8,128)(2,1)} %shard_map.167), calls=%async_computation.21 | async-start | bytes 1048576 | tf_op jit(solution)/shard_map/all_to_all | solution.py:265
  547.9 7.3 %collective-permute-start.20 = (bf16[64,1024]{1,0:T(8,128)(2,1)S(1)}, bf16[64,1024]{1,0:T(8,128)(2,1)S(1)}, u32[]{:S(2)}, u32[]{:S(2)}) collective-permute-start(bf16[64,1024]{1,0:T(8,128)(2,1)S(1)} %get-tuple-element.124), channel_id=1, source_target_pairs={{0,8},{8,16},{16,24},{24,32},{32,40},{40,48},{48,56},{56,0},{1,9},... | collective-permute-start | bytes 393224 | tf_op jit(solution)/shard_map/ppermute | solution.py:286
  561.6 20.0 %all-to-all-start.20 = ((bf16[8,272,128]{2,1,0:T(8,128)(2,1)}), bf16[8,272,128]{2,1,0:T(8,128)(2,1)S(1)}, u32[]{:S(2)}, u32[]{:S(2)}) async-start(bf16[8,272,128]{2,1,0:T(8,128)(2,1)} %copy-done.11), calls=%async_computation.20 | async-start | bytes 1114112 | tf_op jit(solution)/shard_map/all_to_all | solution.py:265
  584.1 13.4 %all-to-all-start.22 = ((bf16[8,64,128]{2,1,0:T(8,128)(2,1)}), bf16[8,64,128]{2,1,0:T(8,128)(2,1)S(1)}, u32[]{:S(2)}, u32[]{:S(2)}) async-start(bf16[8,64,128]{2,1,0:T(8,128)(2,1)} %get-tuple-element.129), calls=%async_computation.22 | async-start | bytes 262144 | tf_op jit(solution)/shard_map/all_to_all | solution.py:265
  593.3 11.2 %copy-start.13 = (bf16[2,64,1024]{2,1,0:T(8,128)(2,1)S(1)}, bf16[2,64,1024]{2,1,0:T(8,128)(2,1)}, u32[]{:S(2)}) copy-start(bf16[2,64,1024]{2,1,0:T(8,128)(2,1)} %copy-done.12) | copy-start | bytes 786436
  593.3 11.2 %copy-start.21 = (bf16[64,1024]{1,0:T(8,128)(2,1)S(1)}, bf16[64,1024]{1,0:T(8,128)(2,1)}, u32[]{:S(2)}) copy-start(bf16[64,1024]{1,0:T(8,128)(2,1)} %copy-done.20) | copy-start | bytes 393220
  597.5 31.9 %all-to-all-start.23 = ((bf16[8,32,1024]{2,1,0:T(8,128)(2,1)}), bf16[8,32,1024]{2,1,0:T(8,128)(2,1)S(1)}, u32[]{:S(2)}, u32[]{:S(2)}) async-start(bf16[8,32,1024]{2,1,0:T(8,128)(2,1)} %shard_map.169), calls=%async_computation.23 | async-start | bytes 1048576 | tf_op jit(solution)/shard_map/all_to_all | solution.py:265
  606.7 16.3 %copy-start.38 = (s32[1,2]{1,0:T(1,128)S(1)}, s32[1,2]{1,0:T(1,128)}, u32[]{:S(2)}) copy-start(s32[1,2]{1,0:T(1,128)} %param.14) | copy-start | bytes 28
  606.7 21.0 %copy-start.32 = (bf16[32,1024]{1,0:T(8,128)(2,1)S(1)}, bf16[32,1024]{1,0:T(8,128)(2,1)}, u32[]{:S(2)}) copy-start(bf16[32,1024]{1,0:T(8,128)(2,1)} %reduce_sum.43) | copy-start | bytes 196612
  608.6 19.2 %collective-permute-start.21 = (bf16[2,64,256]{2,1,0:T(8,128)(2,1)S(1)}, bf16[2,64,256]{2,1,0:T(8,128)(2,1)S(1)}, u32[]{:S(2)}, u32[]{:S(2)}) collective-permute-start(bf16[2,64,256]{2,1,0:T(8,128)(2,1)S(1)} %get-tuple-element.144), channel_id=1, source_target_pairs={{0,0},{4,1},{1,2},{5,3},{2,4},{6,5},{3,6},{7,7},{8,8},{12,9},{9,10... | collective-permute-start | bytes 196616 | tf_op jit(solution)/shard_map/ppermute | solution.py:311
  611.9 15.8 %collective-permute-start.22 = (bf16[2,64,256]{2,1,0:T(8,128)(2,1)S(1)}, bf16[2,64,256]{2,1,0:T(8,128)(2,1)S(1)}, u32[]{:S(2)}, u32[]{:S(2)}) collective-permute-start(bf16[2,64,256]{2,1,0:T(8,128)(2,1)S(1)} %get-tuple-element.147), channel_id=1, source_target_pairs={{1,0},{5,1},{2,2},{6,3},{3,4},{7,5},{0,6},{4,7},{9,8},{13,9},{10,1... | collective-permute-start | bytes 196616 | tf_op jit(solution)/shard_map/ppermute | solution.py:311
  613.9 13.9 %collective-permute-start.23 = (bf16[2,64,256]{2,1,0:T(8,128)(2,1)S(1)}, bf16[2,64,256]{2,1,0:T(8,128)(2,1)S(1)}, u32[]{:S(2)}, u32[]{:S(2)}) collective-permute-start(bf16[2,64,256]{2,1,0:T(8,128)(2,1)S(1)} %get-tuple-element.146), channel_id=1, source_target_pairs={{2,0},{6,1},{3,2},{7,3},{0,4},{4,5},{1,6},{5,7},{10,8},{14,9},{11,... | collective-permute-start | bytes 196616 | tf_op jit(solution)/shard_map/ppermute | solution.py:311
  621.1 8.3 %collective-permute-start.24 = (bf16[2,64,256]{2,1,0:T(8,128)(2,1)S(1)}, bf16[2,64,256]{2,1,0:T(8,128)(2,1)S(1)}, u32[]{:S(2)}, u32[]{:S(2)}) collective-permute-start(bf16[2,64,256]{2,1,0:T(8,128)(2,1)S(1)} %get-tuple-element.145), channel_id=1, source_target_pairs={{3,0},{7,1},{0,2},{4,3},{1,4},{5,5},{2,6},{6,7},{11,8},{15,9},{8,1... | collective-permute-start | bytes 196616 | tf_op jit(solution)/shard_map/ppermute | solution.py:311
  630.3 9.9 %all-to-all-start.24 = ((bf16[8,2,4,1024]{3,2,1,0:T(4,128)(2,1)}), bf16[8,2,4,1024]{3,2,1,0:T(4,128)(2,1)S(1)}, u32[]{:S(2)}, u32[]{:S(2)}) async-start(bf16[8,2,4,1024]{3,2,1,0:T(4,128)(2,1)} %maximum_bitcast_fusion.1), calls=%async_computation.24 | async-start | bytes 262144 | tf_op jit(solution)/shard_map/all_to_all | solution.py:265
  (15 other events, 18.3 us)
Sparse Core Ops, SparseCore 0:
  9.9 43.6 all-gather.5
  85.9 42.1 all-gather.3
  252.7 58.3 all-gather.7

commit v4 on v3

--- a/solution.py
+++ b/solution.py
@@ -29,19 +29,47 @@
     return jnp.clip(step - ints[0], 0, slots - 1)
 
 
+def fetch_kernel(*refs):
+    ints, srcs, dst, sems = refs[0], refs[1:-2], refs[-2], refs[-1]
+    copies = []
+    for i in range(len(srcs)):
+        size = srcs[i].shape[0] // 2
+        for half in range(2):
+            at = pl.ds(half * size, size)
+            copies.append(pltpu.make_async_copy(srcs[i].at[at], dst.at[i, at], sems.at[i, half]))
+            copies[-1].start()
+    for copy in copies:
+        copy.wait()
+
+
+def fetch(ints, arrays):
+    return pl.pallas_call(
+        fetch_kernel,
+        in_specs=[pl.BlockSpec(memory_space=pltpu.SMEM)]
+        + [pl.BlockSpec(memory_space=pl.ANY)] * len(arrays),
+        out_specs=pl.BlockSpec(memory_space=pltpu.VMEM),
+        out_shape=pltpu.VMEM((len(arrays),) + arrays[0].shape, arrays[0].dtype),
+        scratch_shapes=[pltpu.SemaphoreType.DMA((len(arrays), 2))],
+        compiler_params=pltpu.CompilerParams(vmem_limit_bytes=VMEM_BYTES),
+    )(ints, *arrays)
+
+
 def query_kernel(step, ints, text_ref, gain_ref, *refs):
-    h_ref = refs[0] if len(refs) == 9 else None
-    w_refs, q_ref, hq_ref, w_s, sems = refs[-8:-4], refs[-4], refs[-3], refs[-2], refs[-1]
-    n, chunk, cols = w_refs[0].shape
     copies = []
-    for half in range(2):
-        at = pl.ds(half * (n // 2), n // 2)
-        for j in range(4):
-            copy = pltpu.make_async_copy(w_refs[j].at[at], w_s.at[j, at], sems.at[half, j])
-            copy.start()
-            copies.append(copy)
+    if step == 0:
+        w_refs, (q_ref, hq_ref, w_s, sems) = refs[:4], refs[4:]
+        n = w_s.shape[1]
+        for half in range(2):
+            at = pl.ds(half * (n // 2), n // 2)
+            for j in range(4):
+                copy = pltpu.make_async_copy(w_refs[j].at[at], w_s.at[j, at], sems.at[half, j])
+                copy.start()
+                copies.append(copy)
+    else:
+        h_ref, w_s, q_ref, hq_ref = refs
+    _, n, chunk, cols = w_s.shape
     h = text_ref[slot_of(step, ints, text_ref.shape[0])]
-    if h_ref is not None:
+    if step > 0:
         h = jnp.where(ints[0] == 0, h, h_ref[...])
     hq_ref[...] = h
     hf = h.astype(jnp.float32)
@@ -68,24 +96,28 @@
 
 def query(step, ints, text, gain, h, w):
     rows, feats = text.shape[1:]
-    n, chunk, cols = w[0].shape
-    args = [text, gain] + ([] if h is None else [h])
+    n, chunk, cols = w[0].shape if step == 0 else w.shape[1:]
+    vmem = pl.BlockSpec(memory_space=pltpu.VMEM)
+    scratch = []
+    if step == 0:
+        scratch = [
+            pltpu.VMEM((4, n, chunk, cols), jnp.bfloat16),
+            pltpu.SemaphoreType.DMA((2, 4)),
+        ]
+        args, specs = [text, gain] + list(w), [vmem] * 2 + [pl.BlockSpec(memory_space=pl.ANY)] * 4
+    else:
+        args, specs = [text, gain, h, w], [vmem] * 4
     return pl.pallas_call(
         functools.partial(query_kernel, step),
-        in_specs=[pl.BlockSpec(memory_space=pltpu.SMEM)]
-        + [pl.BlockSpec(memory_space=pltpu.VMEM)] * len(args)
-        + [pl.BlockSpec(memory_space=pl.ANY)] * 4,
-        out_specs=[pl.BlockSpec(memory_space=pltpu.VMEM)] * 2,
+        in_specs=[pl.BlockSpec(memory_space=pltpu.SMEM)] + specs,
+        out_specs=[vmem] * 2,
         out_shape=[
             jax.ShapeDtypeStruct((n, cols // LANES * rows + EXTRA, LANES), jnp.bfloat16),
             jax.ShapeDtypeStruct((rows, feats), jnp.bfloat16),
         ],
-        scratch_shapes=[
-            pltpu.VMEM((4, n, chunk, cols), jnp.bfloat16),
-            pltpu.SemaphoreType.DMA((2, 4)),
-        ],
-        compiler_params=pltpu.CompilerParams(vmem_limit_bytes=VMEM_BYTES),
-    )(ints, *args, *w)
+        scratch_shapes=scratch,
+        compiler_params=pltpu.CompilerParams(vmem_limit_bytes=VMEM_BYTES),
+    )(ints, *args)
 
 
 def keep(step, ints, kept_ref, new, old_ref):
@@ -346,7 +378,7 @@
         return jnp.sum(swap(part, "tensor").astype(jnp.float32), axis=0).astype(jnp.bfloat16)
 
     for step in range(S + slots - 1):
-        parts, hq = query(step, ints, text_f, gain_f, h, wq_f)
+        parts, hq = query(step, ints, text_f, gain_f, h, wq_f if step == 0 else w)
         if step == 0:
             across = [dp_flip(own, 2) for own in (wo_a, wo_b)]
             parts = after(parts, across[0])
@@ -373,6 +405,8 @@
         if step >= S - 1:
             grads.append(image_part(step - S + 1))
         h, kept_h = output(step, ints, probs, vo, hq, kept_h)
+        if step < S + slots - 2:
+            w = fetch(ints, [after(own, h) for own in wq_f])
         h = onward(h)
 
     states = unspread(kept_h)

time: 659 us -> 641 us (0.973)
  waiting for transfers between devices: 187 us -> 161 us
  Pallas kernels: 82.5 us -> 90.5 us
    ppermute x8, waiting for transfers between devices: 56.9 us -> 24.7 us  [onward(): return lax.ppermute(x, 'section', [(i, (i + 1) % S) for i in range(S)])]
    pallas_call x0 -> x8, Pallas kernels: none -> 32.1 us  [fetch(): pl.pallas_call(fetch_kernel, in_specs=[pl.BlockSpec(memory_space=pltpu.SM...]
    pallas_call x9, Pallas kernels: 45.4 us -> 22.5 us  [query(): pl.pallas_call(functools.partial(query_kernel, step), in_specs=[pl.BlockS...]
    unnamed x80 -> x70, local copies, waits for them, and re-layouts: 26.2 us -> 28.9 us
  transfers between devices with their start and end apart: 40 -> 40, of which waited for: 23 -> 24; matrix products, arithmetic and copies ran while one was open for 6% -> 6% of each run, Pallas kernels for 8% -> 11%
where the time goes in v4:
time: 641 us; the launch traced here: 630 us
  blocking collectives  192 us (30%)
  waiting for transfers between devices  161 us (25%)
  starting transfers between devices  102 us (16%)
  Pallas kernels  90.5 us (14%)
  local copies, waits for them, and re-layouts  43.1 us (7%)
  between operations  19.9 us (3%)
  other arithmetic  12.2 us (2%)
  matrix products  10.3 us (2%)
    all_to_all x13, blocking collectives, swap(): return lax.all_to_all(x, axis, 0, 0, tiled=True)  192 us
    all_to_all x12, waiting for transfers between devices, swap(): return lax.all_to_all(x, axis, 0, 0, tiled=True)  69.5 us
    all_to_all x12, starting transfers between devices, swap(): return lax.all_to_all(x, axis, 0, 0, tiled=True)  64.6 us
    ppermute x4, waiting for transfers between devices, spread(): got.append(lax.ppermute(pick(parts, (a + k) % D), 'tensor', pairs))  32.9 us
    pallas_call x8, Pallas kernels, fetch(): pl.pallas_call(fetch_kernel, in_specs=[pl.BlockSpec(memory_space=pltpu.SM...  32.1 us
    all_gather x1, waiting for transfers between devices, per_device(): img = lax.all_gather(img, 'tensor', axis=1, tiled=True)  32 us
    unnamed x70, local copies, waits for them, and re-layouts  28.9 us
    ppermute x8, waiting for transfers between devices, onward(): return lax.ppermute(x, 'section', [(i, (i + 1) % S) for i in range(S)])  24.7 us
  transfers between devices with their start and end apart: 40, of which 24 were waited for; matrix products, arithmetic and copies ran while one was open for 6% of the time, Pallas kernels for 11%

profile of v4, /device:TPU:32, one launch (start us, length us, event | category | flops | bytes accessed | tf_op | source)
XLA Modules:
  0.0 630.1 jit_solution(10405462951367506235)
XLA Ops:
  13.7 11.9 %all_to_all.125 = bf16[8,8,1024]{2,1,0:T(8,128)(2,1)} all-to-all(bf16[8,8,1024]{2,1,0:T(8,128)(2,1)S(1)} %broadcast_in_dim.53), channel_id=1, replica_groups=mesh['dp'=4,'section'=8,'tensor'=8] {'section'}, dimensions={0} | all-to-all | bytes 262144 | tf_op jit(solution)/shard_map/all_to_all | solution.py:297
  25.6 8.6 %all-to-all-start.1 = ((bf16[8,256,512]{2,1,0:T(8,128)(2,1)}), bf16[8,256,512]{2,1,0:T(8,128)(2,1)}, u32[]{:S(2)}, u32[]{:S(2)}) async-start(bf16[8,256,512]{2,1,0:T(8,128)(2,1)} %bitcast.112), calls=%async_computation.1 | async-start | bytes 4194304 | tf_op jit(solution)/shard_map/all_to_all | solution.py:297
  35.0 6.4 %collective-permute-start = (bf16[2,64,256]{2,1,0:T(8,128)(2,1)S(1)}, bf16[2,64,256]{2,1,0:T(8,128)(2,1)S(1)}, u32[]{:S(2)}, u32[]{:S(2)}) collective-permute-start(bf16[2,64,256]{2,1,0:T(8,128)(2,1)S(1)} %get-tuple-element.222), channel_id=1, source_target_pairs={{0,0},{1,4},{2,1},{3,5},{4,2},{5,6},{6,3},{7,7},{8,8},{9,12},{10,9... | collective-permute-start | bytes 196616 | tf_op jit(solution)/shard_map/ppermute | solution.py:333
  47.4 3.9 copy.20
  51.4 3.9 copy.21
  55.3 24.9 %collective-permute-done = bf16[2,64,256]{2,1,0:T(8,128)(2,1)S(1)} collective-permute-done((bf16[2,64,256]{2,1,0:T(8,128)(2,1)S(1)}, bf16[2,64,256]{2,1,0:T(8,128)(2,1)S(1)}, u32[]{:S(2)}, u32[]{:S(2)}) %collective-permute-start) | collective-permute-done | bytes 65568 | tf_op jit(solution)/shard_map/ppermute | solution.py:333
  80.2 3.0 collective-permute-done.1
  83.2 4.8 collective-permute-done.2
  88.3 2.8 collective-permute-start.5
  91.1 3.1 fusion.1
  94.2 4.8 all-to-all-start.2
  99.0 32.0 %all-gather.4.cloned.1.call-done = bf16[64,8192]{1,0:T(8,128)(2,1)} async-done(((bf16[64,1024]{1,0:T(8,128)(2,1)}), bf16[64,8192]{1,0:T(8,128)(2,1)}) %all-gather.4.cloned.1.call-update) | async-done | bytes 1048592 | tf_op jit(solution)/shard_map/all_gather | solution.py:359
  133.6 5.5 all-to-all-start.4
  140.2 24.5 %all-to-all-done.4.refs_4_ = bf16[8,256,256]{2,1,0:T(8,128)(2,1)} async-done(((bf16[8,256,256]{2,1,0:T(8,128)(2,1)}), bf16[8,256,256]{2,1,0:T(8,128)(2,1)}, u32[]{:S(2)}, u32[]{:S(2)}) %all-to-all-start.4) | async-done | bytes 1048608 | tf_op jit(solution)/shard_map/all_to_all | solution.py:297
  168.4 4.9 shard_map.140
  174.8 5.7 all-to-all-start.3
  180.4 3.9 fusion.4
  190.9 6.5 %all-to-all-done.3.q_ref = bf16[8,272,128]{2,1,0:T(8,128)(2,1)} async-done(((bf16[8,272,128]{2,1,0:T(8,128)(2,1)}), bf16[8,272,128]{2,1,0:T(8,128)(2,1)}, u32[]{:S(2)}, u32[]{:S(2)}) %all-to-all-start.3) | async-done | bytes 557088 | tf_op jit(solution)/shard_map/all_to_all | solution.py:297
  199.3 14.7 %all_to_all.126 = bf16[8,128,128]{2,1,0:T(8,128)(2,1)S(1)} all-to-all(bf16[8,128,128]{2,1,0:T(8,128)(2,1)S(1)} %pad_maximum_fusion.4), channel_id=1, replica_groups=mesh['dp'=4,'section'=8,'tensor'=8] {'tensor'}, dimensions={0} | all-to-all | bytes 524288 | tf_op jit(solution)/shard_map/all_to_all | solution.py:297
  214.1 5.5 shard_map.142.vo_ref
  224.6 4.0 shard_map.144.refs_1_
  232.0 20.2 %all_to_all.127.q_ref = bf16[8,272,128]{2,1,0:T(8,128)(2,1)S(1)} all-to-all(bf16[8,272,128]{2,1,0:T(8,128)(2,1)S(1)} %get-tuple-element.117), channel_id=1, replica_groups=mesh['dp'=4,'section'=8,'tensor'=8] {'tensor'}, dimensions={0} | all-to-all | bytes 1114112 | tf_op jit(solution)/shard_map/all_to_all | solution.py:297
  253.5 11.5 %all_to_all.128.p_ref = bf16[8,64,128]{2,1,0:T(8,128)(2,1)S(1)} all-to-all(bf16[8,64,128]{2,1,0:T(8,128)(2,1)S(1)} %get-tuple-element.119), channel_id=1, replica_groups=mesh['dp'=4,'section'=8,'tensor'=8] {'tensor'}, dimensions={0} | all-to-all | bytes 262144 | tf_op jit(solution)/shard_map/all_to_all | solution.py:297
  269.2 4.0 shard_map.148.refs_1_
  273.2 5.3 collective-permute-done.14.refs_0_
  280.6 17.9 %all_to_all.129.q_ref = bf16[8,272,128]{2,1,0:T(8,128)(2,1)S(1)} all-to-all(bf16[8,272,128]{2,1,0:T(8,128)(2,1)S(1)} %get-tuple-element.127), channel_id=1, replica_groups=mesh['dp'=4,'section'=8,'tensor'=8] {'tensor'}, dimensions={0} | all-to-all | bytes 1114112 | tf_op jit(solution)/shard_map/all_to_all | solution.py:297
  299.7 11.5 %all_to_all.130.p_ref = bf16[8,64,128]{2,1,0:T(8,128)(2,1)S(1)} all-to-all(bf16[8,64,128]{2,1,0:T(8,128)(2,1)S(1)} %get-tuple-element.129), channel_id=1, replica_groups=mesh['dp'=4,'section'=8,'tensor'=8] {'tensor'}, dimensions={0} | all-to-all | bytes 262144 | tf_op jit(solution)/shard_map/all_to_all | solution.py:297
  312.4 4.0 shard_map.152.refs_1_
  316.4 3.0 collective-permute-done.15.refs_0_
  321.5 16.8 %all_to_all.131.q_ref = bf16[8,272,128]{2,1,0:T(8,128)(2,1)S(1)} all-to-all(bf16[8,272,128]{2,1,0:T(8,128)(2,1)S(1)} %get-tuple-element.137), channel_id=1, replica_groups=mesh['dp'=4,'section'=8,'tensor'=8] {'tensor'}, dimensions={0} | all-to-all | bytes 1114112 | tf_op jit(solution)/shard_map/all_to_all | solution.py:297
  339.6 11.5 %all_to_all.132.p_ref = bf16[8,64,128]{2,1,0:T(8,128)(2,1)S(1)} all-to-all(bf16[8,64,128]{2,1,0:T(8,128)(2,1)S(1)} %get-tuple-element.139), channel_id=1, replica_groups=mesh['dp'=4,'section'=8,'tensor'=8] {'tensor'}, dimensions={0} | all-to-all | bytes 262144 | tf_op jit(solution)/shard_map/all_to_all | solution.py:297
  352.2 4.0 shard_map.156.refs_1_
  356.3 3.0 collective-permute-done.16.refs_0_
  361.4 16.0 %all_to_all.133.q_ref = bf16[8,272,128]{2,1,0:T(8,128)(2,1)S(1)} all-to-all(bf16[8,272,128]{2,1,0:T(8,128)(2,1)S(1)} %get-tuple-element.147), channel_id=1, replica_groups=mesh['dp'=4,'section'=8,'tensor'=8] {'tensor'}, dimensions={0} | all-to-all | bytes 1114112 | tf_op jit(solution)/shard_map/all_to_all | solution.py:297
  378.7 11.6 %all_to_all.134.p_ref = bf16[8,64,128]{2,1,0:T(8,128)(2,1)S(1)} all-to-all(bf16[8,64,128]{2,1,0:T(8,128)(2,1)S(1)} %get-tuple-element.149), channel_id=1, replica_groups=mesh['dp'=4,'section'=8,'tensor'=8] {'tensor'}, dimensions={0} | all-to-all | bytes 262144 | tf_op jit(solution)/shard_map/all_to_all | solution.py:297
  391.6 4.0 shard_map.160.refs_1_
  395.6 3.0 collective-permute-done.17.refs_0_
  398.7 2.9 shard_map.161
  402.2 4.9 all-to-all-start.14
  407.2 12.2 %all-to-all-done.14.q_ref = bf16[8,272,128]{2,1,0:T(8,128)(2,1)S(1)} async-done(((bf16[8,272,128]{2,1,0:T(8,128)(2,1)}), bf16[8,272,128]{2,1,0:T(8,128)(2,1)S(1)}, u32[]{:S(2)}, u32[]{:S(2)}) %all-to-all-start.14) | async-done | bytes 557088 | tf_op jit(solution)/shard_map/all_to_all | solution.py:297
  423.0 4.6 all-to-all-start.15
  427.7 6.3 %fusion.5 = f32[512,128]{0,1:T(8,128)S(1)} fusion(bf16[512,8192]{1,0:T(8,128)(2,1)} %all-gather.8.cloned.1.call-done, bf16[128,8192]{1,0:T(8,128)(2,1)S(1)} %bitcast.97), kind=kOutput, calls=%fused_computation.67 | convolution fusion | flops 1073741824 | bytes 10747904 | tf_op jit(solution)/shard_map/dot_general | solution.py:25
  438.6 4.0 shard_map.164.refs_1_
  442.7 3.0 collective-permute-done.18.refs_0_
  447.8 19.4 %all_to_all.135.q_ref = bf16[8,272,128]{2,1,0:T(8,128)(2,1)S(1)} all-to-all(bf16[8,272,128]{2,1,0:T(8,128)(2,1)S(1)} %get-tuple-element.169), channel_id=1, replica_groups=mesh['dp'=4,'section'=8,'tensor'=8] {'tensor'}, dimensions={0} | all-to-all | bytes 1114112 | tf_op jit(solution)/shard_map/all_to_all | solution.py:297
  468.5 11.5 %all_to_all.136.p_ref = bf16[8,64,128]{2,1,0:T(8,128)(2,1)S(1)} all-to-all(bf16[8,64,128]{2,1,0:T(8,128)(2,1)S(1)} %get-tuple-element.171), channel_id=1, replica_groups=mesh['dp'=4,'section'=8,'tensor'=8] {'tensor'}, dimensions={0} | all-to-all | bytes 262144 | tf_op jit(solution)/shard_map/all_to_all | solution.py:297
  481.1 4.0 shard_map.168.refs_1_
  485.1 3.0 collective-permute-done.19.refs_0_
  490.3 17.4 %all_to_all.137.q_ref = bf16[8,272,128]{2,1,0:T(8,128)(2,1)S(1)} all-to-all(bf16[8,272,128]{2,1,0:T(8,128)(2,1)S(1)} %get-tuple-element.179), channel_id=1, replica_groups=mesh['dp'=4,'section'=8,'tensor'=8] {'tensor'}, dimensions={0} | all-to-all | bytes 1114112 | tf_op jit(solution)/shard_map/all_to_all | solution.py:297
  509.6 4.7 all-to-all-start.19
  516.5 4.0 shard_map.175
  522.0 5.7 all-to-all-start.21
  532.0 4.0 shard_map.172.refs_1_
  536.0 3.0 collective-permute-done.20.refs_0_
  542.6 2.8 all-to-all-done.21
  545.4 5.0 all-to-all-start.20
  552.2 11.9 %all-to-all-done.20.q_ref = bf16[8,272,128]{2,1,0:T(8,128)(2,1)S(1)} async-done(((bf16[8,272,128]{2,1,0:T(8,128)(2,1)}), bf16[8,272,128]{2,1,0:T(8,128)(2,1)S(1)}, u32[]{:S(2)}, u32[]{:S(2)}) %all-to-all-start.20) | async-done | bytes 557088 | tf_op jit(solution)/shard_map/all_to_all | solution.py:297
  565.9 4.7 all-to-all-start.22
  573.6 4.0 shard_map.177
  578.0 6.9 %all-to-all-start.23 = ((bf16[8,32,1024]{2,1,0:T(8,128)(2,1)}), bf16[8,32,1024]{2,1,0:T(8,128)(2,1)S(1)}, u32[]{:S(2)}, u32[]{:S(2)}) async-start(bf16[8,32,1024]{2,1,0:T(8,128)(2,1)} %shard_map.177), calls=%async_computation.23 | async-start | bytes 1048576 | tf_op jit(solution)/shard_map/all_to_all | solution.py:297
  590.8 3.4 collective-permute-start.21
  596.1 7.2 %collective-permute-start.23 = (bf16[2,64,256]{2,1,0:T(8,128)(2,1)S(1)}, bf16[2,64,256]{2,1,0:T(8,128)(2,1)S(1)}, u32[]{:S(2)}, u32[]{:S(2)}) collective-permute-start(bf16[2,64,256]{2,1,0:T(8,128)(2,1)S(1)} %get-tuple-element.210), channel_id=1, source_target_pairs={{2,0},{6,1},{3,2},{7,3},{0,4},{4,5},{1,6},{5,7},{10,8},{14,9},{11,... | collective-permute-start | bytes 196616 | tf_op jit(solution)/shard_map/ppermute | solution.py:343
  612.5 3.4 all-to-all-start.24
  616.6 5.8 all-to-all-done.24
  (194 shorter events, 107.5 us)
Async XLA Ops:
  7.2 420.5 %copy-start = (bf16[1,2,64,8192]{3,2,1,0:T(8,128)(2,1)S(1)}, bf16[1,2,64,8192]{3,2,1,0:T(8,128)(2,1)}, u32[]{:S(2)}) copy-start(bf16[1,2,64,8192]{3,2,1,0:T(8,128)(2,1)} %param.25) | copy-start | bytes 6291460
  7.2 83.9 %all-gather.6.cloned.1.call-start = ((), (), s32[]{:S(2)}) async-start(), calls=%async_computation.26 | async-start | bytes 5242880 | tf_op jit(solution)/shard_map/all_gather | solution.py:353
  7.2 27.0 %copy-start.30 = (bf16[2,64,1024]{2,1,0:T(8,128)(2,1)S(1)}, bf16[2,64,1024]{2,1,0:T(8,128)(2,1)}, u32[]{:S(2)}) copy-start(bf16[2,64,1024]{2,1,0:T(8,128)(2,1)} %param.13) | copy-start | bytes 786436
  25.6 62.6 %all-to-all-start.1 = ((bf16[8,256,512]{2,1,0:T(8,128)(2,1)}), bf16[8,256,512]{2,1,0:T(8,128)(2,1)}, u32[]{:S(2)}, u32[]{:S(2)}) async-start(bf16[8,256,512]{2,1,0:T(8,128)(2,1)} %bitcast.112), calls=%async_computation.1 | async-start | bytes 4194304 | tf_op jit(solution)/shard_map/all_to_all | solution.py:297
  34.2 96.7 %all-gather.4.cloned.1.call-start = ((), (), s32[]{:S(2)}) async-start(), calls=%async_computation.25 | async-start | bytes 1179648 | tf_op jit(solution)/shard_map/all_gather | solution.py:359
  35.0 45.2 %collective-permute-start = (bf16[2,64,256]{2,1,0:T(8,128)(2,1)S(1)}, bf16[2,64,256]{2,1,0:T(8,128)(2,1)S(1)}, u32[]{:S(2)}, u32[]{:S(2)}) collective-permute-start(bf16[2,64,256]{2,1,0:T(8,128)(2,1)S(1)} %get-tuple-element.222), channel_id=1, source_target_pairs={{0,0},{1,4},{2,1},{3,5},{4,2},{5,6},{6,3},{7,7},{8,8},{9,12},{10,9... | collective-permute-start | bytes 196616 | tf_op jit(solution)/shard_map/ppermute | solution.py:333
  41.4 41.8 %collective-permute-start.1 = (bf16[2,64,256]{2,1,0:T(8,128)(2,1)S(1)}, bf16[2,64,256]{2,1,0:T(8,128)(2,1)S(1)}, u32[]{:S(2)}, u32[]{:S(2)}) collective-permute-start(bf16[2,64,256]{2,1,0:T(8,128)(2,1)S(1)} %get-tuple-element.225), channel_id=1, source_target_pairs={{0,1},{1,5},{2,2},{3,6},{4,3},{5,7},{6,0},{7,4},{8,9},{9,13},{10,1... | collective-permute-start | bytes 196616 | tf_op jit(solution)/shard_map/ppermute | solution.py:333
  43.9 44.2 %collective-permute-start.2 = (bf16[2,64,256]{2,1,0:T(8,128)(2,1)S(1)}, bf16[2,64,256]{2,1,0:T(8,128)(2,1)S(1)}, u32[]{:S(2)}, u32[]{:S(2)}) collective-permute-start(bf16[2,64,256]{2,1,0:T(8,128)(2,1)S(1)} %get-tuple-element.224), channel_id=1, source_target_pairs={{0,2},{1,6},{2,3},{3,7},{4,0},{5,4},{6,1},{7,5},{8,10},{9,14},{10,... | collective-permute-start | bytes 196616 | tf_op jit(solution)/shard_map/ppermute | solution.py:333
  44.9 43.3 %collective-permute-start.3 = (bf16[2,64,256]{2,1,0:T(8,128)(2,1)S(1)}, bf16[2,64,256]{2,1,0:T(8,128)(2,1)S(1)}, u32[]{:S(2)}, u32[]{:S(2)}) collective-permute-start(bf16[2,64,256]{2,1,0:T(8,128)(2,1)S(1)} %get-tuple-element.223), channel_id=1, source_target_pairs={{0,3},{1,7},{2,0},{3,4},{4,1},{5,5},{6,2},{7,6},{8,11},{9,15},{10,... | collective-permute-start | bytes 196616 | tf_op jit(solution)/shard_map/ppermute | solution.py:333
  88.3 50.8 %collective-permute-start.5 = (bf16[8,256,512]{2,1,0:T(8,128)(2,1)}, bf16[8,256,512]{2,1,0:T(8,128)(2,1)}, u32[]{:S(2)}, u32[]{:S(2)}) collective-permute-start(bf16[8,256,512]{2,1,0:T(8,128)(2,1)} %all-to-all-done.1.refs_0_.refs_1_), channel_id=1, source_target_pairs={{0,128},{64,192},{128,0},{192,64},{1,129},{65,193},{129,1},{193,65... | collective-permute-start | bytes 6291464 | tf_op jit(solution)/shard_map/ppermute | solution.py:321
  91.1 75.7 %copy-start.32 = (f32[1,8192]{1,0:T(1,128)S(1)}, f32[1,8192]{1,0:T(1,128)}, u32[]{:S(2)}) copy-start(f32[1,8192]{1,0:T(1,128)} %param.17) | copy-start | bytes 98308
  94.2 39.4 %all-to-all-start.2 = ((bf16[8,256,256]{2,1,0:T(8,128)(2,1)}), bf16[8,256,256]{2,1,0:T(8,128)(2,1)S(1)}, u32[]{:S(2)}, u32[]{:S(2)}) async-start(bf16[8,256,256]{2,1,0:T(8,128)(2,1)} %get-tuple-element.203), calls=%async_computation.2 | async-start | bytes 2097152 | tf_op jit(solution)/shard_map/all_to_all | solution.py:297
  133.6 31.1 %all-to-all-start.4 = ((bf16[8,256,256]{2,1,0:T(8,128)(2,1)}), bf16[8,256,256]{2,1,0:T(8,128)(2,1)}, u32[]{:S(2)}, u32[]{:S(2)}) async-start(bf16[8,256,256]{2,1,0:T(8,128)(2,1)} %get-tuple-element.109), calls=%async_computation.4 | async-start | bytes 2097152 | tf_op jit(solution)/shard_map/all_to_all | solution.py:297
  139.1 29.3 %collective-permute-start.4 = (bf16[8,256,512]{2,1,0:T(8,128)(2,1)}, bf16[8,256,512]{2,1,0:T(8,128)(2,1)}, u32[]{:S(2)}, u32[]{:S(2)}) collective-permute-start(bf16[8,256,512]{2,1,0:T(8,128)(2,1)} %all-to-all-done.1.refs_0_.refs_1_), channel_id=1, source_target_pairs={{0,64},{64,0},{128,192},{192,128},{1,65},{65,1},{129,193},{193,129... | collective-permute-start | bytes 6291464 | tf_op jit(solution)/shard_map/ppermute | solution.py:321
  139.1 29.3 %collective-permute-start.6 = (bf16[8,256,512]{2,1,0:T(8,128)(2,1)}, bf16[8,256,512]{2,1,0:T(8,128)(2,1)}, u32[]{:S(2)}, u32[]{:S(2)}) collective-permute-start(bf16[8,256,512]{2,1,0:T(8,128)(2,1)} %collective-permute-done.5.refs_2_.refs_3_), channel_id=1, source_target_pairs={{0,64},{64,0},{128,192},{192,128},{1,65},{65,1},{129,193},{193,129... | collective-permute-start | bytes 6291464 | tf_op jit(solution)/shard_map/ppermute | solution.py:321
  139.6 35.2 %collective-permute-start.7 = (bf16[8,256,256]{2,1,0:T(8,128)(2,1)S(1)}, bf16[8,256,256]{2,1,0:T(8,128)(2,1)}, u32[]{:S(2)}, u32[]{:S(2)}) collective-permute-start(bf16[8,256,256]{2,1,0:T(8,128)(2,1)S(1)} %all-to-all-done.2.refs_0_), channel_id=1, source_target_pairs={{0,128},{64,192},{128,0},{192,64},{1,129},{65,193},{129,1},{193,65... | collective-permute-start | bytes 3145736 | tf_op jit(solution)/shard_map/ppermute | solution.py:321
  164.7 24.2 %collective-permute-start.8 = (bf16[8,256,256]{2,1,0:T(8,128)(2,1)}, bf16[8,256,256]{2,1,0:T(8,128)(2,1)}, u32[]{:S(2)}, u32[]{:S(2)}) collective-permute-start(bf16[8,256,256]{2,1,0:T(8,128)(2,1)} %all-to-all-done.4.refs_4_), channel_id=1, source_target_pairs={{0,128},{64,192},{128,0},{192,64},{1,129},{65,193},{129,1},{193,65... | collective-permute-start | bytes 3145736 | tf_op jit(solution)/shard_map/ppermute | solution.py:321
  174.8 15.3 %copy-start.29 = (f32[1,128]{1,0:T(1,128)S(1)}, f32[1,128]{1,0:T(1,128)}, u32[]{:S(2)}) copy-start(f32[1,128]{1,0:T(1,128)} %gain_ref.21) | copy-start | bytes 1540
  174.8 22.7 %copy-start.28 = (f32[1,128]{1,0:T(1,128)S(1)}, f32[1,128]{1,0:T(1,128)}, u32[]{:S(2)}) copy-start(f32[1,128]{1,0:T(1,128)} %gain_ref.19) | copy-start | bytes 1540
  174.8 22.7 %all-to-all-start.3 = ((bf16[8,272,128]{2,1,0:T(8,128)(2,1)}), bf16[8,272,128]{2,1,0:T(8,128)(2,1)}, u32[]{:S(2)}, u32[]{:S(2)}) async-start(bf16[8,272,128]{2,1,0:T(8,128)(2,1)} %copy-done.10), calls=%async_computation.3 | async-start | bytes 1114112 | tf_op jit(solution)/shard_map/all_to_all | solution.py:297
  180.4 247.2 %all-gather.8.cloned.1.call-start = ((), (), s32[]{:S(2)}) async-start(), calls=%async_computation.27 | async-start | bytes 10485760 | tf_op jit(solution)/shard_map/all_gather | solution.py:399
  188.2 25.8 %collective-permute-start.9 = (bf16[8,256,256]{2,1,0:T(8,128)(2,1)S(1)}, bf16[8,256,256]{2,1,0:T(8,128)(2,1)}, u32[]{:S(2)}, u32[]{:S(2)}) collective-permute-start(bf16[8,256,256]{2,1,0:T(8,128)(2,1)S(1)} %all-to-all-done.2.refs_0_), channel_id=1, source_target_pairs={{0,64},{64,0},{128,192},{192,128},{1,65},{65,1},{129,193},{193,129... | collective-permute-start | bytes 3145736 | tf_op jit(solution)/shard_map/ppermute | solution.py:321
  188.3 25.7 %collective-permute-start.10 = (bf16[8,256,256]{2,1,0:T(8,128)(2,1)}, bf16[8,256,256]{2,1,0:T(8,128)(2,1)}, u32[]{:S(2)}, u32[]{:S(2)}) collective-permute-start(bf16[8,256,256]{2,1,0:T(8,128)(2,1)} %collective-permute-done.7.refs_2_), channel_id=1, source_target_pairs={{0,64},{64,0},{128,192},{192,128},{1,65},{65,1},{129,193},{193,129... | collective-permute-start | bytes 3145736 | tf_op jit(solution)/shard_map/ppermute | solution.py:321
  188.8 25.3 %collective-permute-start.11 = (bf16[8,256,256]{2,1,0:T(8,128)(2,1)}, bf16[8,256,256]{2,1,0:T(8,128)(2,1)}, u32[]{:S(2)}, u32[]{:S(2)}) collective-permute-start(bf16[8,256,256]{2,1,0:T(8,128)(2,1)} %all-to-all-done.4.refs_4_), channel_id=1, source_target_pairs={{0,64},{64,0},{128,192},{192,128},{1,65},{65,1},{129,193},{193,129... | collective-permute-start | bytes 3145736 | tf_op jit(solution)/shard_map/ppermute | solution.py:321
  188.9 25.2 %collective-permute-start.12 = (bf16[8,256,256]{2,1,0:T(8,128)(2,1)}, bf16[8,256,256]{2,1,0:T(8,128)(2,1)}, u32[]{:S(2)}, u32[]{:S(2)}) collective-permute-start(bf16[8,256,256]{2,1,0:T(8,128)(2,1)} %collective-permute-done.8.refs_6_), channel_id=1, source_target_pairs={{0,64},{64,0},{128,192},{192,128},{1,65},{65,1},{129,193},{193,129... | collective-permute-start | bytes 3145736 | tf_op jit(solution)/shard_map/ppermute | solution.py:321
  214.1 5.6 copy-start.21
  220.7 1.9 copy-start.1
  222.7 7.2 %collective-permute-start.13 = (bf16[64,1024]{1,0:T(8,128)(2,1)S(1)}, bf16[64,1024]{1,0:T(8,128)(2,1)S(1)}, u32[]{:S(2)}, u32[]{:S(2)}) collective-permute-start(bf16[64,1024]{1,0:T(8,128)(2,1)S(1)} %get-tuple-element.112), channel_id=1, source_target_pairs={{0,8},{8,16},{16,24},{24,32},{32,40},{40,48},{48,56},{56,0},{1,9},... | collective-permute-start | bytes 393224 | tf_op jit(solution)/shard_map/ppermute | solution.py:318
  265.0 2.4 copy-start.2
  268.5 10.0 %collective-permute-start.14 = (bf16[64,1024]{1,0:T(8,128)(2,1)S(1)}, bf16[64,1024]{1,0:T(8,128)(2,1)S(1)}, u32[]{:S(2)}, u32[]{:S(2)}) collective-permute-start(bf16[64,1024]{1,0:T(8,128)(2,1)S(1)} %get-tuple-element.122), channel_id=1, source_target_pairs={{0,8},{8,16},{16,24},{24,32},{32,40},{40,48},{48,56},{56,0},{1,9},... | collective-permute-start | bytes 393224 | tf_op jit(solution)/shard_map/ppermute | solution.py:318
  273.2 38.0 %copy-start.3 = (bf16[2,1024,1024]{2,1,0:T(8,128)(2,1)S(1)}, bf16[2,1024,1024]{2,1,0:T(8,128)(2,1)}, u32[]{:S(2)}) copy-start(bf16[2,1024,1024]{2,1,0:T(8,128)(2,1)} %copy-done.1) | copy-start | bytes 12582916
  312.3 7.2 %collective-permute-start.15 = (bf16[64,1024]{1,0:T(8,128)(2,1)S(1)}, bf16[64,1024]{1,0:T(8,128)(2,1)S(1)}, u32[]{:S(2)}, u32[]{:S(2)}) collective-permute-start(bf16[64,1024]{1,0:T(8,128)(2,1)S(1)} %get-tuple-element.132), channel_id=1, source_target_pairs={{0,8},{8,16},{16,24},{24,32},{32,40},{40,48},{48,56},{56,0},{1,9},... | collective-permute-start | bytes 393224 | tf_op jit(solution)/shard_map/ppermute | solution.py:318
  352.1 7.2 %collective-permute-start.16 = (bf16[64,1024]{1,0:T(8,128)(2,1)S(1)}, bf16[64,1024]{1,0:T(8,128)(2,1)S(1)}, u32[]{:S(2)}, u32[]{:S(2)}) collective-permute-start(bf16[64,1024]{1,0:T(8,128)(2,1)S(1)} %get-tuple-element.142), channel_id=1, source_target_pairs={{0,8},{8,16},{16,24},{24,32},{32,40},{40,48},{48,56},{56,0},{1,9},... | collective-permute-start | bytes 393224 | tf_op jit(solution)/shard_map/ppermute | solution.py:318
  378.7 11.6 %copy-start.16 = (f32[2,64,512]{2,1,0:T(8,128)}, f32[2,64,512]{2,1,0:T(8,128)S(1)}, u32[]{:S(2)}) copy-start(f32[2,64,512]{2,1,0:T(8,128)S(1)} %get-tuple-element.158.refs_0_) | copy-start | bytes 786436
  391.3 7.4 %collective-permute-start.17 = (bf16[64,1024]{1,0:T(8,128)(2,1)S(1)}, bf16[64,1024]{1,0:T(8,128)(2,1)S(1)}, u32[]{:S(2)}, u32[]{:S(2)}) collective-permute-start(bf16[64,1024]{1,0:T(8,128)(2,1)S(1)} %get-tuple-element.152), channel_id=1, source_target_pairs={{0,8},{8,16},{16,24},{24,32},{32,40},{40,48},{48,56},{56,0},{1,9},... | collective-permute-start | bytes 393224 | tf_op jit(solution)/shard_map/ppermute | solution.py:318
  402.2 17.2 %all-to-all-start.14 = ((bf16[8,272,128]{2,1,0:T(8,128)(2,1)}), bf16[8,272,128]{2,1,0:T(8,128)(2,1)S(1)}, u32[]{:S(2)}, u32[]{:S(2)}) async-start(bf16[8,272,128]{2,1,0:T(8,128)(2,1)} %get-tuple-element.157), calls=%async_computation.14 | async-start | bytes 1114112 | tf_op jit(solution)/shard_map/all_to_all | solution.py:297
  419.5 1.0 copy-start.17
  423.0 12.3 %all-to-all-start.15 = ((bf16[8,64,128]{2,1,0:T(8,128)(2,1)}), bf16[8,64,128]{2,1,0:T(8,128)(2,1)S(1)}, u32[]{:S(2)}, u32[]{:S(2)}) async-start(bf16[8,64,128]{2,1,0:T(8,128)(2,1)} %get-tuple-element.159), calls=%async_computation.15 | async-start | bytes 262144 | tf_op jit(solution)/shard_map/all_to_all | solution.py:297
  427.6 7.6 %copy-start.23 = (bf16[64,1024]{1,0:T(8,128)(2,1)S(1)}, bf16[64,1024]{1,0:T(8,128)(2,1)}, u32[]{:S(2)}) copy-start(bf16[64,1024]{1,0:T(8,128)(2,1)} %copy-done.22) | copy-start | bytes 393220
  435.3 2.2 copy-start.4
  438.6 7.2 %collective-permute-start.18 = (bf16[64,1024]{1,0:T(8,128)(2,1)S(1)}, bf16[64,1024]{1,0:T(8,128)(2,1)S(1)}, u32[]{:S(2)}, u32[]{:S(2)}) collective-permute-start(bf16[64,1024]{1,0:T(8,128)(2,1)S(1)} %get-tuple-element.164), channel_id=1, source_target_pairs={{0,8},{8,16},{16,24},{24,32},{32,40},{40,48},{48,56},{56,0},{1,9},... | collective-permute-start | bytes 393224 | tf_op jit(solution)/shard_map/ppermute | solution.py:318
  442.7 24.6 %copy-start.15 = (f32[2,64,512]{2,1,0:T(8,128)S(1)}, f32[2,64,512]{2,1,0:T(8,128)}, u32[]{:S(2)}) copy-start(f32[2,64,512]{2,1,0:T(8,128)} %copy-done.14) | copy-start | bytes 786436
  442.7 37.3 %copy-start.5 = (bf16[2,1024,1024]{2,1,0:T(8,128)(2,1)S(1)}, bf16[2,1024,1024]{2,1,0:T(8,128)(2,1)}, u32[]{:S(2)}) copy-start(bf16[2,1024,1024]{2,1,0:T(8,128)(2,1)} %copy-done.1) | copy-start | bytes 12582916
  481.0 7.2 %collective-permute-start.19 = (bf16[64,1024]{1,0:T(8,128)(2,1)S(1)}, bf16[64,1024]{1,0:T(8,128)(2,1)S(1)}, u32[]{:S(2)}, u32[]{:S(2)}) collective-permute-start(bf16[64,1024]{1,0:T(8,128)(2,1)S(1)} %get-tuple-element.174), channel_id=1, source_target_pairs={{0,8},{8,16},{16,24},{24,32},{32,40},{40,48},{48,56},{56,0},{1,9},... | collective-permute-start | bytes 393224 | tf_op jit(solution)/shard_map/ppermute | solution.py:318
  490.3 17.4 %copy-start.24 = (bf16[64,1024]{1,0:T(8,128)(2,1)}, bf16[64,1024]{1,0:T(8,128)(2,1)S(1)}, u32[]{:S(2)}) copy-start(bf16[64,1024]{1,0:T(8,128)(2,1)S(1)} %get-tuple-element.182.h_ref) | copy-start | bytes 393220
  507.7 20.0 %copy-start.25 = (bf16[64,1024]{1,0:T(8,128)(2,1)S(1)}, bf16[64,1024]{1,0:T(8,128)(2,1)}, u32[]{:S(2)}) copy-start(bf16[64,1024]{1,0:T(8,128)(2,1)} %copy-done.24) | copy-start | bytes 393220
  509.6 12.4 %all-to-all-start.19 = ((bf16[8,64,128]{2,1,0:T(8,128)(2,1)}), bf16[8,64,128]{2,1,0:T(8,128)(2,1)S(1)}, u32[]{:S(2)}, u32[]{:S(2)}) async-start(bf16[8,64,128]{2,1,0:T(8,128)(2,1)} %copy-done.27), calls=%async_computation.19 | async-start | bytes 262144 | tf_op jit(solution)/shard_map/all_to_all | solution.py:297
  514.4 2.2 copy-start.8
  522.0 23.4 %all-to-all-start.21 = ((bf16[8,32,1024]{2,1,0:T(8,128)(2,1)}), bf16[8,32,1024]{2,1,0:T(8,128)(2,1)}, u32[]{:S(2)}, u32[]{:S(2)}) async-start(bf16[8,32,1024]{2,1,0:T(8,128)(2,1)} %shard_map.175), calls=%async_computation.21 | async-start | bytes 1048576 | tf_op jit(solution)/shard_map/all_to_all | solution.py:297
  527.8 2.2 copy-start.6
  531.7 7.3 %collective-permute-start.20 = (bf16[64,1024]{1,0:T(8,128)(2,1)S(1)}, bf16[64,1024]{1,0:T(8,128)(2,1)S(1)}, u32[]{:S(2)}, u32[]{:S(2)}) collective-permute-start(bf16[64,1024]{1,0:T(8,128)(2,1)S(1)} %get-tuple-element.184), channel_id=1, source_target_pairs={{0,8},{8,16},{16,24},{24,32},{32,40},{40,48},{48,56},{56,0},{1,9},... | collective-permute-start | bytes 393224 | tf_op jit(solution)/shard_map/ppermute | solution.py:318
  536.0 34.7 %copy-start.33 = (s32[1,2]{1,0:T(1,128)S(1)}, s32[1,2]{1,0:T(1,128)}, u32[]{:S(2)}) copy-start(s32[1,2]{1,0:T(1,128)} %param.14) | copy-start | bytes 28
  545.4 18.6 %all-to-all-start.20 = ((bf16[8,272,128]{2,1,0:T(8,128)(2,1)}), bf16[8,272,128]{2,1,0:T(8,128)(2,1)S(1)}, u32[]{:S(2)}, u32[]{:S(2)}) async-start(bf16[8,272,128]{2,1,0:T(8,128)(2,1)} %copy-done.11), calls=%async_computation.20 | async-start | bytes 1114112 | tf_op jit(solution)/shard_map/all_to_all | solution.py:297
  565.9 12.1 %all-to-all-start.22 = ((bf16[8,64,128]{2,1,0:T(8,128)(2,1)}), bf16[8,64,128]{2,1,0:T(8,128)(2,1)S(1)}, u32[]{:S(2)}, u32[]{:S(2)}) async-start(bf16[8,64,128]{2,1,0:T(8,128)(2,1)} %copy-done.26), calls=%async_computation.22 | async-start | bytes 262144 | tf_op jit(solution)/shard_map/all_to_all | solution.py:297
  571.4 2.2 copy-start.9
  577.6 32.4 %copy-start.31 = (bf16[32,1024]{1,0:T(8,128)(2,1)S(1)}, bf16[32,1024]{1,0:T(8,128)(2,1)}, u32[]{:S(2)}) copy-start(bf16[32,1024]{1,0:T(8,128)(2,1)} %reduce_sum.43) | copy-start | bytes 196612
  578.0 33.7 %all-to-all-start.23 = ((bf16[8,32,1024]{2,1,0:T(8,128)(2,1)}), bf16[8,32,1024]{2,1,0:T(8,128)(2,1)S(1)}, u32[]{:S(2)}, u32[]{:S(2)}) async-start(bf16[8,32,1024]{2,1,0:T(8,128)(2,1)} %shard_map.177), calls=%async_computation.23 | async-start | bytes 1048576 | tf_op jit(solution)/shard_map/all_to_all | solution.py:297
  584.9 2.2 copy-start.7
  587.1 0.9 copy-start.13
  590.8 19.2 %collective-permute-start.21 = (bf16[2,64,256]{2,1,0:T(8,128)(2,1)S(1)}, bf16[2,64,256]{2,1,0:T(8,128)(2,1)S(1)}, u32[]{:S(2)}, u32[]{:S(2)}) collective-permute-start(bf16[2,64,256]{2,1,0:T(8,128)(2,1)S(1)} %get-tuple-element.208), channel_id=1, source_target_pairs={{0,0},{4,1},{1,2},{5,3},{2,4},{6,5},{3,6},{7,7},{8,8},{12,9},{9,10... | collective-permute-start | bytes 196616 | tf_op jit(solution)/shard_map/ppermute | solution.py:343
  594.2 15.8 %collective-permute-start.22 = (bf16[2,64,256]{2,1,0:T(8,128)(2,1)S(1)}, bf16[2,64,256]{2,1,0:T(8,128)(2,1)S(1)}, u32[]{:S(2)}, u32[]{:S(2)}) collective-permute-start(bf16[2,64,256]{2,1,0:T(8,128)(2,1)S(1)} %get-tuple-element.211), channel_id=1, source_target_pairs={{1,0},{5,1},{2,2},{6,3},{3,4},{7,5},{0,6},{4,7},{9,8},{13,9},{10,1... | collective-permute-start | bytes 196616 | tf_op jit(solution)/shard_map/ppermute | solution.py:343
  596.1 13.9 %collective-permute-start.23 = (bf16[2,64,256]{2,1,0:T(8,128)(2,1)S(1)}, bf16[2,64,256]{2,1,0:T(8,128)(2,1)S(1)}, u32[]{:S(2)}, u32[]{:S(2)}) collective-permute-start(bf16[2,64,256]{2,1,0:T(8,128)(2,1)S(1)} %get-tuple-element.210), channel_id=1, source_target_pairs={{2,0},{6,1},{3,2},{7,3},{0,4},{4,5},{1,6},{5,7},{10,8},{14,9},{11,... | collective-permute-start | bytes 196616 | tf_op jit(solution)/shard_map/ppermute | solution.py:343
  603.3 8.3 %collective-permute-start.24 = (bf16[2,64,256]{2,1,0:T(8,128)(2,1)S(1)}, bf16[2,64,256]{2,1,0:T(8,128)(2,1)S(1)}, u32[]{:S(2)}, u32[]{:S(2)}) collective-permute-start(bf16[2,64,256]{2,1,0:T(8,128)(2,1)S(1)} %get-tuple-element.209), channel_id=1, source_target_pairs={{3,0},{7,1},{0,2},{4,3},{1,4},{5,5},{2,6},{6,7},{11,8},{15,9},{8,1... | collective-permute-start | bytes 196616 | tf_op jit(solution)/shard_map/ppermute | solution.py:343
  612.5 9.9 %all-to-all-start.24 = ((bf16[8,2,4,1024]{3,2,1,0:T(4,128)(2,1)}), bf16[8,2,4,1024]{3,2,1,0:T(4,128)(2,1)S(1)}, u32[]{:S(2)}, u32[]{:S(2)}) async-start(bf16[8,2,4,1024]{3,2,1,0:T(4,128)(2,1)} %maximum_bitcast_fusion.1), calls=%async_computation.24 | async-start | bytes 262144 | tf_op jit(solution)/shard_map/all_to_all | solution.py:297
  (10 other events, 7.3 us)
Sparse Core Ops, SparseCore 0:
  9.8 43.6 all-gather.5
  88.4 42.4 all-gather.3
  253.6 58.9 all-gather.7

commit v5 on v4

--- a/solution.py
+++ b/solution.py
@@ -380,7 +380,7 @@
     for step in range(S + slots - 1):
         parts, hq = query(step, ints, text_f, gain_f, h, wq_f if step == 0 else w)
         if step == 0:
-            across = [dp_flip(own, 2) for own in (wo_a, wo_b)]
+            across = [dp_flip(own, 2) for own in (wo_a, after(wo_b, hq))]
             parts = after(parts, across[0])
         swapped = swap(parts, "tensor")
         p, kept_qn = attend(step, ints, alpha, width, query_norm_gain, keys, swapped, kept_qn)

time: 641 us -> 644 us (level)
    ppermute x9, waiting for transfers between devices: 0.02 us -> 41.5 us  [dp_flip(): return lax.ppermute(x, 'dp', [(i, i ^ m) for i in range(D)])]
    all_gather x1, waiting for transfers between devices: 32 us -> 0.69 us  [per_device(): img = lax.all_gather(img, 'tensor', axis=1, tiled=True)]
    all_to_all x12, waiting for transfers between devices: 69.5 us -> 52.3 us  [swap(): return lax.all_to_all(x, axis, 0, 0, tiled=True)]
where the time goes in v5:
time: 644 us; the launch traced here: 633 us
  blocking collectives  195 us (30%)
  waiting for transfers between devices  156 us (24%)
  starting transfers between devices  106 us (16%)
  Pallas kernels  90.5 us (14%)
  local copies, waits for them, and re-layouts  43.2 us (7%)
  between operations  19.9 us (3%)
  other arithmetic  12.2 us (2%)
  matrix products  10.3 us (2%)
    all_to_all x13, blocking collectives, swap(): return lax.all_to_all(x, axis, 0, 0, tiled=True)  195 us
    all_to_all x12, starting transfers between devices, swap(): return lax.all_to_all(x, axis, 0, 0, tiled=True)  68.9 us
    all_to_all x12, waiting for transfers between devices, swap(): return lax.all_to_all(x, axis, 0, 0, tiled=True)  52.3 us
    ppermute x9, waiting for transfers between devices, dp_flip(): return lax.ppermute(x, 'dp', [(i, i ^ m) for i in range(D)])  41.5 us
    ppermute x4, waiting for transfers between devices, spread(): got.append(lax.ppermute(pick(parts, (a + k) % D), 'tensor', pairs))  32.9 us
    pallas_call x8, Pallas kernels, fetch(): pl.pallas_call(fetch_kernel, in_specs=[pl.BlockSpec(memory_space=pltpu.SM...  32.1 us
    unnamed x70, local copies, waits for them, and re-layouts  29 us
    ppermute x8, waiting for transfers between devices, onward(): return lax.ppermute(x, 'section', [(i, (i + 1) % S) for i in range(S)])  26.8 us
  transfers between devices with their start and end apart: 40, of which 24 were waited for; matrix products, arithmetic and copies ran while one was open for 6% of the time, Pallas kernels for 11%

profile of v5, /device:TPU:32, one launch (start us, length us, event | category | flops | bytes accessed | tf_op | source)
XLA Modules:
  0.0 633.0 jit_solution(18076035991324391287)
XLA Ops:
  13.7 11.9 %all_to_all.125 = bf16[8,8,1024]{2,1,0:T(8,128)(2,1)} all-to-all(bf16[8,8,1024]{2,1,0:T(8,128)(2,1)S(1)} %broadcast_in_dim.53), channel_id=1, replica_groups=mesh['dp'=4,'section'=8,'tensor'=8] {'section'}, dimensions={0} | all-to-all | bytes 262144 | tf_op jit(solution)/shard_map/all_to_all | solution.py:297
  25.6 8.6 %all-to-all-start.1 = ((bf16[8,256,512]{2,1,0:T(8,128)(2,1)}), bf16[8,256,512]{2,1,0:T(8,128)(2,1)}, u32[]{:S(2)}, u32[]{:S(2)}) async-start(bf16[8,256,512]{2,1,0:T(8,128)(2,1)} %bitcast.112), calls=%async_computation.1 | async-start | bytes 4194304 | tf_op jit(solution)/shard_map/all_to_all | solution.py:297
  35.0 6.4 %collective-permute-start = (bf16[2,64,256]{2,1,0:T(8,128)(2,1)S(1)}, bf16[2,64,256]{2,1,0:T(8,128)(2,1)S(1)}, u32[]{:S(2)}, u32[]{:S(2)}) collective-permute-start(bf16[2,64,256]{2,1,0:T(8,128)(2,1)S(1)} %get-tuple-element.224), channel_id=1, source_target_pairs={{0,0},{1,4},{2,1},{3,5},{4,2},{5,6},{6,3},{7,7},{8,8},{9,12},{10,9... | collective-permute-start | bytes 196616 | tf_op jit(solution)/shard_map/ppermute | solution.py:333
  47.4 3.9 copy.20
  51.4 3.9 copy.21
  55.3 24.9 %collective-permute-done = bf16[2,64,256]{2,1,0:T(8,128)(2,1)S(1)} collective-permute-done((bf16[2,64,256]{2,1,0:T(8,128)(2,1)S(1)}, bf16[2,64,256]{2,1,0:T(8,128)(2,1)S(1)}, u32[]{:S(2)}, u32[]{:S(2)}) %collective-permute-start) | collective-permute-done | bytes 65568 | tf_op jit(solution)/shard_map/ppermute | solution.py:333
  80.2 3.0 collective-permute-done.1
  83.2 4.8 collective-permute-done.2
  88.2 2.8 collective-permute-start.5
  91.1 3.1 fusion.1
  94.2 4.8 all-to-all-start.2
  99.0 32.3 %collective-permute-done.5.refs_2_.refs_3_ = bf16[8,256,512]{2,1,0:T(8,128)(2,1)} collective-permute-done((bf16[8,256,512]{2,1,0:T(8,128)(2,1)}, bf16[8,256,512]{2,1,0:T(8,128)(2,1)}, u32[]{:S(2)}, u32[]{:S(2)}) %collective-permute-start.5) | collective-permute-done | bytes 2097184 | tf_op jit(solution)/shard_map/ppermute | solution.py:321
  133.6 6.8 %all-to-all-start.4 = ((bf16[8,256,256]{2,1,0:T(8,128)(2,1)}), bf16[8,256,256]{2,1,0:T(8,128)(2,1)}, u32[]{:S(2)}, u32[]{:S(2)}) async-start(bf16[8,256,256]{2,1,0:T(8,128)(2,1)} %get-tuple-element.110), calls=%async_computation.4 | async-start | bytes 2097152 | tf_op jit(solution)/shard_map/all_to_all | solution.py:297
  140.4 2.7 collective-permute-start.7
  144.6 4.9 shard_map.140
  150.9 17.9 %all-to-all-done.4.refs_4_ = bf16[8,256,256]{2,1,0:T(8,128)(2,1)} async-done(((bf16[8,256,256]{2,1,0:T(8,128)(2,1)}), bf16[8,256,256]{2,1,0:T(8,128)(2,1)}, u32[]{:S(2)}, u32[]{:S(2)}) %all-to-all-start.4) | async-done | bytes 1048608 | tf_op jit(solution)/shard_map/all_to_all | solution.py:297
  172.2 5.6 all-to-all-start.3
  177.8 3.9 fusion.4
  186.3 9.1 %collective-permute-done.8.refs_6_ = bf16[8,256,256]{2,1,0:T(8,128)(2,1)} collective-permute-done((bf16[8,256,256]{2,1,0:T(8,128)(2,1)}, bf16[8,256,256]{2,1,0:T(8,128)(2,1)}, u32[]{:S(2)}, u32[]{:S(2)}) %collective-permute-start.8) | collective-permute-done | bytes 1048608 | tf_op jit(solution)/shard_map/ppermute | solution.py:321
  198.8 15.6 %all_to_all.126 = bf16[8,128,128]{2,1,0:T(8,128)(2,1)S(1)} all-to-all(bf16[8,128,128]{2,1,0:T(8,128)(2,1)S(1)} %pad_maximum_fusion.4), channel_id=1, replica_groups=mesh['dp'=4,'section'=8,'tensor'=8] {'tensor'}, dimensions={0} | all-to-all | bytes 524288 | tf_op jit(solution)/shard_map/all_to_all | solution.py:297
  214.5 5.5 shard_map.142.vo_ref
  223.7 4.0 shard_map.144.refs_1_
  232.4 20.8 %all_to_all.127.q_ref = bf16[8,272,128]{2,1,0:T(8,128)(2,1)S(1)} all-to-all(bf16[8,272,128]{2,1,0:T(8,128)(2,1)S(1)} %get-tuple-element.119), channel_id=1, replica_groups=mesh['dp'=4,'section'=8,'tensor'=8] {'tensor'}, dimensions={0} | all-to-all | bytes 1114112 | tf_op jit(solution)/shard_map/all_to_all | solution.py:297
  254.4 11.5 %all_to_all.128.p_ref = bf16[8,64,128]{2,1,0:T(8,128)(2,1)S(1)} all-to-all(bf16[8,64,128]{2,1,0:T(8,128)(2,1)S(1)} %get-tuple-element.121), channel_id=1, replica_groups=mesh['dp'=4,'section'=8,'tensor'=8] {'tensor'}, dimensions={0} | all-to-all | bytes 262144 | tf_op jit(solution)/shard_map/all_to_all | solution.py:297
  269.5 4.0 shard_map.148.refs_1_
  273.6 6.1 collective-permute-done.14.refs_0_
  281.8 18.8 %all_to_all.129.q_ref = bf16[8,272,128]{2,1,0:T(8,128)(2,1)S(1)} all-to-all(bf16[8,272,128]{2,1,0:T(8,128)(2,1)S(1)} %get-tuple-element.129), channel_id=1, replica_groups=mesh['dp'=4,'section'=8,'tensor'=8] {'tensor'}, dimensions={0} | all-to-all | bytes 1114112 | tf_op jit(solution)/shard_map/all_to_all | solution.py:297
  301.8 11.5 %all_to_all.130.p_ref = bf16[8,64,128]{2,1,0:T(8,128)(2,1)S(1)} all-to-all(bf16[8,64,128]{2,1,0:T(8,128)(2,1)S(1)} %get-tuple-element.131), channel_id=1, replica_groups=mesh['dp'=4,'section'=8,'tensor'=8] {'tensor'}, dimensions={0} | all-to-all | bytes 262144 | tf_op jit(solution)/shard_map/all_to_all | solution.py:297
  314.4 4.0 shard_map.152.refs_1_
  318.4 3.0 collective-permute-done.15.refs_0_
  323.6 17.7 %all_to_all.131.q_ref = bf16[8,272,128]{2,1,0:T(8,128)(2,1)S(1)} all-to-all(bf16[8,272,128]{2,1,0:T(8,128)(2,1)S(1)} %get-tuple-element.139), channel_id=1, replica_groups=mesh['dp'=4,'section'=8,'tensor'=8] {'tensor'}, dimensions={0} | all-to-all | bytes 1114112 | tf_op jit(solution)/shard_map/all_to_all | solution.py:297
  342.5 11.5 %all_to_all.132.p_ref = bf16[8,64,128]{2,1,0:T(8,128)(2,1)S(1)} all-to-all(bf16[8,64,128]{2,1,0:T(8,128)(2,1)S(1)} %get-tuple-element.141), channel_id=1, replica_groups=mesh['dp'=4,'section'=8,'tensor'=8] {'tensor'}, dimensions={0} | all-to-all | bytes 262144 | tf_op jit(solution)/shard_map/all_to_all | solution.py:297
  355.1 4.0 shard_map.156.refs_1_
  359.1 3.0 collective-permute-done.16.refs_0_
  364.3 16.0 %all_to_all.133.q_ref = bf16[8,272,128]{2,1,0:T(8,128)(2,1)S(1)} all-to-all(bf16[8,272,128]{2,1,0:T(8,128)(2,1)S(1)} %get-tuple-element.149), channel_id=1, replica_groups=mesh['dp'=4,'section'=8,'tensor'=8] {'tensor'}, dimensions={0} | all-to-all | bytes 1114112 | tf_op jit(solution)/shard_map/all_to_all | solution.py:297
  381.6 11.4 %all_to_all.134.p_ref = bf16[8,64,128]{2,1,0:T(8,128)(2,1)S(1)} all-to-all(bf16[8,64,128]{2,1,0:T(8,128)(2,1)S(1)} %get-tuple-element.151), channel_id=1, replica_groups=mesh['dp'=4,'section'=8,'tensor'=8] {'tensor'}, dimensions={0} | all-to-all | bytes 262144 | tf_op jit(solution)/shard_map/all_to_all | solution.py:297
  394.4 4.0 shard_map.160.refs_1_
  398.4 3.0 collective-permute-done.17.refs_0_
  401.4 2.9 shard_map.161
  405.0 4.9 all-to-all-start.14
  410.0 12.2 %all-to-all-done.14.q_ref = bf16[8,272,128]{2,1,0:T(8,128)(2,1)S(1)} async-done(((bf16[8,272,128]{2,1,0:T(8,128)(2,1)}), bf16[8,272,128]{2,1,0:T(8,128)(2,1)S(1)}, u32[]{:S(2)}, u32[]{:S(2)}) %all-to-all-start.14) | async-done | bytes 557088 | tf_op jit(solution)/shard_map/all_to_all | solution.py:297
  425.7 4.7 all-to-all-start.15
  430.4 6.3 %fusion.5 = f32[512,128]{0,1:T(8,128)S(1)} fusion(bf16[512,8192]{1,0:T(8,128)(2,1)} %all-gather.8.cloned.1.call-done, bf16[128,8192]{1,0:T(8,128)(2,1)S(1)} %bitcast.97), kind=kOutput, calls=%fused_computation.67 | convolution fusion | flops 1073741824 | bytes 10747904 | tf_op jit(solution)/shard_map/dot_general | solution.py:25
  441.4 4.0 shard_map.164.refs_1_
  445.4 3.0 collective-permute-done.18.refs_0_
  450.5 19.4 %all_to_all.135.q_ref = bf16[8,272,128]{2,1,0:T(8,128)(2,1)S(1)} all-to-all(bf16[8,272,128]{2,1,0:T(8,128)(2,1)S(1)} %get-tuple-element.171), channel_id=1, replica_groups=mesh['dp'=4,'section'=8,'tensor'=8] {'tensor'}, dimensions={0} | all-to-all | bytes 1114112 | tf_op jit(solution)/shard_map/all_to_all | solution.py:297
  471.2 11.5 %all_to_all.136.p_ref = bf16[8,64,128]{2,1,0:T(8,128)(2,1)S(1)} all-to-all(bf16[8,64,128]{2,1,0:T(8,128)(2,1)S(1)} %get-tuple-element.173), channel_id=1, replica_groups=mesh['dp'=4,'section'=8,'tensor'=8] {'tensor'}, dimensions={0} | all-to-all | bytes 262144 | tf_op jit(solution)/shard_map/all_to_all | solution.py:297
  483.9 4.0 shard_map.168.refs_1_
  487.9 3.0 collective-permute-done.19.refs_0_
  493.0 17.4 %all_to_all.137.q_ref = bf16[8,272,128]{2,1,0:T(8,128)(2,1)S(1)} all-to-all(bf16[8,272,128]{2,1,0:T(8,128)(2,1)S(1)} %get-tuple-element.181), channel_id=1, replica_groups=mesh['dp'=4,'section'=8,'tensor'=8] {'tensor'}, dimensions={0} | all-to-all | bytes 1114112 | tf_op jit(solution)/shard_map/all_to_all | solution.py:297
  512.4 4.7 all-to-all-start.19
  519.3 4.0 shard_map.175
  524.4 6.1 all-to-all-start.21
  534.7 4.0 shard_map.172.refs_1_
  538.7 3.0 collective-permute-done.20.refs_0_
  545.3 7.5 %all-to-all-start.20 = ((bf16[8,272,128]{2,1,0:T(8,128)(2,1)}), bf16[8,272,128]{2,1,0:T(8,128)(2,1)S(1)}, u32[]{:S(2)}, u32[]{:S(2)}) async-start(bf16[8,272,128]{2,1,0:T(8,128)(2,1)} %copy-done.11), calls=%async_computation.20 | async-start | bytes 1114112 | tf_op jit(solution)/shard_map/all_to_all | solution.py:297
  554.6 11.9 %all-to-all-done.20.q_ref = bf16[8,272,128]{2,1,0:T(8,128)(2,1)S(1)} async-done(((bf16[8,272,128]{2,1,0:T(8,128)(2,1)}), bf16[8,272,128]{2,1,0:T(8,128)(2,1)S(1)}, u32[]{:S(2)}, u32[]{:S(2)}) %all-to-all-start.20) | async-done | bytes 557088 | tf_op jit(solution)/shard_map/all_to_all | solution.py:297
  568.3 4.7 all-to-all-start.22
  576.0 4.0 shard_map.177
  580.5 6.8 %all-to-all-start.23 = ((bf16[8,32,1024]{2,1,0:T(8,128)(2,1)}), bf16[8,32,1024]{2,1,0:T(8,128)(2,1)S(1)}, u32[]{:S(2)}, u32[]{:S(2)}) async-start(bf16[8,32,1024]{2,1,0:T(8,128)(2,1)} %shard_map.177), calls=%async_computation.23 | async-start | bytes 1048576 | tf_op jit(solution)/shard_map/all_to_all | solution.py:297
  593.2 3.4 collective-permute-start.21
  598.5 7.2 %collective-permute-start.23 = (bf16[2,64,256]{2,1,0:T(8,128)(2,1)S(1)}, bf16[2,64,256]{2,1,0:T(8,128)(2,1)S(1)}, u32[]{:S(2)}, u32[]{:S(2)}) collective-permute-start(bf16[2,64,256]{2,1,0:T(8,128)(2,1)S(1)} %get-tuple-element.212), channel_id=1, source_target_pairs={{2,0},{6,1},{3,2},{7,3},{0,4},{4,5},{1,6},{5,7},{10,8},{14,9},{11,... | collective-permute-start | bytes 196616 | tf_op jit(solution)/shard_map/ppermute | solution.py:343
  614.9 3.8 all-to-all-start.24
  619.5 5.9 all-to-all-done.24
  (194 shorter events, 105.9 us)
Async XLA Ops:
  7.2 423.2 %copy-start = (bf16[1,2,64,8192]{3,2,1,0:T(8,128)(2,1)S(1)}, bf16[1,2,64,8192]{3,2,1,0:T(8,128)(2,1)}, u32[]{:S(2)}) copy-start(bf16[1,2,64,8192]{3,2,1,0:T(8,128)(2,1)} %param.25) | copy-start | bytes 6291460
  7.2 83.9 %all-gather.6.cloned.1.call-start = ((), (), s32[]{:S(2)}) async-start(), calls=%async_computation.26 | async-start | bytes 5242880 | tf_op jit(solution)/shard_map/all_gather | solution.py:353
  7.2 27.0 %copy-start.30 = (bf16[2,64,1024]{2,1,0:T(8,128)(2,1)S(1)}, bf16[2,64,1024]{2,1,0:T(8,128)(2,1)}, u32[]{:S(2)}) copy-start(bf16[2,64,1024]{2,1,0:T(8,128)(2,1)} %param.13) | copy-start | bytes 786436
  25.6 62.6 %all-to-all-start.1 = ((bf16[8,256,512]{2,1,0:T(8,128)(2,1)}), bf16[8,256,512]{2,1,0:T(8,128)(2,1)}, u32[]{:S(2)}, u32[]{:S(2)}) async-start(bf16[8,256,512]{2,1,0:T(8,128)(2,1)} %bitcast.112), calls=%async_computation.1 | async-start | bytes 4194304 | tf_op jit(solution)/shard_map/all_to_all | solution.py:297
  34.2 97.8 %all-gather.4.cloned.1.call-start = ((), (), s32[]{:S(2)}) async-start(), calls=%async_computation.25 | async-start | bytes 1179648 | tf_op jit(solution)/shard_map/all_gather | solution.py:359
  35.0 45.2 %collective-permute-start = (bf16[2,64,256]{2,1,0:T(8,128)(2,1)S(1)}, bf16[2,64,256]{2,1,0:T(8,128)(2,1)S(1)}, u32[]{:S(2)}, u32[]{:S(2)}) collective-permute-start(bf16[2,64,256]{2,1,0:T(8,128)(2,1)S(1)} %get-tuple-element.224), channel_id=1, source_target_pairs={{0,0},{1,4},{2,1},{3,5},{4,2},{5,6},{6,3},{7,7},{8,8},{9,12},{10,9... | collective-permute-start | bytes 196616 | tf_op jit(solution)/shard_map/ppermute | solution.py:333
  41.4 41.8 %collective-permute-start.1 = (bf16[2,64,256]{2,1,0:T(8,128)(2,1)S(1)}, bf16[2,64,256]{2,1,0:T(8,128)(2,1)S(1)}, u32[]{:S(2)}, u32[]{:S(2)}) collective-permute-start(bf16[2,64,256]{2,1,0:T(8,128)(2,1)S(1)} %get-tuple-element.227), channel_id=1, source_target_pairs={{0,1},{1,5},{2,2},{3,6},{4,3},{5,7},{6,0},{7,4},{8,9},{9,13},{10,1... | collective-permute-start | bytes 196616 | tf_op jit(solution)/shard_map/ppermute | solution.py:333
  43.9 44.2 %collective-permute-start.2 = (bf16[2,64,256]{2,1,0:T(8,128)(2,1)S(1)}, bf16[2,64,256]{2,1,0:T(8,128)(2,1)S(1)}, u32[]{:S(2)}, u32[]{:S(2)}) collective-permute-start(bf16[2,64,256]{2,1,0:T(8,128)(2,1)S(1)} %get-tuple-element.226), channel_id=1, source_target_pairs={{0,2},{1,6},{2,3},{3,7},{4,0},{5,4},{6,1},{7,5},{8,10},{9,14},{10,... | collective-permute-start | bytes 196616 | tf_op jit(solution)/shard_map/ppermute | solution.py:333
  44.9 43.3 %collective-permute-start.3 = (bf16[2,64,256]{2,1,0:T(8,128)(2,1)S(1)}, bf16[2,64,256]{2,1,0:T(8,128)(2,1)S(1)}, u32[]{:S(2)}, u32[]{:S(2)}) collective-permute-start(bf16[2,64,256]{2,1,0:T(8,128)(2,1)S(1)} %get-tuple-element.225), channel_id=1, source_target_pairs={{0,3},{1,7},{2,0},{3,4},{4,1},{5,5},{6,2},{7,6},{8,11},{9,15},{10,... | collective-permute-start | bytes 196616 | tf_op jit(solution)/shard_map/ppermute | solution.py:333
  88.2 43.1 %collective-permute-start.5 = (bf16[8,256,512]{2,1,0:T(8,128)(2,1)}, bf16[8,256,512]{2,1,0:T(8,128)(2,1)}, u32[]{:S(2)}, u32[]{:S(2)}) collective-permute-start(bf16[8,256,512]{2,1,0:T(8,128)(2,1)} %all-to-all-done.1.refs_0_.refs_1_), channel_id=1, source_target_pairs={{0,128},{64,192},{128,0},{192,64},{1,129},{65,193},{129,1},{193,65... | collective-permute-start | bytes 6291464 | tf_op jit(solution)/shard_map/ppermute | solution.py:321
  91.1 52.6 %copy-start.32 = (f32[1,8192]{1,0:T(1,128)S(1)}, f32[1,8192]{1,0:T(1,128)}, u32[]{:S(2)}) copy-start(f32[1,8192]{1,0:T(1,128)} %param.17) | copy-start | bytes 98308
  94.2 39.4 %all-to-all-start.2 = ((bf16[8,256,256]{2,1,0:T(8,128)(2,1)}), bf16[8,256,256]{2,1,0:T(8,128)(2,1)S(1)}, u32[]{:S(2)}, u32[]{:S(2)}) async-start(bf16[8,256,256]{2,1,0:T(8,128)(2,1)} %get-tuple-element.205), calls=%async_computation.2 | async-start | bytes 2097152 | tf_op jit(solution)/shard_map/all_to_all | solution.py:297
  99.0 45.6 %collective-permute-start.4 = (bf16[8,256,512]{2,1,0:T(8,128)(2,1)}, bf16[8,256,512]{2,1,0:T(8,128)(2,1)}, u32[]{:S(2)}, u32[]{:S(2)}) collective-permute-start(bf16[8,256,512]{2,1,0:T(8,128)(2,1)} %all-to-all-done.1.refs_0_.refs_1_), channel_id=1, source_target_pairs={{0,64},{64,0},{128,192},{192,128},{1,65},{65,1},{129,193},{193,129... | collective-permute-start | bytes 6291464 | tf_op jit(solution)/shard_map/ppermute | solution.py:321
  131.3 13.2 %collective-permute-start.6 = (bf16[8,256,512]{2,1,0:T(8,128)(2,1)}, bf16[8,256,512]{2,1,0:T(8,128)(2,1)}, u32[]{:S(2)}, u32[]{:S(2)}) collective-permute-start(bf16[8,256,512]{2,1,0:T(8,128)(2,1)} %collective-permute-done.5.refs_2_.refs_3_), channel_id=1, source_target_pairs={{0,64},{64,0},{128,192},{192,128},{1,65},{65,1},{129,193},{193,129... | collective-permute-start | bytes 6291464 | tf_op jit(solution)/shard_map/ppermute | solution.py:321
  133.6 35.1 %all-to-all-start.4 = ((bf16[8,256,256]{2,1,0:T(8,128)(2,1)}), bf16[8,256,256]{2,1,0:T(8,128)(2,1)}, u32[]{:S(2)}, u32[]{:S(2)}) async-start(bf16[8,256,256]{2,1,0:T(8,128)(2,1)} %get-tuple-element.110), calls=%async_computation.4 | async-start | bytes 2097152 | tf_op jit(solution)/shard_map/all_to_all | solution.py:297
  140.4 31.8 %collective-permute-start.7 = (bf16[8,256,256]{2,1,0:T(8,128)(2,1)S(1)}, bf16[8,256,256]{2,1,0:T(8,128)(2,1)}, u32[]{:S(2)}, u32[]{:S(2)}) collective-permute-start(bf16[8,256,256]{2,1,0:T(8,128)(2,1)S(1)} %all-to-all-done.2.refs_0_), channel_id=1, source_target_pairs={{0,128},{64,192},{128,0},{192,64},{1,129},{65,193},{129,1},{193,65... | collective-permute-start | bytes 3145736 | tf_op jit(solution)/shard_map/ppermute | solution.py:321
  150.9 45.2 %copy-start.29 = (f32[1,128]{1,0:T(1,128)S(1)}, f32[1,128]{1,0:T(1,128)}, u32[]{:S(2)}) copy-start(f32[1,128]{1,0:T(1,128)} %gain_ref.21) | copy-start | bytes 1540
  150.9 46.1 %copy-start.28 = (f32[1,128]{1,0:T(1,128)S(1)}, f32[1,128]{1,0:T(1,128)}, u32[]{:S(2)}) copy-start(f32[1,128]{1,0:T(1,128)} %gain_ref.19) | copy-start | bytes 1540
  168.8 26.6 %collective-permute-start.8 = (bf16[8,256,256]{2,1,0:T(8,128)(2,1)}, bf16[8,256,256]{2,1,0:T(8,128)(2,1)}, u32[]{:S(2)}, u32[]{:S(2)}) collective-permute-start(bf16[8,256,256]{2,1,0:T(8,128)(2,1)} %all-to-all-done.4.refs_4_), channel_id=1, source_target_pairs={{0,128},{64,192},{128,0},{192,64},{1,129},{65,193},{129,1},{193,65... | collective-permute-start | bytes 3145736 | tf_op jit(solution)/shard_map/ppermute | solution.py:321
  172.2 24.8 %all-to-all-start.3 = ((bf16[8,272,128]{2,1,0:T(8,128)(2,1)}), bf16[8,272,128]{2,1,0:T(8,128)(2,1)}, u32[]{:S(2)}, u32[]{:S(2)}) async-start(bf16[8,272,128]{2,1,0:T(8,128)(2,1)} %copy-done.10), calls=%async_computation.3 | async-start | bytes 1114112 | tf_op jit(solution)/shard_map/all_to_all | solution.py:297
  177.8 252.6 %all-gather.8.cloned.1.call-start = ((), (), s32[]{:S(2)}) async-start(), calls=%async_computation.27 | async-start | bytes 10485760 | tf_op jit(solution)/shard_map/all_gather | solution.py:399
  185.6 28.9 %collective-permute-start.9 = (bf16[8,256,256]{2,1,0:T(8,128)(2,1)S(1)}, bf16[8,256,256]{2,1,0:T(8,128)(2,1)}, u32[]{:S(2)}, u32[]{:S(2)}) collective-permute-start(bf16[8,256,256]{2,1,0:T(8,128)(2,1)S(1)} %all-to-all-done.2.refs_0_), channel_id=1, source_target_pairs={{0,64},{64,0},{128,192},{192,128},{1,65},{65,1},{129,193},{193,129... | collective-permute-start | bytes 3145736 | tf_op jit(solution)/shard_map/ppermute | solution.py:321
  185.7 28.8 %collective-permute-start.10 = (bf16[8,256,256]{2,1,0:T(8,128)(2,1)}, bf16[8,256,256]{2,1,0:T(8,128)(2,1)}, u32[]{:S(2)}, u32[]{:S(2)}) collective-permute-start(bf16[8,256,256]{2,1,0:T(8,128)(2,1)} %collective-permute-done.7.refs_2_), channel_id=1, source_target_pairs={{0,64},{64,0},{128,192},{192,128},{1,65},{65,1},{129,193},{193,129... | collective-permute-start | bytes 3145736 | tf_op jit(solution)/shard_map/ppermute | solution.py:321
  186.2 28.3 %collective-permute-start.11 = (bf16[8,256,256]{2,1,0:T(8,128)(2,1)}, bf16[8,256,256]{2,1,0:T(8,128)(2,1)}, u32[]{:S(2)}, u32[]{:S(2)}) collective-permute-start(bf16[8,256,256]{2,1,0:T(8,128)(2,1)} %all-to-all-done.4.refs_4_), channel_id=1, source_target_pairs={{0,64},{64,0},{128,192},{192,128},{1,65},{65,1},{129,193},{193,129... | collective-permute-start | bytes 3145736 | tf_op jit(solution)/shard_map/ppermute | solution.py:321
  195.4 19.1 %collective-permute-start.12 = (bf16[8,256,256]{2,1,0:T(8,128)(2,1)}, bf16[8,256,256]{2,1,0:T(8,128)(2,1)}, u32[]{:S(2)}, u32[]{:S(2)}) collective-permute-start(bf16[8,256,256]{2,1,0:T(8,128)(2,1)} %collective-permute-done.8.refs_6_), channel_id=1, source_target_pairs={{0,64},{64,0},{128,192},{192,128},{1,65},{65,1},{129,193},{193,129... | collective-permute-start | bytes 3145736 | tf_op jit(solution)/shard_map/ppermute | solution.py:321
  214.5 5.6 copy-start.21
  221.1 1.9 copy-start.1
  223.1 7.2 %collective-permute-start.13 = (bf16[64,1024]{1,0:T(8,128)(2,1)S(1)}, bf16[64,1024]{1,0:T(8,128)(2,1)S(1)}, u32[]{:S(2)}, u32[]{:S(2)}) collective-permute-start(bf16[64,1024]{1,0:T(8,128)(2,1)S(1)} %get-tuple-element.114), channel_id=1, source_target_pairs={{0,8},{8,16},{16,24},{24,32},{32,40},{40,48},{48,56},{56,0},{1,9},... | collective-permute-start | bytes 393224 | tf_op jit(solution)/shard_map/ppermute | solution.py:318
  265.9 2.5 copy-start.2
  269.4 10.2 %collective-permute-start.14 = (bf16[64,1024]{1,0:T(8,128)(2,1)S(1)}, bf16[64,1024]{1,0:T(8,128)(2,1)S(1)}, u32[]{:S(2)}, u32[]{:S(2)}) collective-permute-start(bf16[64,1024]{1,0:T(8,128)(2,1)S(1)} %get-tuple-element.124), channel_id=1, source_target_pairs={{0,8},{8,16},{16,24},{24,32},{32,40},{40,48},{48,56},{56,0},{1,9},... | collective-permute-start | bytes 393224 | tf_op jit(solution)/shard_map/ppermute | solution.py:318
  273.6 39.7 %copy-start.3 = (bf16[2,1024,1024]{2,1,0:T(8,128)(2,1)S(1)}, bf16[2,1024,1024]{2,1,0:T(8,128)(2,1)}, u32[]{:S(2)}) copy-start(bf16[2,1024,1024]{2,1,0:T(8,128)(2,1)} %copy-done.1) | copy-start | bytes 12582916
  314.3 7.2 %collective-permute-start.15 = (bf16[64,1024]{1,0:T(8,128)(2,1)S(1)}, bf16[64,1024]{1,0:T(8,128)(2,1)S(1)}, u32[]{:S(2)}, u32[]{:S(2)}) collective-permute-start(bf16[64,1024]{1,0:T(8,128)(2,1)S(1)} %get-tuple-element.134), channel_id=1, source_target_pairs={{0,8},{8,16},{16,24},{24,32},{32,40},{40,48},{48,56},{56,0},{1,9},... | collective-permute-start | bytes 393224 | tf_op jit(solution)/shard_map/ppermute | solution.py:318
  355.0 7.2 %collective-permute-start.16 = (bf16[64,1024]{1,0:T(8,128)(2,1)S(1)}, bf16[64,1024]{1,0:T(8,128)(2,1)S(1)}, u32[]{:S(2)}, u32[]{:S(2)}) collective-permute-start(bf16[64,1024]{1,0:T(8,128)(2,1)S(1)} %get-tuple-element.144), channel_id=1, source_target_pairs={{0,8},{8,16},{16,24},{24,32},{32,40},{40,48},{48,56},{56,0},{1,9},... | collective-permute-start | bytes 393224 | tf_op jit(solution)/shard_map/ppermute | solution.py:318
  381.5 11.5 %copy-start.16 = (f32[2,64,512]{2,1,0:T(8,128)}, f32[2,64,512]{2,1,0:T(8,128)S(1)}, u32[]{:S(2)}) copy-start(f32[2,64,512]{2,1,0:T(8,128)S(1)} %get-tuple-element.160.refs_0_) | copy-start | bytes 786436
  394.1 7.4 %collective-permute-start.17 = (bf16[64,1024]{1,0:T(8,128)(2,1)S(1)}, bf16[64,1024]{1,0:T(8,128)(2,1)S(1)}, u32[]{:S(2)}, u32[]{:S(2)}) collective-permute-start(bf16[64,1024]{1,0:T(8,128)(2,1)S(1)} %get-tuple-element.154), channel_id=1, source_target_pairs={{0,8},{8,16},{16,24},{24,32},{32,40},{40,48},{48,56},{56,0},{1,9},... | collective-permute-start | bytes 393224 | tf_op jit(solution)/shard_map/ppermute | solution.py:318
  405.0 17.2 %all-to-all-start.14 = ((bf16[8,272,128]{2,1,0:T(8,128)(2,1)}), bf16[8,272,128]{2,1,0:T(8,128)(2,1)S(1)}, u32[]{:S(2)}, u32[]{:S(2)}) async-start(bf16[8,272,128]{2,1,0:T(8,128)(2,1)} %get-tuple-element.159), calls=%async_computation.14 | async-start | bytes 1114112 | tf_op jit(solution)/shard_map/all_to_all | solution.py:297
  422.2 1.0 copy-start.17
  425.7 12.3 %all-to-all-start.15 = ((bf16[8,64,128]{2,1,0:T(8,128)(2,1)}), bf16[8,64,128]{2,1,0:T(8,128)(2,1)S(1)}, u32[]{:S(2)}, u32[]{:S(2)}) async-start(bf16[8,64,128]{2,1,0:T(8,128)(2,1)} %get-tuple-element.161), calls=%async_computation.15 | async-start | bytes 262144 | tf_op jit(solution)/shard_map/all_to_all | solution.py:297
  430.4 7.6 %copy-start.23 = (bf16[64,1024]{1,0:T(8,128)(2,1)S(1)}, bf16[64,1024]{1,0:T(8,128)(2,1)}, u32[]{:S(2)}) copy-start(bf16[64,1024]{1,0:T(8,128)(2,1)} %copy-done.22) | copy-start | bytes 393220
  438.0 2.2 copy-start.4
  441.3 7.2 %collective-permute-start.18 = (bf16[64,1024]{1,0:T(8,128)(2,1)S(1)}, bf16[64,1024]{1,0:T(8,128)(2,1)S(1)}, u32[]{:S(2)}, u32[]{:S(2)}) collective-permute-start(bf16[64,1024]{1,0:T(8,128)(2,1)S(1)} %get-tuple-element.166), channel_id=1, source_target_pairs={{0,8},{8,16},{16,24},{24,32},{32,40},{40,48},{48,56},{56,0},{1,9},... | collective-permute-start | bytes 393224 | tf_op jit(solution)/shard_map/ppermute | solution.py:318
  445.4 24.6 %copy-start.15 = (f32[2,64,512]{2,1,0:T(8,128)S(1)}, f32[2,64,512]{2,1,0:T(8,128)}, u32[]{:S(2)}) copy-start(f32[2,64,512]{2,1,0:T(8,128)} %copy-done.14) | copy-start | bytes 786436
  445.4 37.3 %copy-start.5 = (bf16[2,1024,1024]{2,1,0:T(8,128)(2,1)S(1)}, bf16[2,1024,1024]{2,1,0:T(8,128)(2,1)}, u32[]{:S(2)}) copy-start(bf16[2,1024,1024]{2,1,0:T(8,128)(2,1)} %copy-done.1) | copy-start | bytes 12582916
  483.8 7.2 %collective-permute-start.19 = (bf16[64,1024]{1,0:T(8,128)(2,1)S(1)}, bf16[64,1024]{1,0:T(8,128)(2,1)S(1)}, u32[]{:S(2)}, u32[]{:S(2)}) collective-permute-start(bf16[64,1024]{1,0:T(8,128)(2,1)S(1)} %get-tuple-element.176), channel_id=1, source_target_pairs={{0,8},{8,16},{16,24},{24,32},{32,40},{40,48},{48,56},{56,0},{1,9},... | collective-permute-start | bytes 393224 | tf_op jit(solution)/shard_map/ppermute | solution.py:318
  493.0 17.4 %copy-start.24 = (bf16[64,1024]{1,0:T(8,128)(2,1)}, bf16[64,1024]{1,0:T(8,128)(2,1)S(1)}, u32[]{:S(2)}) copy-start(bf16[64,1024]{1,0:T(8,128)(2,1)S(1)} %get-tuple-element.184.h_ref) | copy-start | bytes 393220
  510.5 20.0 %copy-start.25 = (bf16[64,1024]{1,0:T(8,128)(2,1)S(1)}, bf16[64,1024]{1,0:T(8,128)(2,1)}, u32[]{:S(2)}) copy-start(bf16[64,1024]{1,0:T(8,128)(2,1)} %copy-done.24) | copy-start | bytes 393220
  512.4 12.0 %all-to-all-start.19 = ((bf16[8,64,128]{2,1,0:T(8,128)(2,1)}), bf16[8,64,128]{2,1,0:T(8,128)(2,1)S(1)}, u32[]{:S(2)}, u32[]{:S(2)}) async-start(bf16[8,64,128]{2,1,0:T(8,128)(2,1)} %copy-done.27), calls=%async_computation.19 | async-start | bytes 262144 | tf_op jit(solution)/shard_map/all_to_all | solution.py:297
  517.1 2.2 copy-start.8
  524.4 21.0 %all-to-all-start.21 = ((bf16[8,32,1024]{2,1,0:T(8,128)(2,1)}), bf16[8,32,1024]{2,1,0:T(8,128)(2,1)}, u32[]{:S(2)}, u32[]{:S(2)}) async-start(bf16[8,32,1024]{2,1,0:T(8,128)(2,1)} %shard_map.175), calls=%async_computation.21 | async-start | bytes 1048576 | tf_op jit(solution)/shard_map/all_to_all | solution.py:297
  530.5 2.2 copy-start.6
  534.5 7.3 %collective-permute-start.20 = (bf16[64,1024]{1,0:T(8,128)(2,1)S(1)}, bf16[64,1024]{1,0:T(8,128)(2,1)S(1)}, u32[]{:S(2)}, u32[]{:S(2)}) collective-permute-start(bf16[64,1024]{1,0:T(8,128)(2,1)S(1)} %get-tuple-element.186), channel_id=1, source_target_pairs={{0,8},{8,16},{16,24},{24,32},{32,40},{40,48},{48,56},{56,0},{1,9},... | collective-permute-start | bytes 393224 | tf_op jit(solution)/shard_map/ppermute | solution.py:318
  538.7 34.3 %copy-start.33 = (s32[1,2]{1,0:T(1,128)S(1)}, s32[1,2]{1,0:T(1,128)}, u32[]{:S(2)}) copy-start(s32[1,2]{1,0:T(1,128)} %param.14) | copy-start | bytes 28
  545.3 21.1 %all-to-all-start.20 = ((bf16[8,272,128]{2,1,0:T(8,128)(2,1)}), bf16[8,272,128]{2,1,0:T(8,128)(2,1)S(1)}, u32[]{:S(2)}, u32[]{:S(2)}) async-start(bf16[8,272,128]{2,1,0:T(8,128)(2,1)} %copy-done.11), calls=%async_computation.20 | async-start | bytes 1114112 | tf_op jit(solution)/shard_map/all_to_all | solution.py:297
  568.3 12.2 %all-to-all-start.22 = ((bf16[8,64,128]{2,1,0:T(8,128)(2,1)}), bf16[8,64,128]{2,1,0:T(8,128)(2,1)S(1)}, u32[]{:S(2)}, u32[]{:S(2)}) async-start(bf16[8,64,128]{2,1,0:T(8,128)(2,1)} %copy-done.26), calls=%async_computation.22 | async-start | bytes 262144 | tf_op jit(solution)/shard_map/all_to_all | solution.py:297
  573.8 2.2 copy-start.9
  580.0 32.4 %copy-start.31 = (bf16[32,1024]{1,0:T(8,128)(2,1)S(1)}, bf16[32,1024]{1,0:T(8,128)(2,1)}, u32[]{:S(2)}) copy-start(bf16[32,1024]{1,0:T(8,128)(2,1)} %reduce_sum.43) | copy-start | bytes 196612
  580.5 33.5 %all-to-all-start.23 = ((bf16[8,32,1024]{2,1,0:T(8,128)(2,1)}), bf16[8,32,1024]{2,1,0:T(8,128)(2,1)S(1)}, u32[]{:S(2)}, u32[]{:S(2)}) async-start(bf16[8,32,1024]{2,1,0:T(8,128)(2,1)} %shard_map.177), calls=%async_computation.23 | async-start | bytes 1048576 | tf_op jit(solution)/shard_map/all_to_all | solution.py:297
  587.3 2.2 copy-start.7
  589.5 0.9 copy-start.13
  593.2 19.2 %collective-permute-start.21 = (bf16[2,64,256]{2,1,0:T(8,128)(2,1)S(1)}, bf16[2,64,256]{2,1,0:T(8,128)(2,1)S(1)}, u32[]{:S(2)}, u32[]{:S(2)}) collective-permute-start(bf16[2,64,256]{2,1,0:T(8,128)(2,1)S(1)} %get-tuple-element.210), channel_id=1, source_target_pairs={{0,0},{4,1},{1,2},{5,3},{2,4},{6,5},{3,6},{7,7},{8,8},{12,9},{9,10... | collective-permute-start | bytes 196616 | tf_op jit(solution)/shard_map/ppermute | solution.py:343
  596.6 15.8 %collective-permute-start.22 = (bf16[2,64,256]{2,1,0:T(8,128)(2,1)S(1)}, bf16[2,64,256]{2,1,0:T(8,128)(2,1)S(1)}, u32[]{:S(2)}, u32[]{:S(2)}) collective-permute-start(bf16[2,64,256]{2,1,0:T(8,128)(2,1)S(1)} %get-tuple-element.213), channel_id=1, source_target_pairs={{1,0},{5,1},{2,2},{6,3},{3,4},{7,5},{0,6},{4,7},{9,8},{13,9},{10,1... | collective-permute-start | bytes 196616 | tf_op jit(solution)/shard_map/ppermute | solution.py:343
  598.5 13.9 %collective-permute-start.23 = (bf16[2,64,256]{2,1,0:T(8,128)(2,1)S(1)}, bf16[2,64,256]{2,1,0:T(8,128)(2,1)S(1)}, u32[]{:S(2)}, u32[]{:S(2)}) collective-permute-start(bf16[2,64,256]{2,1,0:T(8,128)(2,1)S(1)} %get-tuple-element.212), channel_id=1, source_target_pairs={{2,0},{6,1},{3,2},{7,3},{0,4},{4,5},{1,6},{5,7},{10,8},{14,9},{11,... | collective-permute-start | bytes 196616 | tf_op jit(solution)/shard_map/ppermute | solution.py:343
  605.7 8.3 %collective-permute-start.24 = (bf16[2,64,256]{2,1,0:T(8,128)(2,1)S(1)}, bf16[2,64,256]{2,1,0:T(8,128)(2,1)S(1)}, u32[]{:S(2)}, u32[]{:S(2)}) collective-permute-start(bf16[2,64,256]{2,1,0:T(8,128)(2,1)S(1)} %get-tuple-element.211), channel_id=1, source_target_pairs={{3,0},{7,1},{0,2},{4,3},{1,4},{5,5},{2,6},{6,7},{11,8},{15,9},{8,1... | collective-permute-start | bytes 196616 | tf_op jit(solution)/shard_map/ppermute | solution.py:343
  614.9 10.4 %all-to-all-start.24 = ((bf16[8,2,4,1024]{3,2,1,0:T(4,128)(2,1)}), bf16[8,2,4,1024]{3,2,1,0:T(4,128)(2,1)S(1)}, u32[]{:S(2)}, u32[]{:S(2)}) async-start(bf16[8,2,4,1024]{3,2,1,0:T(4,128)(2,1)} %maximum_bitcast_fusion.1), calls=%async_computation.24 | async-start | bytes 262144 | tf_op jit(solution)/shard_map/all_to_all | solution.py:297
  (10 other events, 7.2 us)
Sparse Core Ops, SparseCore 0:
  9.8 43.6 all-gather.5
  91.2 40.7 all-gather.3
  254.5 59.2 all-gather.7
